TPU v7x, 32 devices: a whole 2x2x4 slice. The times are simulated.
32 devices in a mesh: dp: 8 (over z, x), section: 4 (over y, core).
Axes of the slice: x: 2, y: 2, z: 4, core: 2. Of those that a mesh axis runs over, the one named last changes fastest.
Arguments:
- weights: bfloat16 [4, 6144, 256], P('section'), may hold values from -0.125 to 0.125
- inputs: bfloat16 [4, 4096, 2048], P('section', 'dp'), may hold values from -40 to 40
- out_grads: bfloat16 [4, 4096, 2048], P('section', 'dp'), may hold values from -40 to 40
- master: float32 [4, 6144, 256], P('section', 'dp'), may hold values from -0.125 to 0.125
- moment1: float32 [4, 6144, 256], P('section', 'dp'), may hold values from -6 to 6
- moment2: float32 [4, 6144, 256], P('section', 'dp'), may hold values from 0.1 to 10
Outputs:
- new_master: float32 [4, 6144, 256], P('section', 'dp')
- new_moment1: float32 [4, 6144, 256], P('section', 'dp')
- new_moment2: float32 [4, 6144, 256], P('section', 'dp')
- new_weights: bfloat16 [4, 6144, 256], P('section')
All inputs are finite; a program needn't handle non-finite values.
Results may differ from a plain program's by a relative error of at most 0.001.
Values may be sent and summed in bfloat16 or wider, within the bound.
No kernel may reach another device: no remote copies, remote signals or barrier semaphores. Data moves between devices by JAX's collectives and lax.ppermute only.
A program may use at most 64 MiB of HBM per device.

v0:
```python
import math

import jax
import jax.numpy as jnp
from jax import lax
from jax.experimental import pallas as pl
from jax.experimental.pallas import tpu as pltpu
from jax.sharding import PartitionSpec as P

MROWS = 256
STEP = 10
LITTLE = 16 << 20
CHUNK = 32
PAD = 16
POWER = 8
TOP = 32768.0


def cost_of(micros):
    return pl.CostEstimate(flops=int(micros * 1.18e9), bytes_accessed=1024, transcendentals=0)


PIECE = cost_of(1.7)
CHEAP = pl.CostEstimate(flops=1024, bytes_accessed=1024, transcendentals=0)


def forward_pieces(x_rows, dy_rows, w_gate, w_up, w_down):
    pre_gate = jnp.dot(x_rows, w_gate, preferred_element_type=jnp.float32)
    pre_up = jnp.dot(x_rows, w_up, preferred_element_type=jnp.float32)
    d_hidden = jnp.dot(dy_rows, w_down, preferred_element_type=jnp.float32)
    return activation(pre_gate, pre_up, d_hidden)


def activation(pre_gate, pre_up, d_hidden):
    sigma = jax.nn.sigmoid(pre_gate)
    silu_val = pre_gate * sigma
    hidden = (silu_val * pre_up).astype(jnp.bfloat16)
    d_gate = (d_hidden * pre_up * sigma * (1.0 + pre_gate * (1.0 - sigma))).astype(jnp.bfloat16)
    d_up = (d_hidden * silu_val).astype(jnp.bfloat16)
    return d_gate, d_up, hidden


def block_grads(x_rows, dy_rows, w_gate, w_up, w_down):
    d_gate, d_up, hidden = forward_pieces(x_rows, dy_rows, w_gate, w_up, w_down)
    g_gate = jnp.dot(x_rows.T, d_gate, preferred_element_type=jnp.float32)
    g_up = jnp.dot(x_rows.T, d_up, preferred_element_type=jnp.float32)
    g_down = jnp.dot(dy_rows.T, hidden, preferred_element_type=jnp.float32)
    return jnp.concatenate([g_gate, g_up, g_down], axis=0)


def adam(clip, shard, old_param, first, second):
    clipped = clip * shard
    new_first = 0.9 * first + 0.1 * clipped
    new_second = 0.95 * second + 0.05 * clipped * clipped
    first_fix = 1.0 / (1.0 - 0.9**STEP)
    second_fix = 1.0 / (1.0 - 0.95**STEP)
    update = new_first * first_fix / (jnp.sqrt(new_second * second_fix) + 1e-08) + 0.1 * old_param
    return old_param - 0.01 * update, new_first, new_second


def clip_of(total, max_norm):
    return jnp.minimum(jnp.float32(1.0), max_norm / (jnp.sqrt(total) + 1e-06))


def plain(weights, inputs, out_grads, master, moment1, moment2):
    stacked = weights[0]
    width = stacked.shape[0] // 3
    local_grad = jnp.zeros(stacked.shape, jnp.float32)
    for start in range(0, inputs.shape[1], MROWS):
        x_rows = inputs[0, start : start + MROWS]
        dy_rows = out_grads[0, start : start + MROWS]
        local_grad = local_grad + block_grads(
            x_rows, dy_rows, stacked[:width], stacked[width : 2 * width], stacked[2 * width :]
        )
    shard = lax.psum_scatter(local_grad, "dp", scatter_dimension=0, tiled=True)
    total = lax.psum(jnp.sum(shard * shard), ("dp", "section"))
    max_norm = jnp.sqrt(jnp.float32(lax.axis_size("section") * stacked.size))
    new_param, new_first, new_second = adam(clip_of(total, max_norm), shard, master[0], moment1[0], moment2[0])
    gathered = lax.all_gather(new_param.astype(jnp.bfloat16), "dp", axis=0, tiled=True)
    return new_param[None], new_first[None], new_second[None], gathered[None]


def chunks(rows):
    return [slice(at, min(at + CHUNK, rows)) for at in range(0, rows, CHUNK)]


def fold(value):
    return jnp.max(jnp.abs(value).reshape(-1, 8, value.shape[1]), axis=0)


def scale_of(top):
    scale = jnp.max(top, axis=0, keepdims=True)
    return jnp.maximum(scale, 1e-30).astype(jnp.bfloat16).astype(jnp.float32)


def encode(value, factor):
    v = value * factor
    v2 = v * v
    v4 = v2 * v2
    v8 = v4 * v4
    return jnp.where(v < 0.0, -v8, v8).astype(jnp.bfloat16)


def decode(code, factor):
    code = code.astype(jnp.float32)
    size = jnp.abs(code)
    root = jnp.exp(jnp.log(jnp.maximum(size, 1e-37)) * (1.0 / POWER)) * factor
    root = jnp.where(size > 0.0, root, 0.0)
    return jnp.where(code < 0.0, -root, root)


def write_codes(total_ref, top, out_ref, first):
    scale = scale_of(top)
    factor = TOP / scale
    for part in chunks(total_ref.shape[0]):
        size = part.stop - part.start
        out_ref[pl.ds(first + part.start, size), :] = encode(total_ref[part, :], factor)
    return scale


def lookup(table, index):
    bits = max(max(table).bit_length(), 1)
    if bits * len(table) < 32:
        packed = sum(value << (bits * at) for at, value in enumerate(table))
        return jnp.bitwise_and(jnp.right_shift(jnp.int32(packed), index * bits), (1 << bits) - 1)
    out = jnp.int32(table[0])
    for at, value in enumerate(table[1:], 1):
        out = jnp.where(index == at, jnp.int32(value), out)
    return out


def forward_kernel(messages, rows, x_hbm, dy_hbm, w_hbm, factors_ref, *refs):
    outs = refs[: len(messages)]
    x_ref, dy_ref, w_ref, a_ref, b_ref, h_ref, total_ref, sems = refs[len(messages) :]
    width = x_hbm.shape[1]
    half = width // 2

    def fetch(at, source, target, index):
        copy = pltpu.make_async_copy(source.at[index], target.at[index], sems.at[at])
        copy.start()
        return copy

    copies = []
    for columns in (pl.ds(0, half), pl.ds(half, half)):
        copies.append(fetch(len(copies), x_hbm, x_ref, (slice(None), columns)))
        copies.append(fetch(len(copies), w_hbm, w_ref, columns))
        copies.append(fetch(len(copies), w_hbm, w_ref, pl.ds(columns.start + width, half)))
    for columns in (pl.ds(0, half), pl.ds(half, half)):
        copies.append(fetch(len(copies), dy_hbm, dy_ref, (slice(None), columns)))
        copies.append(fetch(len(copies), w_hbm, w_ref, pl.ds(columns.start + 2 * width, half)))

    def product(left, start, which):
        weight = w_ref[which * width + start : which * width + start + half]
        return jnp.dot(left[:, start : start + half], weight, preferred_element_type=jnp.float32)

    for copy in copies[:3]:
        copy.wait()
    a_ref[...] = product(x_ref, 0, 0)
    b_ref[...] = product(x_ref, 0, 1)
    for copy in copies[3:6]:
        copy.wait()
    a_ref[...] += product(x_ref, half, 0)
    b_ref[...] += product(x_ref, half, 1)
    for copy in copies[6:8]:
        copy.wait()
    h_ref[...] = product(dy_ref, 0, 2)
    for copy in copies[8:]:
        copy.wait()
    h_ref[...] += product(dy_ref, half, 2)
    for part in chunks(x_ref.shape[0]):
        d_gate, d_up, hidden = activation(a_ref[part, :], b_ref[part, :], h_ref[part, :])
        factors_ref[0, part, :] = d_gate
        factors_ref[1, part, :] = d_up
        factors_ref[2, part, :] = hidden
    per = width // rows
    for places, out_ref in zip(messages, outs):
        scales = jnp.zeros((PAD, out_ref.shape[1]), jnp.float32)
        for step, place in enumerate(places):
            at = place()
            kind = lax.div(at, per)
            column = pl.ds(pl.multiple_of(lax.rem(at, per) * rows, rows), rows)
            left = jnp.where(kind == 2, dy_ref[:, column], x_ref[:, column])
            total_ref[...] = lax.dot_general(
                left, factors_ref[kind], (((0,), (0,)), ((), ())), preferred_element_type=jnp.float32
            )
            top = fold(total_ref[:CHUNK, :])
            for part in chunks(rows)[1:]:
                top = jnp.maximum(top, fold(total_ref[part, :]))
            scale = write_codes(total_ref, top, out_ref, step * rows)
            row = lax.broadcasted_iota(jnp.int32, scales.shape, 0)
            scales = jnp.where(row == step, scale, scales)
        out_ref[len(places) * rows :, :] = scales.astype(jnp.bfloat16)


def forward(x, dy, stacked, messages, rows):
    tokens, width = x.shape
    hidden = stacked.shape[1]

    def place_of(table, block):
        steps = stacked.shape[0] // len(table) // rows
        return lambda: lookup(table, lax.axis_index("dp")) * steps + block

    places = [[place_of(*block) for block in blocks] for blocks in messages]
    return pl.pallas_call(
        lambda *refs: forward_kernel(places, rows, *refs),
        in_specs=[pl.BlockSpec(memory_space=pltpu.HBM)] * 3,
        out_shape=[jax.ShapeDtypeStruct((3, tokens, hidden), jnp.bfloat16)]
        + [jax.ShapeDtypeStruct((len(blocks) * rows + PAD, hidden), jnp.bfloat16) for blocks in messages],
        scratch_shapes=[
            pltpu.VMEM(x.shape, x.dtype),
            pltpu.VMEM(dy.shape, dy.dtype),
            pltpu.VMEM(stacked.shape, stacked.dtype),
            *[pltpu.VMEM((tokens, hidden), jnp.float32)] * 3,
            pltpu.VMEM((rows, hidden), jnp.float32),
            pltpu.SemaphoreType.DMA((10,)),
        ],
        compiler_params=pltpu.CompilerParams(vmem_limit_bytes=60 << 20),
        cost_estimate=CHEAP,
        name="forward",
    )(x, dy, stacked)


def pick(values, step):
    if all(value == values[0] + at for at, value in enumerate(values)):
        return step + values[0] if len(values) > 1 else jnp.int32(values[0])
    out = jnp.int32(values[0])
    for at, value in enumerate(values[1:], 1):
        out = jnp.where(step == at, value, out)
    return out


def piece_kernel(place, per, got, extra, last, *refs):
    step = pl.program_id(0)
    x_ref, dy_ref, d_ref = refs[:3]
    outs = refs[3 + 2 * len(got) + extra :]
    rows = x_ref.shape[1]
    left = jnp.where(lax.div(place(step), per) == 2, dy_ref[...], x_ref[...])
    total_ref = outs[-1]
    total_ref[...] = lax.dot_general(left, d_ref[0], (((0,), (0,)), ((), ())), preferred_element_type=jnp.float32)
    factors = []
    for at, blocks in enumerate(got):
        scales = refs[4 + 2 * at][...].astype(jnp.float32)
        row = lax.broadcasted_iota(jnp.int32, scales.shape, 0)
        here = pick([PAD if block is None else block for block in blocks], step)
        factors.append(jnp.sum(jnp.where(row == here, scales, 0.0), axis=0, keepdims=True) * (1.0 / TOP))
    top = jnp.zeros((8, total_ref.shape[1]), jnp.float32)
    for part in chunks(rows):
        total = total_ref[part, :]
        for at, factor in enumerate(factors):
            total = total + decode(refs[3 + 2 * at][part, :], factor)
        if last:
            outs[0][part, :] = total
        else:
            if factors:
                total_ref[part, :] = total
            top = jnp.maximum(top, fold(total))
    if not last:
        out_ref, scales_ref = outs[:2]
        scale = write_codes(total_ref, top, out_ref, pl.multiple_of(step * rows, rows))
        row = lax.broadcasted_iota(jnp.int32, scales_ref.shape, 0)
        scales_ref[...] = jnp.where(row == step, scale, jnp.where(step == 0, 0.0, scales_ref[...]))
        out_ref[pl.ds(out_ref.shape[0] - PAD, PAD), :] = scales_ref[...].astype(jnp.bfloat16)


def piece(x, dy, factors, rows, blocks, got=(), after=None, last=False, cost=PIECE):
    tokens, width = x.shape
    hidden = factors.shape[2]
    per = width // rows
    shard = 3 * width // len(blocks[0][0])
    steps = shard // rows
    tables = [table for table, _ in blocks]
    within = [block for _, block in blocks]

    def place(i):
        r = lax.axis_index("dp")
        owner = lookup(tables[0], r)
        for at, table in enumerate(tables[1:], 1):
            if table != tables[at - 1]:
                owner = jnp.where(i >= at, lookup(table, r), owner)
        return owner * steps + pick(within, i)

    def column(i):
        return (0, lax.rem(place(i), per))

    in_specs = [
        pl.BlockSpec((tokens, rows), column),
        pl.BlockSpec((tokens, rows), column),
        pl.BlockSpec((1, tokens, hidden), lambda i: (lax.div(place(i), per), 0, 0)),
    ]
    operands = [x, dy, factors]
    for message, parts in got:
        present = [part for part in parts if part is not None]
        nearest = [present[0] if part is None else part for part in parts]
        scales = (message.shape[0] - PAD) // PAD
        in_specs += [
            pl.BlockSpec((rows, hidden), lambda i, nearest=nearest: (pick(nearest, i), 0)),
            pl.BlockSpec((PAD, hidden), lambda i, scales=scales: (scales, 0)),
        ]
        operands += [message, message]
    extra = 0
    if after is not None:
        extra = 1
        operands.append(after)
        in_specs.append(pl.BlockSpec(memory_space=pl.ANY))
    if last:
        out_specs = pl.BlockSpec((rows, hidden), lambda i: (i, 0))
        out_shape = jax.ShapeDtypeStruct((len(blocks) * rows, hidden), jnp.float32)
        scratch = [pltpu.VMEM((rows, hidden), jnp.float32)]
    else:
        out_specs = pl.BlockSpec((len(blocks) * rows + PAD, hidden), lambda i: (0, 0))
        out_shape = jax.ShapeDtypeStruct((len(blocks) * rows + PAD, hidden), jnp.bfloat16)
        scratch = [pltpu.VMEM((PAD, hidden), jnp.float32), pltpu.VMEM((rows, hidden), jnp.float32)]
    return pl.pallas_call(
        lambda *refs: piece_kernel(place, per, [parts for _, parts in got], extra, last, *refs),
        grid=(len(blocks),),
        in_specs=in_specs,
        out_specs=out_specs,
        out_shape=out_shape,
        scratch_shapes=scratch,
        compiler_params=pltpu.CompilerParams(vmem_limit_bytes=LITTLE),
        cost_estimate=cost,
        name="piece",
    )(*operands)


def finish_kernel(sum_ref, *refs):
    step = pl.program_id(0)
    out_ref, squares_ref = refs[-2:]
    factors = []
    for scales_ref in refs[1:-2:2]:
        scales = scales_ref[...].astype(jnp.float32)
        row = lax.broadcasted_iota(jnp.int32, scales.shape, 0)
        factors.append(jnp.sum(jnp.where(row == step, scales, 0.0), axis=0, keepdims=True) * (1.0 / TOP))
    top = jnp.zeros((8, out_ref.shape[1]), jnp.float32)
    for part in chunks(out_ref.shape[0]):
        total = sum_ref[part, :]
        for code_ref, factor in zip(refs[:-2:2], factors):
            total = total + decode(code_ref[part, :], factor)
        out_ref[part, :] = total
        top = top + jnp.sum((total * total).reshape(-1, 8, total.shape[1]), axis=0)
    row = jnp.sum(sum(top[:, at : at + 128] for at in range(0, top.shape[1], 128)), axis=0, keepdims=True)
    squares_ref[...] = jnp.broadcast_to(row, squares_ref.shape) + jnp.where(step == 0, 0.0, squares_ref[...])


def finish(partial, messages, rows, count):
    height, hidden = partial.shape
    block = pl.BlockSpec((rows, hidden), lambda i: (i, 0))
    scales = pl.BlockSpec((PAD, hidden), lambda i: (height // PAD, 0))
    return pl.pallas_call(
        finish_kernel,
        grid=(height // rows,),
        in_specs=[block] + [block, scales] * len(messages),
        out_specs=[block, pl.BlockSpec((count, 128), lambda i: (0, 0))],
        out_shape=[
            jax.ShapeDtypeStruct(partial.shape, jnp.float32),
            jax.ShapeDtypeStruct((count, 128), jnp.float32),
        ],
        compiler_params=pltpu.CompilerParams(vmem_limit_bytes=LITTLE),
        cost_estimate=PIECE,
        name="finish",
    )(partial, *[m for message in messages for m in (message, message)])


def join_kernel(sum_ref, code_ref, scales_ref, out_ref, total_ref, out_scales_ref):
    step = pl.program_id(0)
    rows = sum_ref.shape[0]
    scales = scales_ref[...].astype(jnp.float32)
    row = lax.broadcasted_iota(jnp.int32, scales.shape, 0)
    factor = jnp.sum(jnp.where(row == step, scales, 0.0), axis=0, keepdims=True) * (1.0 / TOP)
    top = jnp.zeros((8, sum_ref.shape[1]), jnp.float32)
    for part in chunks(rows):
        total = sum_ref[part, :] + decode(code_ref[part, :], factor)
        total_ref[part, :] = total
        top = jnp.maximum(top, fold(total))
    scale = write_codes(total_ref, top, out_ref, pl.multiple_of(step * rows, rows))
    out_scales_ref[...] = jnp.where(row == step, scale, jnp.where(step == 0, 0.0, out_scales_ref[...]))
    out_ref[pl.ds(out_ref.shape[0] - PAD, PAD), :] = out_scales_ref[...].astype(jnp.bfloat16)


def join(partial, message, rows):
    height, hidden = partial.shape
    block = pl.BlockSpec((rows, hidden), lambda i: (i, 0))
    return pl.pallas_call(
        join_kernel,
        grid=(height // rows,),
        in_specs=[block, block, pl.BlockSpec((PAD, hidden), lambda i: (height // PAD, 0))],
        out_specs=pl.BlockSpec(message.shape, lambda i: (0, 0)),
        out_shape=jax.ShapeDtypeStruct(message.shape, message.dtype),
        scratch_shapes=[pltpu.VMEM((rows, hidden), jnp.float32), pltpu.VMEM((PAD, hidden), jnp.float32)],
        compiler_params=pltpu.CompilerParams(vmem_limit_bytes=LITTLE),
        cost_estimate=PIECE,
        name="join",
    )(partial, message, message)


def update_kernel(max_norm, states, total_ref, g_ref, p_ref, m1_ref, m2_ref, *outs):
    clip = clip_of(jnp.sum(total_ref[...], keepdims=True), max_norm)
    for part in chunks(g_ref.shape[0]):
        param, first, second = adam(clip, g_ref[part, :], p_ref[part, :], m1_ref[part, :], m2_ref[part, :])
        values = (param, first, second) if states else (param.astype(jnp.bfloat16),)
        for out, value in zip(outs, values):
            out[part, :] = value


def update(total, shard, param, first, second, max_norm, rows, states):
    block = pl.BlockSpec((rows, shard.shape[1]), lambda i: (i, 0))
    dtypes = [jnp.float32] * 3 if states else [jnp.bfloat16]
    return pl.pallas_call(
        lambda *refs: update_kernel(max_norm, states, *refs),
        grid=(shard.shape[0] // rows,),
        in_specs=[pl.BlockSpec(total.shape, lambda i: (0, 0))] + [block] * 4,
        out_specs=[block] * len(dtypes),
        out_shape=[jax.ShapeDtypeStruct(shard.shape, dtype) for dtype in dtypes],
        compiler_params=pltpu.CompilerParams(vmem_limit_bytes=LITTLE),
        cost_estimate=CHEAP,
        name="states" if states else "update",
    )(total, shard, param, first, second)


def behind_of(value, other, cost=CHEAP):
    return pl.pallas_call(
        lambda *refs: None,
        grid=(1,),
        in_specs=[pl.BlockSpec(memory_space=pl.ANY), pl.BlockSpec((PAD, 128), lambda i: (0, 0))],
        out_specs=pl.BlockSpec(memory_space=pl.ANY),
        out_shape=jax.ShapeDtypeStruct(value.shape, value.dtype),
        input_output_aliases={0: 0},
        compiler_params=pltpu.CompilerParams(vmem_limit_bytes=LITTLE),
        cost_estimate=cost,
        name="behind",
    )(value, other)


def both_of(own, other, after, cut):
    columns = own.shape[1]

    def kernel(own_ref, other_ref, after_ref, both_ref):
        both_ref[...] = jnp.where(pl.program_id(0) == 0, own_ref[...], other_ref[...])

    return pl.pallas_call(
        kernel,
        grid=(2,),
        in_specs=[
            pl.BlockSpec((cut, columns), lambda i: (0, 0)),
            pl.BlockSpec((cut, columns), lambda i: (0, 0)),
            pl.BlockSpec((PAD, 128), lambda i: (0, 0)),
        ],
        out_specs=pl.BlockSpec((cut, columns), lambda i: (i, 0)),
        out_shape=jax.ShapeDtypeStruct((2 * cut, columns), own.dtype),
        compiler_params=pltpu.CompilerParams(vmem_limit_bytes=LITTLE),
        cost_estimate=PIECE,
        name="both",
    )(own, other, after)


def fill_kernel(moves, count, *refs):
    out, sems = refs[-2:]
    r = lax.axis_index("dp")
    copies = []
    for at, (source, low, size, table, shard, first) in enumerate(moves):
        to = pl.multiple_of(lookup(table, r) * shard + first, PAD)
        copies.append(pltpu.make_async_copy(refs[source].at[low : low + size], out.at[pl.ds(to, size)], sems.at[at]))
        copies[-1].start()
    for copy in copies:
        copy.wait()


def fill(buffer, values, moves, height):
    columns = values[0].shape[1]
    return pl.pallas_call(
        lambda *refs: fill_kernel(moves, len(values), *refs),
        in_specs=[pl.BlockSpec(memory_space=pltpu.VMEM)] * len(values)
        + [pl.BlockSpec(memory_space=pltpu.HBM)] * (buffer is not None),
        out_specs=pl.BlockSpec(memory_space=pltpu.HBM),
        out_shape=jax.ShapeDtypeStruct((height, columns), values[0].dtype),
        input_output_aliases={} if buffer is None else {len(values): 0},
        scratch_shapes=[pltpu.SemaphoreType.DMA((len(moves),))],
        compiler_params=pltpu.CompilerParams(vmem_limit_bytes=LITTLE),
        cost_estimate=CHEAP,
        name="fill",
    )(*values, *([] if buffer is None else [buffer]))


def paired(weights, inputs, out_grads, master, moment1, moment2):
    n = lax.axis_size("dp")
    pairs = n // 2
    ring = list(range(0, pairs, 2)) + list(range(pairs - 1 - pairs % 2, 0, -2))
    place = {pair: at for at, pair in enumerate(ring)}

    def at_offset(r, offset, flip):
        return 2 * ring[(place[r // 2] + offset) % pairs] + ((r % 2) ^ flip)

    def table(offset, flip):
        return [at_offset(r, offset, flip) for r in range(n)]

    def send(value, offset, flip=0):
        return lax.ppermute(value, "dp", [(r, at_offset(r, offset, flip)) for r in range(n)])

    stacked = weights[0]
    x, dy = inputs[0], out_grads[0]
    width = x.shape[1]
    shard_rows = stacked.shape[0] // n
    rows = math.gcd(shard_rows, width, 256)

    steps = shard_rows // rows

    every, most, rest, end = list(range(steps)), list(range(steps - 1)), list(range(1, steps)), steps - 1

    def at(*blocks):
        return [(table(offset, flip), block) for offset, flip, block in blocks]

    def made(blocks, got=(), **more):
        return piece(x, dy, factors, rows, blocks, got, **more)

    factors, message = forward(x, dy, stacked, [at(*[(2, 1, b) for b in every])], rows)
    cross_far = send(message, 0, 1)
    message = made(at((-1, 0, end), (-1, 1, end)))
    ahead = send(message, -1)
    message = made(at(*[(-1, 1, b) for b in most]), after=message)
    cross_back = send(message, 0, 1)
    own_far = made(at(*[(2, 0, b) for b in every]), after=message, last=True)
    message = made(at(*[(1, 1, b) for b in every]), after=own_far)
    cross_next = send(message, 0, 1)
    message = made(at(*[(0, 1, b) for b in every]), [(ahead, [None] * end + [1])], after=message)
    cross_own = send(message, 0, 1)

    by_ring = send(join(own_far, cross_far, rows), 1)
    from_ahead = send(made(at(*[(-1, 0, b) for b in most]), [(cross_back, most)]), -1)
    from_behind = send(join(made(at(*[(1, 0, b) for b in every]), [(by_ring, every)], last=True), cross_next, rows), 1)
    partial = made(at(*[(0, 0, b) for b in every]), [(from_ahead, most + [None]), (ahead, [None] * end + [0])], last=True)
    shard, squares = finish(partial, [cross_own, from_behind], rows, n * lax.axis_size("section"))

    total = lax.all_to_all(squares, ("dp", "section"), 0, 0, tiled=True)
    max_norm = math.sqrt(lax.axis_size("section") * stacked.size)
    states = (shard, master[0], moment1[0], moment2[0], max_norm, rows // 2)
    (own,) = update(total, *states, False)

    cut = shard_rows * 7 // 12 // PAD * PAD
    other = send(own, 0, 1)
    behind = behind_of(send(own, 1), other)
    tail = send(own[cut:], -1)
    behind_cross = send(behind, 0, 1)
    far = send(behind, 1)
    tail = behind_of(tail, behind, cost_of(3.4))
    tail_cross = send(tail, 0, 1)
    both = send(both_of(own, other, behind_cross, cut), -1)
    far = behind_of(behind_of(far, behind_cross), tail_cross)
    far_cross = send(far, 0, 1)
    new_param, new_first, new_second = update(total, *states, True)

    def move(value, offset, flip, low=0, first=0, size=shard_rows):
        return (value, low, size, table(offset, flip), shard_rows, first)

    gathered = fill(
        None,
        [own, other, behind, tail, behind_cross, tail_cross, far],
        [
            move(0, 0, 0),
            move(1, 0, 1),
            move(2, -1, 0),
            move(3, 1, 0, 0, cut, shard_rows - cut),
            move(4, -1, 1),
            move(5, 1, 1, 0, cut, shard_rows - cut),
            move(6, -2, 0),
        ],
        stacked.shape[0],
    )
    gathered = fill(
        gathered,
        [both, far_cross],
        [move(0, 1, 0, 0, 0, cut), move(0, 1, 1, cut, 0, cut), move(1, -2, 1)],
        stacked.shape[0],
    )
    return new_param[None], new_first[None], new_second[None], gathered[None]


def local(weights, *rest):
    n = lax.axis_size("dp")
    height = weights.shape[1]
    shard, width = height // n, height // 3
    fits = n == 8 and height % n == 0 and math.gcd(shard, width, 256) % 128 == 0 and shard // math.gcd(shard, width, 256) > 2
    return (paired if fits else plain)(weights, *rest)


def solution(mesh):
    whole = P("section", None, None)
    split = P("section", "dp", None)
    return jax.shard_map(
        local,
        mesh=mesh,
        in_specs=(whole, split, split, split, split, split),
        out_specs=(split, split, split, whole),
        check_vma=False,
    )
```

profile of v0, /device:TPU:0, one launch (start us, length us, event | category | flops | bytes accessed | tf_op | source)
XLA Modules:
  0.0 96.9 jit_solution(4298621348125543206)
XLA Ops:
  0.6 0.0 copy-start.3
  0.6 6.2 %forward.1 = (bf16[3,512,256]{2,1,0:T(8,128)(2,1)}, bf16[784,256]{1,0:T(8,128)(2,1)}) custom-call(bf16[512,2048]{1,0:T(8,128)(2,1)} %bitcast.20, bf16[512,2048]{1,0:T(8,128)(2,1)} %bitcast.29, bf16[6144,256]{1,0:T(8,128)(2,1)} %bitcast.42), custom_call_target="tpu_custom_call" | custom-call | flops 1024 | bytes 1024 | tf_op jit(solution)/shard_map/forward/pallas_call | solution.py:204
  6.9 3.0 %collective-permute-start.4 = (bf16[784,256]{1,0:T(8,128)(2,1)}, bf16[784,256]{1,0:T(8,128)(2,1)S(1)}, u32[]{:S(2)}, u32[]{:S(2)}) collective-permute-start(bf16[784,256]{1,0:T(8,128)(2,1)} %get-tuple-element.12), channel_id=1, source_target_pairs={{0,4},{4,0},{8,12},{12,8},{16,20},{20,16},{24,28},{28,24},{1,5},{5... | collective-permute-start | bytes 1204232 | tf_op jit(solution)/shard_map/ppermute | solution.py:497
  9.9 0.0 copy-done.3
  9.9 0.0 copy-start.4
  9.9 1.6 %copy-done.4 = bf16[1,512,2048]{2,1,0:T(8,128)(2,1)S(1)} copy-done((bf16[1,512,2048]{2,1,0:T(8,128)(2,1)S(1)}, bf16[1,512,2048]{2,1,0:T(8,128)(2,1)}, u32[]{:S(2)}) %copy-start.4) | copy-done | bytes 2097176
  11.5 0.0 copy-start.6
  11.5 1.1 %copy-done.6 = bf16[3,512,256]{2,1,0:T(8,128)(2,1)S(1)} copy-done((bf16[3,512,256]{2,1,0:T(8,128)(2,1)S(1)}, bf16[3,512,256]{2,1,0:T(8,128)(2,1)}, u32[]{:S(2)}) %copy-start.6) | copy-done | bytes 786456
  12.6 1.1 %piece.8.refs_3_ = bf16[528,256]{1,0:T(8,128)(2,1)S(1)} custom-call(bf16[512,2048]{1,0:T(8,128)(2,1)S(1)} %bitcast.21, bf16[512,2048]{1,0:T(8,128)(2,1)S(1)} %bitcast.30, bf16[3,512,256]{2,1,0:T(8,128)(2,1)S(1)} %copy-done.6), custom_call_target="tpu_custom_call" | custom-call | flops 2006000000 | bytes 1024 | tf_op jit(solution)/shard_map/piece/pallas_call | solution.py:313
  13.7 1.6 %collective-permute-start.2 = (bf16[528,256]{1,0:T(8,128)(2,1)S(1)}, bf16[528,256]{1,0:T(8,128)(2,1)S(1)}, u32[]{:S(2)}, u32[]{:S(2)}) collective-permute-start(bf16[528,256]{1,0:T(8,128)(2,1)S(1)} %piece.8.refs_3_), channel_id=1, source_target_pairs={{0,8},{4,12},{8,24},{12,28},{16,0},{20,4},{24,16},{28,20},{1,9},{5... | collective-permute-start | bytes 811016 | tf_op jit(solution)/shard_map/ppermute | solution.py:497
  15.3 1.1 %piece.9.refs_3_ = bf16[528,256]{1,0:T(8,128)(2,1)S(1)} custom-call(bf16[512,2048]{1,0:T(8,128)(2,1)S(1)} %bitcast.22, bf16[512,2048]{1,0:T(8,128)(2,1)S(1)} %bitcast.31, bf16[3,512,256]{2,1,0:T(8,128)(2,1)S(1)} %copy-done.6, bf16[528,256]{1,0:T(8,128)(2,1)S(1)} %piece.8.refs_3_), custom_call_target="tpu_custom_call" | custom-call | flops 2006000000 | bytes 1024 | tf_op jit(solution)/shard_map/piece/pallas_call | solution.py:313
  16.3 0.6 collective-permute-start
  17.0 1.3 %piece.12.refs_3_.sum_ref = f32[768,256]{1,0:T(8,128)S(1)} custom-call(bf16[512,2048]{1,0:T(8,128)(2,1)S(1)} %bitcast.23, bf16[512,2048]{1,0:T(8,128)(2,1)S(1)} %bitcast.32, bf16[3,512,256]{2,1,0:T(8,128)(2,1)S(1)} %copy-done.6, bf16[528,256]{1,0:T(8,128)(2,1)S(1)} %piece.9.refs_3_), custom_call_target="tpu_custom_call" | custom-call | flops 2006000000 | bytes 1024 | tf_op jit(solution)/shard_map/piece/pallas_call | solution.py:313
  18.3 0.0 copy-start.5
  18.3 1.9 %collective-permute-done.4.code_ref.scales_ref = bf16[784,256]{1,0:T(8,128)(2,1)S(1)} collective-permute-done((bf16[784,256]{1,0:T(8,128)(2,1)}, bf16[784,256]{1,0:T(8,128)(2,1)S(1)}, u32[]{:S(2)}, u32[]{:S(2)}) %collective-permute-start.4) | collective-permute-done | bytes 401440 | tf_op jit(solution)/shard_map/ppermute | solution.py:497
  20.2 0.8 join.2
  21.0 3.2 %collective-permute-start.5 = (bf16[784,256]{1,0:T(8,128)(2,1)S(1)}, bf16[784,256]{1,0:T(8,128)(2,1)S(1)}, u32[]{:S(2)}, u32[]{:S(2)}) collective-permute-start(bf16[784,256]{1,0:T(8,128)(2,1)S(1)} %join.2), channel_id=1, source_target_pairs={{0,16},{4,20},{8,0},{12,4},{16,24},{20,28},{24,8},{28,12},{1,17},{... | collective-permute-start | bytes 1204232 | tf_op jit(solution)/shard_map/ppermute | solution.py:497
  24.2 0.0 copy-done.5
  24.2 1.6 %piece.13.refs_5_ = bf16[784,256]{1,0:T(8,128)(2,1)S(1)} custom-call(bf16[512,2048]{1,0:T(8,128)(2,1)S(1)} %bitcast.24, bf16[512,2048]{1,0:T(8,128)(2,1)S(1)} %bitcast.33, bf16[3,512,256]{2,1,0:T(8,128)(2,1)S(1)} %copy-done.6, f32[768,256]{1,0:T(8,128)S(1)} %piece.12.refs_3_.sum_ref), custom_call_target="tpu_custom_call" | custom-call | flops 2006000000 | bytes 1024 | tf_op jit(solution)/shard_map/piece/pallas_call | solution.py:313
  25.8 1.6 %collective-permute-start.6 = (bf16[784,256]{1,0:T(8,128)(2,1)S(1)}, bf16[784,256]{1,0:T(8,128)(2,1)S(1)}, u32[]{:S(2)}, u32[]{:S(2)}) collective-permute-start(bf16[784,256]{1,0:T(8,128)(2,1)S(1)} %piece.13.refs_5_), channel_id=1, source_target_pairs={{0,4},{4,0},{8,12},{12,8},{16,20},{20,16},{24,28},{28,24},{1,5},{5... | collective-permute-start | bytes 1204232 | tf_op jit(solution)/shard_map/ppermute | solution.py:497
  27.3 0.0 collective-permute-done.refs_3_.refs_4_
  27.3 1.1 %piece.10 = bf16[528,256]{1,0:T(8,128)(2,1)S(1)} custom-call(bf16[512,2048]{1,0:T(8,128)(2,1)S(1)} %bitcast.25, bf16[512,2048]{1,0:T(8,128)(2,1)S(1)} %bitcast.34, bf16[3,512,256]{2,1,0:T(8,128)(2,1)S(1)} %copy-done.6, bf16[528,256]{1,0:T(8,128)(2,1)S(1)} %collective-permute-done.refs_3_.refs_4_, bf16[528,256]{1,0:T(8,128)(2,1)S(1)} %collective-permute-done.refs_3_.refs_4_), custom_call_target="tpu_custom_call" | custom-call | flops 2006000000 | bytes 1024 | tf_op jit(solution)/shard_map/piece/pallas_call | solution.py:313
  28.5 0.9 collective-permute-start.1
  29.4 0.0 collective-permute-done.2.refs_5_.refs_6_.refs_3_.refs_4_
  29.4 1.7 %piece.14 = bf16[784,256]{1,0:T(8,128)(2,1)S(1)} custom-call(bf16[512,2048]{1,0:T(8,128)(2,1)S(1)} %bitcast.26, bf16[512,2048]{1,0:T(8,128)(2,1)S(1)} %bitcast.35, bf16[3,512,256]{2,1,0:T(8,128)(2,1)S(1)} %copy-done.6, bf16[528,256]{1,0:T(8,128)(2,1)S(1)} %collective-permute-done.2.refs_5_.refs_6_.refs_3_.refs_4_, ...), custom_call_target="tpu_custom_call" | custom-call | flops 2006000000 | bytes 1024 | tf_op jit(solution)/shard_map/piece/pallas_call | solution.py:313
  31.1 1.5 %collective-permute-start.3 = (bf16[784,256]{1,0:T(8,128)(2,1)S(1)}, bf16[784,256]{1,0:T(8,128)(2,1)S(1)}, u32[]{:S(2)}, u32[]{:S(2)}) collective-permute-start(bf16[784,256]{1,0:T(8,128)(2,1)S(1)} %piece.14), channel_id=1, source_target_pairs={{0,4},{4,0},{8,12},{12,8},{16,20},{20,16},{24,28},{28,24},{1,5},{5... | collective-permute-start | bytes 1204232 | tf_op jit(solution)/shard_map/ppermute | solution.py:497
  32.5 1.1 %collective-permute-done.5.refs_3_.refs_4_ = bf16[784,256]{1,0:T(8,128)(2,1)S(1)} collective-permute-done((bf16[784,256]{1,0:T(8,128)(2,1)S(1)}, bf16[784,256]{1,0:T(8,128)(2,1)S(1)}, u32[]{:S(2)}, u32[]{:S(2)}) %collective-permute-start.5) | collective-permute-done | bytes 401440 | tf_op jit(solution)/shard_map/ppermute | solution.py:497
  33.6 1.4 %piece.15.sum_ref = f32[768,256]{1,0:T(8,128)S(1)} custom-call(bf16[512,2048]{1,0:T(8,128)(2,1)S(1)} %bitcast.27, bf16[512,2048]{1,0:T(8,128)(2,1)S(1)} %bitcast.36, bf16[3,512,256]{2,1,0:T(8,128)(2,1)S(1)} %copy-done.6, bf16[784,256]{1,0:T(8,128)(2,1)S(1)} %collective-permute-done.5.refs_3_.refs_4_, bf16[784,256]{1,0:T(8,128)(2,1)S(1)} %collective-permute-done.5.refs_3_.refs_4_), custom_call_target="tpu_custom_call" | custom-call | flops 2006000000 | bytes 1024 | tf_op jit(solution)/shard_map/piece/pallas_call | solution.py:313
  35.0 3.1 %collective-permute-done.6.code_ref.scales_ref = bf16[784,256]{1,0:T(8,128)(2,1)S(1)} collective-permute-done((bf16[784,256]{1,0:T(8,128)(2,1)S(1)}, bf16[784,256]{1,0:T(8,128)(2,1)S(1)}, u32[]{:S(2)}, u32[]{:S(2)}) %collective-permute-start.6) | collective-permute-done | bytes 401440 | tf_op jit(solution)/shard_map/ppermute | solution.py:497
  38.0 0.8 join.3
  38.8 1.6 %collective-permute-start.7 = (bf16[784,256]{1,0:T(8,128)(2,1)S(1)}, bf16[784,256]{1,0:T(8,128)(2,1)S(1)}, u32[]{:S(2)}, u32[]{:S(2)}) collective-permute-start(bf16[784,256]{1,0:T(8,128)(2,1)S(1)} %join.3), channel_id=1, source_target_pairs={{0,16},{4,20},{8,0},{12,4},{16,24},{20,28},{24,8},{28,12},{1,17},{... | collective-permute-start | bytes 1204232 | tf_op jit(solution)/shard_map/ppermute | solution.py:497
  40.5 0.0 collective-permute-done.1.refs_3_.refs_4_
  40.5 1.8 %piece.11.sum_ref = f32[768,256]{1,0:T(8,128)S(1)} custom-call(bf16[512,2048]{1,0:T(8,128)(2,1)S(1)} %bitcast.28, bf16[512,2048]{1,0:T(8,128)(2,1)S(1)} %bitcast.37, bf16[3,512,256]{2,1,0:T(8,128)(2,1)S(1)} %copy-done.6, bf16[528,256]{1,0:T(8,128)(2,1)S(1)} %collective-permute-done.1.refs_3_.refs_4_, ...), custom_call_target="tpu_custom_call" | custom-call | flops 2006000000 | bytes 1024 | tf_op jit(solution)/shard_map/piece/pallas_call | solution.py:313
  42.3 0.0 copy-start
  42.3 0.0 copy-start.1
  42.3 0.0 copy-start.2
  42.3 0.9 collective-permute-done.3.refs_0_.refs_1_
  43.2 3.7 %collective-permute-done.7.refs_2_.refs_3_ = bf16[784,256]{1,0:T(8,128)(2,1)S(1)} collective-permute-done((bf16[784,256]{1,0:T(8,128)(2,1)S(1)}, bf16[784,256]{1,0:T(8,128)(2,1)S(1)}, u32[]{:S(2)}, u32[]{:S(2)}) %collective-permute-start.7) | collective-permute-done | bytes 401440 | tf_op jit(solution)/shard_map/ppermute | solution.py:497
  46.9 0.9 finish.1
  47.8 12.3 %all_to_all.11 = f32[32,1,128]{2,1,0:T(1,128)S(1)} all-to-all(f32[32,1,128]{2,1,0:T(1,128)S(1)} %bitcast.40), channel_id=1, replica_groups=mesh['dp'=8,'section'=4] {'dp','section'}, dimensions={0} | all-to-all | bytes 32768 | tf_op jit(solution)/shard_map/all_to_all | solution.py:533
  60.1 0.0 copy-done
  60.1 0.0 copy-done.1
  60.1 0.0 copy-done.2
  60.1 1.5 %update.1.own_ref.refs_0_ = bf16[768,256]{1,0:T(8,128)(2,1)S(1)} custom-call(f32[32,128]{1,0:T(8,128)S(1)} %bitcast.38, f32[768,256]{1,0:T(8,128)S(1)} %get-tuple-element.14.refs_1_, f32[768,256]{1,0:T(8,128)S(1)} %bitcast.14, f32[768,256]{1,0:T(8,128)S(1)} %bitcast.16, f32[768,256]{1,0:T(8,128)S(1)} %bitcast.18), custom_call_target="tpu_custom_call" | custom-call | flops 1024 | bytes 1024 | tf_op jit(solution)/shard_map/update/pallas_call | solution.py:408
  61.6 0.6 collective-permute-start.9
  62.3 0.6 collective-permute-start.8
  62.9 1.5 %collective-permute-start.13 = (bf16[320,256]{1,0:T(8,128)(2,1)S(1)}, bf16[320,256]{1,0:T(8,128)(2,1)S(1)}, u32[]{:S(2)}, u32[]{:S(2)}) collective-permute-start(bf16[320,256]{1,0:T(8,128)(2,1)S(1)} %slice.4), channel_id=1, source_target_pairs={{0,8},{4,12},{8,24},{12,28},{16,0},{20,4},{24,16},{28,20},{1,9},{5... | collective-permute-start | bytes 491528 | tf_op jit(solution)/shard_map/ppermute | solution.py:497
  64.4 8.8 %collective-permute-done.9.refs_0_ = bf16[768,256]{1,0:T(8,128)(2,1)S(1)} collective-permute-done((bf16[768,256]{1,0:T(8,128)(2,1)S(1)}, bf16[768,256]{1,0:T(8,128)(2,1)S(1)}, u32[]{:S(2)}, u32[]{:S(2)}) %collective-permute-start.9) | collective-permute-done | bytes 393248 | tf_op jit(solution)/shard_map/ppermute | solution.py:497
  73.1 0.0 collective-permute-done.8.refs_1_.other_ref
  73.1 0.3 collective-permute-start.10
  73.4 2.4 %collective-permute-start.12 = (bf16[768,256]{1,0:T(8,128)(2,1)S(1)}, bf16[768,256]{1,0:T(8,128)(2,1)S(1)}, u32[]{:S(2)}, u32[]{:S(2)}) collective-permute-start(bf16[768,256]{1,0:T(8,128)(2,1)S(1)} %behind.4.refs_1_.refs_2_), channel_id=1, source_target_pairs={{0,16},{4,20},{8,0},{12,4},{16,24},{20,28},{24,8},{28,12},{1,17},{... | collective-permute-start | bytes 1179656 | tf_op jit(solution)/shard_map/ppermute | solution.py:497
  75.8 1.8 %collective-permute-done.13.refs_0_ = bf16[320,256]{1,0:T(8,128)(2,1)S(1)} collective-permute-done((bf16[320,256]{1,0:T(8,128)(2,1)S(1)}, bf16[320,256]{1,0:T(8,128)(2,1)S(1)}, u32[]{:S(2)}, u32[]{:S(2)}) %collective-permute-start.13) | collective-permute-done | bytes 163872 | tf_op jit(solution)/shard_map/ppermute | solution.py:497
  77.6 0.1 collective-permute-start.14
  77.6 6.8 %collective-permute-done.10.after_ref.refs_1_.refs_4_ = bf16[768,256]{1,0:T(8,128)(2,1)S(1)} collective-permute-done((bf16[768,256]{1,0:T(8,128)(2,1)S(1)}, bf16[768,256]{1,0:T(8,128)(2,1)S(1)}, u32[]{:S(2)}, u32[]{:S(2)}) %collective-permute-start.10) | collective-permute-done | bytes 393248 | tf_op jit(solution)/shard_map/ppermute | solution.py:497
  84.5 0.1 both.1
  84.6 1.4 %collective-permute-start.11 = (bf16[896,256]{1,0:T(8,128)(2,1)S(1)}, bf16[896,256]{1,0:T(8,128)(2,1)S(1)}, u32[]{:S(2)}, u32[]{:S(2)}) collective-permute-start(bf16[896,256]{1,0:T(8,128)(2,1)S(1)} %both.1), channel_id=1, source_target_pairs={{0,8},{4,12},{8,24},{12,28},{16,0},{20,4},{24,16},{28,20},{1,9},{5... | collective-permute-start | bytes 1376264 | tf_op jit(solution)/shard_map/ppermute | solution.py:497
  85.9 0.4 collective-permute-done.12.refs_0_
  86.4 0.0 collective-permute-done.14.refs_1_.refs_5_
  86.4 0.9 collective-permute-start.15
  87.3 3.1 %states.1 = (f32[768,256]{1,0:T(8,128)}, f32[768,256]{1,0:T(8,128)}, f32[768,256]{1,0:T(8,128)}) custom-call(f32[32,128]{1,0:T(8,128)S(1)} %bitcast.39, f32[768,256]{1,0:T(8,128)S(1)} %get-tuple-element.14.refs_1_, f32[768,256]{1,0:T(8,128)S(1)} %bitcast.15, f32[768,256]{1,0:T(8,128)S(1)} %bitcast.17, f32[768,256]{1,0:T(8,128)S(1)} %bitcast.19), custom_call_target="tpu_custom_call" | custom-call | flops 1024 | bytes 1024 | tf_op jit(solution)/shard_map/states/pallas_call | solution.py:408
  90.4 1.4 %fill.2.refs_2_ = bf16[6144,256]{1,0:T(8,128)(2,1)} custom-call(bf16[768,256]{1,0:T(8,128)(2,1)S(1)} %update.1.own_ref.refs_0_, bf16[768,256]{1,0:T(8,128)(2,1)S(1)} %collective-permute-done.8.refs_1_.other_ref, bf16[768,256]{1,0:T(8,128)(2,1)S(1)} %behind.4.refs_1_.refs_2_, bf16[320,256]{1,0:T(8,128)(2,1)S(1)} %behind.6.refs_3_, ...), custom_call_target="tpu_custom_call" | custom-call | flops 1024 | bytes 1024 | tf_op jit(solution)/shard_map/fill/pallas_call | solution.py:470
  91.8 4.2 %collective-permute-done.15.refs_1_ = bf16[768,256]{1,0:T(8,128)(2,1)S(1)} collective-permute-done((bf16[768,256]{1,0:T(8,128)(2,1)S(1)}, bf16[768,256]{1,0:T(8,128)(2,1)S(1)}, u32[]{:S(2)}, u32[]{:S(2)}) %collective-permute-start.15) | collective-permute-done | bytes 393248 | tf_op jit(solution)/shard_map/ppermute | solution.py:497
  96.0 0.0 collective-permute-done.11.refs_0_
  96.0 0.9 fill.3
  (5 shorter events, 0.0 us)
Async XLA Ops:
  0.6 9.2 %copy-start.3 = (bf16[1,512,2048]{2,1,0:T(8,128)(2,1)S(1)}, bf16[1,512,2048]{2,1,0:T(8,128)(2,1)}, u32[]{:S(2)}) copy-start(bf16[1,512,2048]{2,1,0:T(8,128)(2,1)} %param.7) | copy-start | bytes 6291460
  6.9 13.3 %collective-permute-start.4 = (bf16[784,256]{1,0:T(8,128)(2,1)}, bf16[784,256]{1,0:T(8,128)(2,1)S(1)}, u32[]{:S(2)}, u32[]{:S(2)}) collective-permute-start(bf16[784,256]{1,0:T(8,128)(2,1)} %get-tuple-element.12), channel_id=1, source_target_pairs={{0,4},{4,0},{8,12},{12,8},{16,20},{20,16},{24,28},{28,24},{1,5},{5... | collective-permute-start | bytes 1204232 | tf_op jit(solution)/shard_map/ppermute | solution.py:497
  9.9 1.6 %copy-start.4 = (bf16[1,512,2048]{2,1,0:T(8,128)(2,1)S(1)}, bf16[1,512,2048]{2,1,0:T(8,128)(2,1)}, u32[]{:S(2)}) copy-start(bf16[1,512,2048]{2,1,0:T(8,128)(2,1)} %param.8) | copy-start | bytes 6291460
  11.5 1.1 %copy-start.6 = (bf16[3,512,256]{2,1,0:T(8,128)(2,1)S(1)}, bf16[3,512,256]{2,1,0:T(8,128)(2,1)}, u32[]{:S(2)}) copy-start(bf16[3,512,256]{2,1,0:T(8,128)(2,1)} %get-tuple-element.11.refs_2_) | copy-start | bytes 2359300
  13.7 15.7 %collective-permute-start.2 = (bf16[528,256]{1,0:T(8,128)(2,1)S(1)}, bf16[528,256]{1,0:T(8,128)(2,1)S(1)}, u32[]{:S(2)}, u32[]{:S(2)}) collective-permute-start(bf16[528,256]{1,0:T(8,128)(2,1)S(1)} %piece.8.refs_3_), channel_id=1, source_target_pairs={{0,8},{4,12},{8,24},{12,28},{16,0},{20,4},{24,16},{28,20},{1,9},{5... | collective-permute-start | bytes 811016 | tf_op jit(solution)/shard_map/ppermute | solution.py:497
  16.3 11.0 %collective-permute-start = (bf16[528,256]{1,0:T(8,128)(2,1)S(1)}, bf16[528,256]{1,0:T(8,128)(2,1)S(1)}, u32[]{:S(2)}, u32[]{:S(2)}) collective-permute-start(bf16[528,256]{1,0:T(8,128)(2,1)S(1)} %piece.9.refs_3_), channel_id=1, source_target_pairs={{0,4},{4,0},{8,12},{12,8},{16,20},{20,16},{24,28},{28,24},{1,5},{5... | collective-permute-start | bytes 811016 | tf_op jit(solution)/shard_map/ppermute | solution.py:497
  18.3 5.9 %copy-start.5 = (bf16[1,512,2048]{2,1,0:T(8,128)(2,1)S(1)}, bf16[1,512,2048]{2,1,0:T(8,128)(2,1)}, u32[]{:S(2)}) copy-start(bf16[1,512,2048]{2,1,0:T(8,128)(2,1)} %param.8) | copy-start | bytes 6291460
  21.0 12.6 %collective-permute-start.5 = (bf16[784,256]{1,0:T(8,128)(2,1)S(1)}, bf16[784,256]{1,0:T(8,128)(2,1)S(1)}, u32[]{:S(2)}, u32[]{:S(2)}) collective-permute-start(bf16[784,256]{1,0:T(8,128)(2,1)S(1)} %join.2), channel_id=1, source_target_pairs={{0,16},{4,20},{8,0},{12,4},{16,24},{20,28},{24,8},{28,12},{1,17},{... | collective-permute-start | bytes 1204232 | tf_op jit(solution)/shard_map/ppermute | solution.py:497
  25.8 12.3 %collective-permute-start.6 = (bf16[784,256]{1,0:T(8,128)(2,1)S(1)}, bf16[784,256]{1,0:T(8,128)(2,1)S(1)}, u32[]{:S(2)}, u32[]{:S(2)}) collective-permute-start(bf16[784,256]{1,0:T(8,128)(2,1)S(1)} %piece.13.refs_5_), channel_id=1, source_target_pairs={{0,4},{4,0},{8,12},{12,8},{16,20},{20,16},{24,28},{28,24},{1,5},{5... | collective-permute-start | bytes 1204232 | tf_op jit(solution)/shard_map/ppermute | solution.py:497
  28.5 12.0 %collective-permute-start.1 = (bf16[528,256]{1,0:T(8,128)(2,1)S(1)}, bf16[528,256]{1,0:T(8,128)(2,1)S(1)}, u32[]{:S(2)}, u32[]{:S(2)}) collective-permute-start(bf16[528,256]{1,0:T(8,128)(2,1)S(1)} %piece.10), channel_id=1, source_target_pairs={{0,8},{4,12},{8,24},{12,28},{16,0},{20,4},{24,16},{28,20},{1,9},{5... | collective-permute-start | bytes 811016 | tf_op jit(solution)/shard_map/ppermute | solution.py:497
  31.1 12.1 %collective-permute-start.3 = (bf16[784,256]{1,0:T(8,128)(2,1)S(1)}, bf16[784,256]{1,0:T(8,128)(2,1)S(1)}, u32[]{:S(2)}, u32[]{:S(2)}) collective-permute-start(bf16[784,256]{1,0:T(8,128)(2,1)S(1)} %piece.14), channel_id=1, source_target_pairs={{0,4},{4,0},{8,12},{12,8},{16,20},{20,16},{24,28},{28,24},{1,5},{5... | collective-permute-start | bytes 1204232 | tf_op jit(solution)/shard_map/ppermute | solution.py:497
  38.8 8.1 %collective-permute-start.7 = (bf16[784,256]{1,0:T(8,128)(2,1)S(1)}, bf16[784,256]{1,0:T(8,128)(2,1)S(1)}, u32[]{:S(2)}, u32[]{:S(2)}) collective-permute-start(bf16[784,256]{1,0:T(8,128)(2,1)S(1)} %join.3), channel_id=1, source_target_pairs={{0,16},{4,20},{8,0},{12,4},{16,24},{20,28},{24,8},{28,12},{1,17},{... | collective-permute-start | bytes 1204232 | tf_op jit(solution)/shard_map/ppermute | solution.py:497
  42.3 17.8 %copy-start = (f32[1,768,256]{2,1,0:T(8,128)S(1)}, f32[1,768,256]{2,1,0:T(8,128)}, u32[]{:S(2)}) copy-start(f32[1,768,256]{2,1,0:T(8,128)} %param.9) | copy-start | bytes 2359300
  42.3 17.8 %copy-start.1 = (f32[1,768,256]{2,1,0:T(8,128)S(1)}, f32[1,768,256]{2,1,0:T(8,128)}, u32[]{:S(2)}) copy-start(f32[1,768,256]{2,1,0:T(8,128)} %param.10) | copy-start | bytes 2359300
  42.3 17.8 %copy-start.2 = (f32[1,768,256]{2,1,0:T(8,128)S(1)}, f32[1,768,256]{2,1,0:T(8,128)}, u32[]{:S(2)}) copy-start(f32[1,768,256]{2,1,0:T(8,128)} %param.11) | copy-start | bytes 2359300
  61.6 11.5 %collective-permute-start.9 = (bf16[768,256]{1,0:T(8,128)(2,1)S(1)}, bf16[768,256]{1,0:T(8,128)(2,1)S(1)}, u32[]{:S(2)}, u32[]{:S(2)}) collective-permute-start(bf16[768,256]{1,0:T(8,128)(2,1)S(1)} %update.1.own_ref.refs_0_), channel_id=1, source_target_pairs={{0,16},{4,20},{8,0},{12,4},{16,24},{20,28},{24,8},{28,12},{1,17},{... | collective-permute-start | bytes 1179656 | tf_op jit(solution)/shard_map/ppermute | solution.py:497
  62.3 10.8 %collective-permute-start.8 = (bf16[768,256]{1,0:T(8,128)(2,1)S(1)}, bf16[768,256]{1,0:T(8,128)(2,1)S(1)}, u32[]{:S(2)}, u32[]{:S(2)}) collective-permute-start(bf16[768,256]{1,0:T(8,128)(2,1)S(1)} %update.1.own_ref.refs_0_), channel_id=1, source_target_pairs={{0,4},{4,0},{8,12},{12,8},{16,20},{20,16},{24,28},{28,24},{1,5},{5... | collective-permute-start | bytes 1179656 | tf_op jit(solution)/shard_map/ppermute | solution.py:497
  62.9 14.7 %collective-permute-start.13 = (bf16[320,256]{1,0:T(8,128)(2,1)S(1)}, bf16[320,256]{1,0:T(8,128)(2,1)S(1)}, u32[]{:S(2)}, u32[]{:S(2)}) collective-permute-start(bf16[320,256]{1,0:T(8,128)(2,1)S(1)} %slice.4), channel_id=1, source_target_pairs={{0,8},{4,12},{8,24},{12,28},{16,0},{20,4},{24,16},{28,20},{1,9},{5... | collective-permute-start | bytes 491528 | tf_op jit(solution)/shard_map/ppermute | solution.py:497
  73.1 11.4 %collective-permute-start.10 = (bf16[768,256]{1,0:T(8,128)(2,1)S(1)}, bf16[768,256]{1,0:T(8,128)(2,1)S(1)}, u32[]{:S(2)}, u32[]{:S(2)}) collective-permute-start(bf16[768,256]{1,0:T(8,128)(2,1)S(1)} %behind.4.refs_1_.refs_2_), channel_id=1, source_target_pairs={{0,4},{4,0},{8,12},{12,8},{16,20},{20,16},{24,28},{28,24},{1,5},{5... | collective-permute-start | bytes 1179656 | tf_op jit(solution)/shard_map/ppermute | solution.py:497
  73.4 13.0 %collective-permute-start.12 = (bf16[768,256]{1,0:T(8,128)(2,1)S(1)}, bf16[768,256]{1,0:T(8,128)(2,1)S(1)}, u32[]{:S(2)}, u32[]{:S(2)}) collective-permute-start(bf16[768,256]{1,0:T(8,128)(2,1)S(1)} %behind.4.refs_1_.refs_2_), channel_id=1, source_target_pairs={{0,16},{4,20},{8,0},{12,4},{16,24},{20,28},{24,8},{28,12},{1,17},{... | collective-permute-start | bytes 1179656 | tf_op jit(solution)/shard_map/ppermute | solution.py:497
  77.6 8.8 %collective-permute-start.14 = (bf16[320,256]{1,0:T(8,128)(2,1)S(1)}, bf16[320,256]{1,0:T(8,128)(2,1)S(1)}, u32[]{:S(2)}, u32[]{:S(2)}) collective-permute-start(bf16[320,256]{1,0:T(8,128)(2,1)S(1)} %behind.6.refs_3_), channel_id=1, source_target_pairs={{0,4},{4,0},{8,12},{12,8},{16,20},{20,16},{24,28},{28,24},{1,5},{5... | collective-permute-start | bytes 491528 | tf_op jit(solution)/shard_map/ppermute | solution.py:497
  84.6 11.4 %collective-permute-start.11 = (bf16[896,256]{1,0:T(8,128)(2,1)S(1)}, bf16[896,256]{1,0:T(8,128)(2,1)S(1)}, u32[]{:S(2)}, u32[]{:S(2)}) collective-permute-start(bf16[896,256]{1,0:T(8,128)(2,1)S(1)} %both.1), channel_id=1, source_target_pairs={{0,8},{4,12},{8,24},{12,28},{16,0},{20,4},{24,16},{28,20},{1,9},{5... | collective-permute-start | bytes 1376264 | tf_op jit(solution)/shard_map/ppermute | solution.py:497
  86.4 9.6 %collective-permute-start.15 = (bf16[768,256]{1,0:T(8,128)(2,1)S(1)}, bf16[768,256]{1,0:T(8,128)(2,1)S(1)}, u32[]{:S(2)}, u32[]{:S(2)}) collective-permute-start(bf16[768,256]{1,0:T(8,128)(2,1)S(1)} %behind.7.refs_6_), channel_id=1, source_target_pairs={{0,4},{4,0},{8,12},{12,8},{16,20},{20,16},{24,28},{28,24},{1,5},{5... | collective-permute-start | bytes 1179656 | tf_op jit(solution)/shard_map/ppermute | solution.py:497
where the time goes:
time: 97.1 us; the launch traced here: 96.9 us
  waiting for transfers between devices  32.7 us (34%)
  Pallas kernels  26.6 us (27%)
  starting transfers between devices  21.8 us (22%)
  blocking collectives  12.3 us (13%)
  local copies, waits for them, and re-layouts  2.76 us (3%)
    ppermute x16, waiting for transfers between devices, send(): lax.ppermute(value, 'dp', [(r, at_offset(r, offset, flip)) for r in range...  32.7 us
    ppermute x16, starting transfers between devices, send(): lax.ppermute(value, 'dp', [(r, at_offset(r, offset, flip)) for r in range...  21.8 us
    all_to_all x1, blocking collectives, paired(): total = lax.all_to_all(squares, ('dp', 'section'), 0, 0, tiled=True)  12.3 us
    pallas_call x8, Pallas kernels, piece(): pl.pallas_call(lambda *refs: piece_kernel(place, per, [parts for _, parts...  10.9 us
    pallas_call x1, Pallas kernels, forward(): pl.pallas_call(lambda *refs: forward_kernel(places, rows, *refs), in_spec...  6.21 us
    pallas_call x2, Pallas kernels, update(): pl.pallas_call(lambda *refs: update_kernel(max_norm, states, *refs), grid...  4.58 us
    unnamed x14, local copies, waits for them, and re-layouts  2.75 us
    pallas_call x2, Pallas kernels, fill(): pl.pallas_call(lambda *refs: fill_kernel(moves, len(values), *refs), in_s...  2.35 us
  transfers between devices with their start and end apart: 16, of which 10 were waited for; matrix products, arithmetic and copies ran while one was open for 0% of the time, Pallas kernels for 18%

commit v1 on v0

--- a/solution.py
+++ b/solution.py
@@ -323,34 +323,30 @@
     )(*operands)
 
 
-def finish_kernel(sum_ref, *refs):
-    step = pl.program_id(0)
+def finish_kernel(rows, sum_ref, *refs):
     out_ref, squares_ref = refs[-2:]
-    factors = []
-    for scales_ref in refs[1:-2:2]:
-        scales = scales_ref[...].astype(jnp.float32)
-        row = lax.broadcasted_iota(jnp.int32, scales.shape, 0)
-        factors.append(jnp.sum(jnp.where(row == step, scales, 0.0), axis=0, keepdims=True) * (1.0 / TOP))
-    top = jnp.zeros((8, out_ref.shape[1]), jnp.float32)
-    for part in chunks(out_ref.shape[0]):
+    height, hidden = out_ref.shape
+    codes = refs[:-2]
+    scales = [code[height:, :].astype(jnp.float32) * (1.0 / TOP) for code in codes]
+    top = jnp.zeros((8, hidden), jnp.float32)
+    for part in chunks(height):
+        block = part.start // rows
         total = sum_ref[part, :]
-        for code_ref, factor in zip(refs[:-2:2], factors):
-            total = total + decode(code_ref[part, :], factor)
+        for code, factor in zip(codes, scales):
+            total = total + decode(code[part, :], factor[block : block + 1])
         out_ref[part, :] = total
-        top = top + jnp.sum((total * total).reshape(-1, 8, total.shape[1]), axis=0)
-    row = jnp.sum(sum(top[:, at : at + 128] for at in range(0, top.shape[1], 128)), axis=0, keepdims=True)
-    squares_ref[...] = jnp.broadcast_to(row, squares_ref.shape) + jnp.where(step == 0, 0.0, squares_ref[...])
+        top = top + jnp.sum((total * total).reshape(-1, 8, hidden), axis=0)
+    row = jnp.sum(sum(top[:, at : at + 128] for at in range(0, hidden, 128)), axis=0, keepdims=True)
+    squares_ref[...] = jnp.broadcast_to(row, squares_ref.shape)
 
 
 def finish(partial, messages, rows, count):
-    height, hidden = partial.shape
-    block = pl.BlockSpec((rows, hidden), lambda i: (i, 0))
-    scales = pl.BlockSpec((PAD, hidden), lambda i: (height // PAD, 0))
-    return pl.pallas_call(
-        finish_kernel,
-        grid=(height // rows,),
-        in_specs=[block] + [block, scales] * len(messages),
-        out_specs=[block, pl.BlockSpec((count, 128), lambda i: (0, 0))],
+    whole = pl.BlockSpec(partial.shape, lambda i: (0, 0))
+    return pl.pallas_call(
+        lambda *refs: finish_kernel(rows, *refs),
+        grid=(1,),
+        in_specs=[whole] + [pl.BlockSpec(message.shape, lambda i: (0, 0)) for message in messages],
+        out_specs=[whole, pl.BlockSpec((count, 128), lambda i: (0, 0))],
         out_shape=[
             jax.ShapeDtypeStruct(partial.shape, jnp.float32),
             jax.ShapeDtypeStruct((count, 128), jnp.float32),
@@ -358,39 +354,39 @@
         compiler_params=pltpu.CompilerParams(vmem_limit_bytes=LITTLE),
         cost_estimate=PIECE,
         name="finish",
-    )(partial, *[m for message in messages for m in (message, message)])
-
-
-def join_kernel(sum_ref, code_ref, scales_ref, out_ref, total_ref, out_scales_ref):
-    step = pl.program_id(0)
-    rows = sum_ref.shape[0]
-    scales = scales_ref[...].astype(jnp.float32)
+    )(partial, *messages)
+
+
+def join_kernel(rows, sum_ref, code_ref, out_ref, total_ref):
+    height, hidden = sum_ref.shape
+    scales = code_ref[height:, :].astype(jnp.float32) * (1.0 / TOP)
     row = lax.broadcasted_iota(jnp.int32, scales.shape, 0)
-    factor = jnp.sum(jnp.where(row == step, scales, 0.0), axis=0, keepdims=True) * (1.0 / TOP)
-    top = jnp.zeros((8, sum_ref.shape[1]), jnp.float32)
-    for part in chunks(rows):
-        total = sum_ref[part, :] + decode(code_ref[part, :], factor)
-        total_ref[part, :] = total
-        top = jnp.maximum(top, fold(total))
-    scale = write_codes(total_ref, top, out_ref, pl.multiple_of(step * rows, rows))
-    out_scales_ref[...] = jnp.where(row == step, scale, jnp.where(step == 0, 0.0, out_scales_ref[...]))
-    out_ref[pl.ds(out_ref.shape[0] - PAD, PAD), :] = out_scales_ref[...].astype(jnp.bfloat16)
+    new_scales = jnp.zeros_like(scales)
+    for block in range(height // rows):
+        top = jnp.zeros((8, hidden), jnp.float32)
+        for part in chunks(rows):
+            here = slice(block * rows + part.start, block * rows + part.stop)
+            total = sum_ref[here, :] + decode(code_ref[here, :], scales[block : block + 1])
+            total_ref[part, :] = total
+            top = jnp.maximum(top, fold(total))
+        scale = write_codes(total_ref, top, out_ref, block * rows)
+        new_scales = jnp.where(row == block, scale, new_scales)
+    out_ref[height:, :] = new_scales.astype(jnp.bfloat16)
 
 
 def join(partial, message, rows):
-    height, hidden = partial.shape
-    block = pl.BlockSpec((rows, hidden), lambda i: (i, 0))
-    return pl.pallas_call(
-        join_kernel,
-        grid=(height // rows,),
-        in_specs=[block, block, pl.BlockSpec((PAD, hidden), lambda i: (height // PAD, 0))],
-        out_specs=pl.BlockSpec(message.shape, lambda i: (0, 0)),
+    whole = pl.BlockSpec(message.shape, lambda i: (0, 0))
+    return pl.pallas_call(
+        lambda *refs: join_kernel(rows, *refs),
+        grid=(1,),
+        in_specs=[pl.BlockSpec(partial.shape, lambda i: (0, 0)), whole],
+        out_specs=whole,
         out_shape=jax.ShapeDtypeStruct(message.shape, message.dtype),
-        scratch_shapes=[pltpu.VMEM((rows, hidden), jnp.float32), pltpu.VMEM((PAD, hidden), jnp.float32)],
+        scratch_shapes=[pltpu.VMEM((rows, partial.shape[1]), jnp.float32)],
         compiler_params=pltpu.CompilerParams(vmem_limit_bytes=LITTLE),
         cost_estimate=PIECE,
         name="join",
-    )(partial, message, message)
+    )(partial, message)
 
 
 def update_kernel(max_norm, states, total_ref, g_ref, p_ref, m1_ref, m2_ref, *outs):
@@ -532,8 +528,8 @@
 
     total = lax.all_to_all(squares, ("dp", "section"), 0, 0, tiled=True)
     max_norm = math.sqrt(lax.axis_size("section") * stacked.size)
-    states = (shard, master[0], moment1[0], moment2[0], max_norm, rows // 2)
-    (own,) = update(total, *states, False)
+    states = (shard, master[0], moment1[0], moment2[0], max_norm)
+    (own,) = update(total, *states, shard_rows, False)
 
     cut = shard_rows * 7 // 12 // PAD * PAD
     other = send(own, 0, 1)
@@ -546,7 +542,7 @@
     both = send(both_of(own, other, behind_cross, cut), -1)
     far = behind_of(behind_of(far, behind_cross), tail_cross)
     far_cross = send(far, 0, 1)
-    new_param, new_first, new_second = update(total, *states, True)
+    new_param, new_first, new_second = update(total, *states, rows, True)
 
     def move(value, offset, flip, low=0, first=0, size=shard_rows):
         return (value, low, size, table(offset, flip), shard_rows, first)

time: 97.1 us -> 96.3 us (level)
  Pallas kernels: 26.6 us -> 24.8 us
    pallas_call x2, Pallas kernels: 4.58 us -> 3.07 us  [update(): pl.pallas_call(lambda *refs: update_kernel(max_norm, states, *refs), grid...]
  transfers between devices with their start and end apart: 16 -> 16, of which waited for: 10 -> 10; matrix products, arithmetic and copies ran while one was open for 0% -> 0% of each run, Pallas kernels for 18% -> 17%
where the time goes in v1:
time: 96.3 us; the launch traced here: 96.1 us
  waiting for transfers between devices  33.5 us (35%)
  Pallas kernels  24.8 us (26%)
  starting transfers between devices  21.9 us (23%)
  blocking collectives  12.3 us (13%)
  local copies, waits for them, and re-layouts  2.76 us (3%)
    ppermute x16, waiting for transfers between devices, send(): lax.ppermute(value, 'dp', [(r, at_offset(r, offset, flip)) for r in range...  33.5 us
    ppermute x16, starting transfers between devices, send(): lax.ppermute(value, 'dp', [(r, at_offset(r, offset, flip)) for r in range...  21.9 us
    all_to_all x1, blocking collectives, paired(): total = lax.all_to_all(squares, ('dp', 'section'), 0, 0, tiled=True)  12.3 us
    pallas_call x8, Pallas kernels, piece(): pl.pallas_call(lambda *refs: piece_kernel(place, per, [parts for _, parts...  10.9 us
    pallas_call x1, Pallas kernels, forward(): pl.pallas_call(lambda *refs: forward_kernel(places, rows, *refs), in_spec...  6.21 us
    pallas_call x2, Pallas kernels, update(): pl.pallas_call(lambda *refs: update_kernel(max_norm, states, *refs), grid...  3.07 us
    unnamed x14, local copies, waits for them, and re-layouts  2.75 us
    pallas_call x2, Pallas kernels, fill(): pl.pallas_call(lambda *refs: fill_kernel(moves, len(values), *refs), in_s...  2.35 us
  transfers between devices with their start and end apart: 16, of which 10 were waited for; matrix products, arithmetic and copies ran while one was open for 0% of the time, Pallas kernels for 17%

profile of v1, /device:TPU:0, one launch (start us, length us, event | category | flops | bytes accessed | tf_op | source)
XLA Modules:
  0.0 96.1 jit_solution(11918163250738816808)
XLA Ops:
  0.6 0.0 copy-start.3
  0.6 6.2 %forward.1 = (bf16[3,512,256]{2,1,0:T(8,128)(2,1)}, bf16[784,256]{1,0:T(8,128)(2,1)}) custom-call(bf16[512,2048]{1,0:T(8,128)(2,1)} %bitcast.20, bf16[512,2048]{1,0:T(8,128)(2,1)} %bitcast.29, bf16[6144,256]{1,0:T(8,128)(2,1)} %bitcast.42), custom_call_target="tpu_custom_call" | custom-call | flops 1024 | bytes 1024 | tf_op jit(solution)/shard_map/forward/pallas_call | solution.py:204
  6.9 3.0 %collective-permute-start.4 = (bf16[784,256]{1,0:T(8,128)(2,1)}, bf16[784,256]{1,0:T(8,128)(2,1)S(1)}, u32[]{:S(2)}, u32[]{:S(2)}) collective-permute-start(bf16[784,256]{1,0:T(8,128)(2,1)} %get-tuple-element.12), channel_id=1, source_target_pairs={{0,4},{4,0},{8,12},{12,8},{16,20},{20,16},{24,28},{28,24},{1,5},{5... | collective-permute-start | bytes 1204232 | tf_op jit(solution)/shard_map/ppermute | solution.py:493
  9.9 0.0 copy-done.3
  9.9 0.0 copy-start.4
  9.9 1.6 %copy-done.4 = bf16[1,512,2048]{2,1,0:T(8,128)(2,1)S(1)} copy-done((bf16[1,512,2048]{2,1,0:T(8,128)(2,1)S(1)}, bf16[1,512,2048]{2,1,0:T(8,128)(2,1)}, u32[]{:S(2)}) %copy-start.4) | copy-done | bytes 2097176
  11.5 0.0 copy-start.6
  11.5 1.1 %copy-done.6 = bf16[3,512,256]{2,1,0:T(8,128)(2,1)S(1)} copy-done((bf16[3,512,256]{2,1,0:T(8,128)(2,1)S(1)}, bf16[3,512,256]{2,1,0:T(8,128)(2,1)}, u32[]{:S(2)}) %copy-start.6) | copy-done | bytes 786456
  12.6 1.1 %piece.8.refs_3_ = bf16[528,256]{1,0:T(8,128)(2,1)S(1)} custom-call(bf16[512,2048]{1,0:T(8,128)(2,1)S(1)} %bitcast.21, bf16[512,2048]{1,0:T(8,128)(2,1)S(1)} %bitcast.30, bf16[3,512,256]{2,1,0:T(8,128)(2,1)S(1)} %copy-done.6), custom_call_target="tpu_custom_call" | custom-call | flops 2006000000 | bytes 1024 | tf_op jit(solution)/shard_map/piece/pallas_call | solution.py:313
  13.7 1.6 %collective-permute-start.2 = (bf16[528,256]{1,0:T(8,128)(2,1)S(1)}, bf16[528,256]{1,0:T(8,128)(2,1)S(1)}, u32[]{:S(2)}, u32[]{:S(2)}) collective-permute-start(bf16[528,256]{1,0:T(8,128)(2,1)S(1)} %piece.8.refs_3_), channel_id=1, source_target_pairs={{0,8},{4,12},{8,24},{12,28},{16,0},{20,4},{24,16},{28,20},{1,9},{5... | collective-permute-start | bytes 811016 | tf_op jit(solution)/shard_map/ppermute | solution.py:493
  15.3 1.1 %piece.9.refs_3_ = bf16[528,256]{1,0:T(8,128)(2,1)S(1)} custom-call(bf16[512,2048]{1,0:T(8,128)(2,1)S(1)} %bitcast.22, bf16[512,2048]{1,0:T(8,128)(2,1)S(1)} %bitcast.31, bf16[3,512,256]{2,1,0:T(8,128)(2,1)S(1)} %copy-done.6, bf16[528,256]{1,0:T(8,128)(2,1)S(1)} %piece.8.refs_3_), custom_call_target="tpu_custom_call" | custom-call | flops 2006000000 | bytes 1024 | tf_op jit(solution)/shard_map/piece/pallas_call | solution.py:313
  16.3 0.6 collective-permute-start
  17.0 1.3 %piece.12.refs_3_.refs_0_ = f32[768,256]{1,0:T(8,128)S(1)} custom-call(bf16[512,2048]{1,0:T(8,128)(2,1)S(1)} %bitcast.23, bf16[512,2048]{1,0:T(8,128)(2,1)S(1)} %bitcast.32, bf16[3,512,256]{2,1,0:T(8,128)(2,1)S(1)} %copy-done.6, bf16[528,256]{1,0:T(8,128)(2,1)S(1)} %piece.9.refs_3_), custom_call_target="tpu_custom_call" | custom-call | flops 2006000000 | bytes 1024 | tf_op jit(solution)/shard_map/piece/pallas_call | solution.py:313
  18.3 0.0 copy-start.5
  18.3 1.9 %collective-permute-done.4.refs_1_ = bf16[784,256]{1,0:T(8,128)(2,1)S(1)} collective-permute-done((bf16[784,256]{1,0:T(8,128)(2,1)}, bf16[784,256]{1,0:T(8,128)(2,1)S(1)}, u32[]{:S(2)}, u32[]{:S(2)}) %collective-permute-start.4) | collective-permute-done | bytes 401440 | tf_op jit(solution)/shard_map/ppermute | solution.py:493
  20.2 0.7 join.2
  20.9 3.2 %collective-permute-start.5 = (bf16[784,256]{1,0:T(8,128)(2,1)S(1)}, bf16[784,256]{1,0:T(8,128)(2,1)S(1)}, u32[]{:S(2)}, u32[]{:S(2)}) collective-permute-start(bf16[784,256]{1,0:T(8,128)(2,1)S(1)} %join.2), channel_id=1, source_target_pairs={{0,16},{4,20},{8,0},{12,4},{16,24},{20,28},{24,8},{28,12},{1,17},{... | collective-permute-start | bytes 1204232 | tf_op jit(solution)/shard_map/ppermute | solution.py:493
  24.1 0.0 copy-done.5
  24.1 1.6 %piece.13.refs_5_ = bf16[784,256]{1,0:T(8,128)(2,1)S(1)} custom-call(bf16[512,2048]{1,0:T(8,128)(2,1)S(1)} %bitcast.24, bf16[512,2048]{1,0:T(8,128)(2,1)S(1)} %bitcast.33, bf16[3,512,256]{2,1,0:T(8,128)(2,1)S(1)} %copy-done.6, f32[768,256]{1,0:T(8,128)S(1)} %piece.12.refs_3_.refs_0_), custom_call_target="tpu_custom_call" | custom-call | flops 2006000000 | bytes 1024 | tf_op jit(solution)/shard_map/piece/pallas_call | solution.py:313
  25.7 1.6 %collective-permute-start.6 = (bf16[784,256]{1,0:T(8,128)(2,1)S(1)}, bf16[784,256]{1,0:T(8,128)(2,1)S(1)}, u32[]{:S(2)}, u32[]{:S(2)}) collective-permute-start(bf16[784,256]{1,0:T(8,128)(2,1)S(1)} %piece.13.refs_5_), channel_id=1, source_target_pairs={{0,4},{4,0},{8,12},{12,8},{16,20},{20,16},{24,28},{28,24},{1,5},{5... | collective-permute-start | bytes 1204232 | tf_op jit(solution)/shard_map/ppermute | solution.py:493
  27.2 0.0 collective-permute-done.refs_3_.refs_4_
  27.2 1.1 %piece.10 = bf16[528,256]{1,0:T(8,128)(2,1)S(1)} custom-call(bf16[512,2048]{1,0:T(8,128)(2,1)S(1)} %bitcast.25, bf16[512,2048]{1,0:T(8,128)(2,1)S(1)} %bitcast.34, bf16[3,512,256]{2,1,0:T(8,128)(2,1)S(1)} %copy-done.6, bf16[528,256]{1,0:T(8,128)(2,1)S(1)} %collective-permute-done.refs_3_.refs_4_, bf16[528,256]{1,0:T(8,128)(2,1)S(1)} %collective-permute-done.refs_3_.refs_4_), custom_call_target="tpu_custom_call" | custom-call | flops 2006000000 | bytes 1024 | tf_op jit(solution)/shard_map/piece/pallas_call | solution.py:313
  28.4 1.0 %collective-permute-start.1 = (bf16[528,256]{1,0:T(8,128)(2,1)S(1)}, bf16[528,256]{1,0:T(8,128)(2,1)S(1)}, u32[]{:S(2)}, u32[]{:S(2)}) collective-permute-start(bf16[528,256]{1,0:T(8,128)(2,1)S(1)} %piece.10), channel_id=1, source_target_pairs={{0,8},{4,12},{8,24},{12,28},{16,0},{20,4},{24,16},{28,20},{1,9},{5... | collective-permute-start | bytes 811016 | tf_op jit(solution)/shard_map/ppermute | solution.py:493
  29.4 0.0 collective-permute-done.2.refs_5_.refs_6_.refs_3_.refs_4_
  29.4 1.7 %piece.14 = bf16[784,256]{1,0:T(8,128)(2,1)S(1)} custom-call(bf16[512,2048]{1,0:T(8,128)(2,1)S(1)} %bitcast.26, bf16[512,2048]{1,0:T(8,128)(2,1)S(1)} %bitcast.35, bf16[3,512,256]{2,1,0:T(8,128)(2,1)S(1)} %copy-done.6, bf16[528,256]{1,0:T(8,128)(2,1)S(1)} %collective-permute-done.2.refs_5_.refs_6_.refs_3_.refs_4_, ...), custom_call_target="tpu_custom_call" | custom-call | flops 2006000000 | bytes 1024 | tf_op jit(solution)/shard_map/piece/pallas_call | solution.py:313
  31.1 1.5 %collective-permute-start.3 = (bf16[784,256]{1,0:T(8,128)(2,1)S(1)}, bf16[784,256]{1,0:T(8,128)(2,1)S(1)}, u32[]{:S(2)}, u32[]{:S(2)}) collective-permute-start(bf16[784,256]{1,0:T(8,128)(2,1)S(1)} %piece.14), channel_id=1, source_target_pairs={{0,4},{4,0},{8,12},{12,8},{16,20},{20,16},{24,28},{28,24},{1,5},{5... | collective-permute-start | bytes 1204232 | tf_op jit(solution)/shard_map/ppermute | solution.py:493
  32.5 1.0 %collective-permute-done.5.refs_3_.refs_4_ = bf16[784,256]{1,0:T(8,128)(2,1)S(1)} collective-permute-done((bf16[784,256]{1,0:T(8,128)(2,1)S(1)}, bf16[784,256]{1,0:T(8,128)(2,1)S(1)}, u32[]{:S(2)}, u32[]{:S(2)}) %collective-permute-start.5) | collective-permute-done | bytes 401440 | tf_op jit(solution)/shard_map/ppermute | solution.py:493
  33.5 1.4 %piece.15.refs_0_ = f32[768,256]{1,0:T(8,128)S(1)} custom-call(bf16[512,2048]{1,0:T(8,128)(2,1)S(1)} %bitcast.27, bf16[512,2048]{1,0:T(8,128)(2,1)S(1)} %bitcast.36, bf16[3,512,256]{2,1,0:T(8,128)(2,1)S(1)} %copy-done.6, bf16[784,256]{1,0:T(8,128)(2,1)S(1)} %collective-permute-done.5.refs_3_.refs_4_, bf16[784,256]{1,0:T(8,128)(2,1)S(1)} %collective-permute-done.5.refs_3_.refs_4_), custom_call_target="tpu_custom_call" | custom-call | flops 2006000000 | bytes 1024 | tf_op jit(solution)/shard_map/piece/pallas_call | solution.py:313
  34.9 3.1 %collective-permute-done.6.refs_1_ = bf16[784,256]{1,0:T(8,128)(2,1)S(1)} collective-permute-done((bf16[784,256]{1,0:T(8,128)(2,1)S(1)}, bf16[784,256]{1,0:T(8,128)(2,1)S(1)}, u32[]{:S(2)}, u32[]{:S(2)}) %collective-permute-start.6) | collective-permute-done | bytes 401440 | tf_op jit(solution)/shard_map/ppermute | solution.py:493
  38.0 0.7 join.3
  38.6 1.6 %collective-permute-start.7 = (bf16[784,256]{1,0:T(8,128)(2,1)S(1)}, bf16[784,256]{1,0:T(8,128)(2,1)S(1)}, u32[]{:S(2)}, u32[]{:S(2)}) collective-permute-start(bf16[784,256]{1,0:T(8,128)(2,1)S(1)} %join.3), channel_id=1, source_target_pairs={{0,16},{4,20},{8,0},{12,4},{16,24},{20,28},{24,8},{28,12},{1,17},{... | collective-permute-start | bytes 1204232 | tf_op jit(solution)/shard_map/ppermute | solution.py:493
  40.3 0.0 collective-permute-done.1.refs_3_.refs_4_
  40.3 1.8 %piece.11.refs_0_ = f32[768,256]{1,0:T(8,128)S(1)} custom-call(bf16[512,2048]{1,0:T(8,128)(2,1)S(1)} %bitcast.28, bf16[512,2048]{1,0:T(8,128)(2,1)S(1)} %bitcast.37, bf16[3,512,256]{2,1,0:T(8,128)(2,1)S(1)} %copy-done.6, bf16[528,256]{1,0:T(8,128)(2,1)S(1)} %collective-permute-done.1.refs_3_.refs_4_, ...), custom_call_target="tpu_custom_call" | custom-call | flops 2006000000 | bytes 1024 | tf_op jit(solution)/shard_map/piece/pallas_call | solution.py:313
  42.1 0.0 copy-start
  42.1 0.0 copy-start.1
  42.1 0.0 copy-start.2
  42.1 1.0 collective-permute-done.3.refs_1_
  43.1 3.7 %collective-permute-done.7.refs_2_ = bf16[784,256]{1,0:T(8,128)(2,1)S(1)} collective-permute-done((bf16[784,256]{1,0:T(8,128)(2,1)S(1)}, bf16[784,256]{1,0:T(8,128)(2,1)S(1)}, u32[]{:S(2)}, u32[]{:S(2)}) %collective-permute-start.7) | collective-permute-done | bytes 401440 | tf_op jit(solution)/shard_map/ppermute | solution.py:493
  46.8 0.8 finish.1
  47.6 12.3 %all_to_all.11 = f32[32,1,128]{2,1,0:T(1,128)S(1)} all-to-all(f32[32,1,128]{2,1,0:T(1,128)S(1)} %bitcast.40), channel_id=1, replica_groups=mesh['dp'=8,'section'=4] {'dp','section'}, dimensions={0} | all-to-all | bytes 32768 | tf_op jit(solution)/shard_map/all_to_all | solution.py:529
  60.0 0.0 copy-done
  60.0 0.0 copy-done.1
  60.0 0.0 copy-done.2
  60.0 0.8 update.1.own_ref.refs_0_
  60.8 0.6 collective-permute-start.9
  61.4 0.6 collective-permute-start.8
  62.0 1.5 %collective-permute-start.13 = (bf16[320,256]{1,0:T(8,128)(2,1)S(1)}, bf16[320,256]{1,0:T(8,128)(2,1)S(1)}, u32[]{:S(2)}, u32[]{:S(2)}) collective-permute-start(bf16[320,256]{1,0:T(8,128)(2,1)S(1)} %slice.4), channel_id=1, source_target_pairs={{0,8},{4,12},{8,24},{12,28},{16,0},{20,4},{24,16},{28,20},{1,9},{5... | collective-permute-start | bytes 491528 | tf_op jit(solution)/shard_map/ppermute | solution.py:493
  63.5 8.8 %collective-permute-done.9.refs_0_ = bf16[768,256]{1,0:T(8,128)(2,1)S(1)} collective-permute-done((bf16[768,256]{1,0:T(8,128)(2,1)S(1)}, bf16[768,256]{1,0:T(8,128)(2,1)S(1)}, u32[]{:S(2)}, u32[]{:S(2)}) %collective-permute-start.9) | collective-permute-done | bytes 393248 | tf_op jit(solution)/shard_map/ppermute | solution.py:493
  72.3 0.0 collective-permute-done.8.refs_1_.other_ref
  72.3 0.3 collective-permute-start.10
  72.5 2.4 %collective-permute-start.12 = (bf16[768,256]{1,0:T(8,128)(2,1)S(1)}, bf16[768,256]{1,0:T(8,128)(2,1)S(1)}, u32[]{:S(2)}, u32[]{:S(2)}) collective-permute-start(bf16[768,256]{1,0:T(8,128)(2,1)S(1)} %behind.4.refs_1_.refs_2_), channel_id=1, source_target_pairs={{0,16},{4,20},{8,0},{12,4},{16,24},{20,28},{24,8},{28,12},{1,17},{... | collective-permute-start | bytes 1179656 | tf_op jit(solution)/shard_map/ppermute | solution.py:493
  74.9 1.8 %collective-permute-done.13.refs_0_ = bf16[320,256]{1,0:T(8,128)(2,1)S(1)} collective-permute-done((bf16[320,256]{1,0:T(8,128)(2,1)S(1)}, bf16[320,256]{1,0:T(8,128)(2,1)S(1)}, u32[]{:S(2)}, u32[]{:S(2)}) %collective-permute-start.13) | collective-permute-done | bytes 163872 | tf_op jit(solution)/shard_map/ppermute | solution.py:493
  76.7 0.1 collective-permute-start.14
  76.8 6.8 %collective-permute-done.10.after_ref.refs_1_.refs_4_ = bf16[768,256]{1,0:T(8,128)(2,1)S(1)} collective-permute-done((bf16[768,256]{1,0:T(8,128)(2,1)S(1)}, bf16[768,256]{1,0:T(8,128)(2,1)S(1)}, u32[]{:S(2)}, u32[]{:S(2)}) %collective-permute-start.10) | collective-permute-done | bytes 393248 | tf_op jit(solution)/shard_map/ppermute | solution.py:493
  83.6 0.1 both.1
  83.7 1.4 %collective-permute-start.11 = (bf16[896,256]{1,0:T(8,128)(2,1)S(1)}, bf16[896,256]{1,0:T(8,128)(2,1)S(1)}, u32[]{:S(2)}, u32[]{:S(2)}) collective-permute-start(bf16[896,256]{1,0:T(8,128)(2,1)S(1)} %both.1), channel_id=1, source_target_pairs={{0,8},{4,12},{8,24},{12,28},{16,0},{20,4},{24,16},{28,20},{1,9},{5... | collective-permute-start | bytes 1376264 | tf_op jit(solution)/shard_map/ppermute | solution.py:493
  85.1 0.4 collective-permute-done.12.refs_0_
  85.5 0.0 collective-permute-done.14.refs_1_.refs_5_
  85.5 0.9 collective-permute-start.15
  86.5 2.3 %states.1 = (f32[768,256]{1,0:T(8,128)}, f32[768,256]{1,0:T(8,128)}, f32[768,256]{1,0:T(8,128)}) custom-call(f32[32,128]{1,0:T(8,128)S(1)} %bitcast.39, f32[768,256]{1,0:T(8,128)S(1)} %get-tuple-element.14.refs_1_, f32[768,256]{1,0:T(8,128)S(1)} %bitcast.15, f32[768,256]{1,0:T(8,128)S(1)} %bitcast.17, f32[768,256]{1,0:T(8,128)S(1)} %bitcast.19), custom_call_target="tpu_custom_call" | custom-call | flops 1024 | bytes 1024 | tf_op jit(solution)/shard_map/states/pallas_call | solution.py:404
  88.7 1.4 %fill.2.refs_2_ = bf16[6144,256]{1,0:T(8,128)(2,1)} custom-call(bf16[768,256]{1,0:T(8,128)(2,1)S(1)} %update.1.own_ref.refs_0_, bf16[768,256]{1,0:T(8,128)(2,1)S(1)} %collective-permute-done.8.refs_1_.other_ref, bf16[768,256]{1,0:T(8,128)(2,1)S(1)} %behind.4.refs_1_.refs_2_, bf16[320,256]{1,0:T(8,128)(2,1)S(1)} %behind.6.refs_3_, ...), custom_call_target="tpu_custom_call" | custom-call | flops 1024 | bytes 1024 | tf_op jit(solution)/shard_map/fill/pallas_call | solution.py:466
  90.2 5.0 %collective-permute-done.15.refs_1_ = bf16[768,256]{1,0:T(8,128)(2,1)S(1)} collective-permute-done((bf16[768,256]{1,0:T(8,128)(2,1)S(1)}, bf16[768,256]{1,0:T(8,128)(2,1)S(1)}, u32[]{:S(2)}, u32[]{:S(2)}) %collective-permute-start.15) | collective-permute-done | bytes 393248 | tf_op jit(solution)/shard_map/ppermute | solution.py:493
  95.1 0.0 collective-permute-done.11.refs_0_
  95.1 0.9 fill.3
  (5 shorter events, 0.0 us)
Async XLA Ops:
  0.6 9.2 %copy-start.3 = (bf16[1,512,2048]{2,1,0:T(8,128)(2,1)S(1)}, bf16[1,512,2048]{2,1,0:T(8,128)(2,1)}, u32[]{:S(2)}) copy-start(bf16[1,512,2048]{2,1,0:T(8,128)(2,1)} %param.7) | copy-start | bytes 6291460
  6.9 13.3 %collective-permute-start.4 = (bf16[784,256]{1,0:T(8,128)(2,1)}, bf16[784,256]{1,0:T(8,128)(2,1)S(1)}, u32[]{:S(2)}, u32[]{:S(2)}) collective-permute-start(bf16[784,256]{1,0:T(8,128)(2,1)} %get-tuple-element.12), channel_id=1, source_target_pairs={{0,4},{4,0},{8,12},{12,8},{16,20},{20,16},{24,28},{28,24},{1,5},{5... | collective-permute-start | bytes 1204232 | tf_op jit(solution)/shard_map/ppermute | solution.py:493
  9.9 1.6 %copy-start.4 = (bf16[1,512,2048]{2,1,0:T(8,128)(2,1)S(1)}, bf16[1,512,2048]{2,1,0:T(8,128)(2,1)}, u32[]{:S(2)}) copy-start(bf16[1,512,2048]{2,1,0:T(8,128)(2,1)} %param.8) | copy-start | bytes 6291460
  11.5 1.1 %copy-start.6 = (bf16[3,512,256]{2,1,0:T(8,128)(2,1)S(1)}, bf16[3,512,256]{2,1,0:T(8,128)(2,1)}, u32[]{:S(2)}) copy-start(bf16[3,512,256]{2,1,0:T(8,128)(2,1)} %get-tuple-element.11.refs_2_) | copy-start | bytes 2359300
  13.7 15.7 %collective-permute-start.2 = (bf16[528,256]{1,0:T(8,128)(2,1)S(1)}, bf16[528,256]{1,0:T(8,128)(2,1)S(1)}, u32[]{:S(2)}, u32[]{:S(2)}) collective-permute-start(bf16[528,256]{1,0:T(8,128)(2,1)S(1)} %piece.8.refs_3_), channel_id=1, source_target_pairs={{0,8},{4,12},{8,24},{12,28},{16,0},{20,4},{24,16},{28,20},{1,9},{5... | collective-permute-start | bytes 811016 | tf_op jit(solution)/shard_map/ppermute | solution.py:493
  16.3 10.9 %collective-permute-start = (bf16[528,256]{1,0:T(8,128)(2,1)S(1)}, bf16[528,256]{1,0:T(8,128)(2,1)S(1)}, u32[]{:S(2)}, u32[]{:S(2)}) collective-permute-start(bf16[528,256]{1,0:T(8,128)(2,1)S(1)} %piece.9.refs_3_), channel_id=1, source_target_pairs={{0,4},{4,0},{8,12},{12,8},{16,20},{20,16},{24,28},{28,24},{1,5},{5... | collective-permute-start | bytes 811016 | tf_op jit(solution)/shard_map/ppermute | solution.py:493
  18.3 5.8 %copy-start.5 = (bf16[1,512,2048]{2,1,0:T(8,128)(2,1)S(1)}, bf16[1,512,2048]{2,1,0:T(8,128)(2,1)}, u32[]{:S(2)}) copy-start(bf16[1,512,2048]{2,1,0:T(8,128)(2,1)} %param.8) | copy-start | bytes 6291460
  20.9 12.6 %collective-permute-start.5 = (bf16[784,256]{1,0:T(8,128)(2,1)S(1)}, bf16[784,256]{1,0:T(8,128)(2,1)S(1)}, u32[]{:S(2)}, u32[]{:S(2)}) collective-permute-start(bf16[784,256]{1,0:T(8,128)(2,1)S(1)} %join.2), channel_id=1, source_target_pairs={{0,16},{4,20},{8,0},{12,4},{16,24},{20,28},{24,8},{28,12},{1,17},{... | collective-permute-start | bytes 1204232 | tf_op jit(solution)/shard_map/ppermute | solution.py:493
  25.7 12.3 %collective-permute-start.6 = (bf16[784,256]{1,0:T(8,128)(2,1)S(1)}, bf16[784,256]{1,0:T(8,128)(2,1)S(1)}, u32[]{:S(2)}, u32[]{:S(2)}) collective-permute-start(bf16[784,256]{1,0:T(8,128)(2,1)S(1)} %piece.13.refs_5_), channel_id=1, source_target_pairs={{0,4},{4,0},{8,12},{12,8},{16,20},{20,16},{24,28},{28,24},{1,5},{5... | collective-permute-start | bytes 1204232 | tf_op jit(solution)/shard_map/ppermute | solution.py:493
  28.4 11.9 %collective-permute-start.1 = (bf16[528,256]{1,0:T(8,128)(2,1)S(1)}, bf16[528,256]{1,0:T(8,128)(2,1)S(1)}, u32[]{:S(2)}, u32[]{:S(2)}) collective-permute-start(bf16[528,256]{1,0:T(8,128)(2,1)S(1)} %piece.10), channel_id=1, source_target_pairs={{0,8},{4,12},{8,24},{12,28},{16,0},{20,4},{24,16},{28,20},{1,9},{5... | collective-permute-start | bytes 811016 | tf_op jit(solution)/shard_map/ppermute | solution.py:493
  31.1 12.0 %collective-permute-start.3 = (bf16[784,256]{1,0:T(8,128)(2,1)S(1)}, bf16[784,256]{1,0:T(8,128)(2,1)S(1)}, u32[]{:S(2)}, u32[]{:S(2)}) collective-permute-start(bf16[784,256]{1,0:T(8,128)(2,1)S(1)} %piece.14), channel_id=1, source_target_pairs={{0,4},{4,0},{8,12},{12,8},{16,20},{20,16},{24,28},{28,24},{1,5},{5... | collective-permute-start | bytes 1204232 | tf_op jit(solution)/shard_map/ppermute | solution.py:493
  38.6 8.2 %collective-permute-start.7 = (bf16[784,256]{1,0:T(8,128)(2,1)S(1)}, bf16[784,256]{1,0:T(8,128)(2,1)S(1)}, u32[]{:S(2)}, u32[]{:S(2)}) collective-permute-start(bf16[784,256]{1,0:T(8,128)(2,1)S(1)} %join.3), channel_id=1, source_target_pairs={{0,16},{4,20},{8,0},{12,4},{16,24},{20,28},{24,8},{28,12},{1,17},{... | collective-permute-start | bytes 1204232 | tf_op jit(solution)/shard_map/ppermute | solution.py:493
  42.1 17.9 %copy-start = (f32[1,768,256]{2,1,0:T(8,128)S(1)}, f32[1,768,256]{2,1,0:T(8,128)}, u32[]{:S(2)}) copy-start(f32[1,768,256]{2,1,0:T(8,128)} %param.9) | copy-start | bytes 2359300
  42.1 17.9 %copy-start.1 = (f32[1,768,256]{2,1,0:T(8,128)S(1)}, f32[1,768,256]{2,1,0:T(8,128)}, u32[]{:S(2)}) copy-start(f32[1,768,256]{2,1,0:T(8,128)} %param.10) | copy-start | bytes 2359300
  42.1 17.9 %copy-start.2 = (f32[1,768,256]{2,1,0:T(8,128)S(1)}, f32[1,768,256]{2,1,0:T(8,128)}, u32[]{:S(2)}) copy-start(f32[1,768,256]{2,1,0:T(8,128)} %param.11) | copy-start | bytes 2359300
  60.8 11.5 %collective-permute-start.9 = (bf16[768,256]{1,0:T(8,128)(2,1)S(1)}, bf16[768,256]{1,0:T(8,128)(2,1)S(1)}, u32[]{:S(2)}, u32[]{:S(2)}) collective-permute-start(bf16[768,256]{1,0:T(8,128)(2,1)S(1)} %update.1.own_ref.refs_0_), channel_id=1, source_target_pairs={{0,16},{4,20},{8,0},{12,4},{16,24},{20,28},{24,8},{28,12},{1,17},{... | collective-permute-start | bytes 1179656 | tf_op jit(solution)/shard_map/ppermute | solution.py:493
  61.4 10.8 %collective-permute-start.8 = (bf16[768,256]{1,0:T(8,128)(2,1)S(1)}, bf16[768,256]{1,0:T(8,128)(2,1)S(1)}, u32[]{:S(2)}, u32[]{:S(2)}) collective-permute-start(bf16[768,256]{1,0:T(8,128)(2,1)S(1)} %update.1.own_ref.refs_0_), channel_id=1, source_target_pairs={{0,4},{4,0},{8,12},{12,8},{16,20},{20,16},{24,28},{28,24},{1,5},{5... | collective-permute-start | bytes 1179656 | tf_op jit(solution)/shard_map/ppermute | solution.py:493
  62.0 14.7 %collective-permute-start.13 = (bf16[320,256]{1,0:T(8,128)(2,1)S(1)}, bf16[320,256]{1,0:T(8,128)(2,1)S(1)}, u32[]{:S(2)}, u32[]{:S(2)}) collective-permute-start(bf16[320,256]{1,0:T(8,128)(2,1)S(1)} %slice.4), channel_id=1, source_target_pairs={{0,8},{4,12},{8,24},{12,28},{16,0},{20,4},{24,16},{28,20},{1,9},{5... | collective-permute-start | bytes 491528 | tf_op jit(solution)/shard_map/ppermute | solution.py:493
  72.3 11.4 %collective-permute-start.10 = (bf16[768,256]{1,0:T(8,128)(2,1)S(1)}, bf16[768,256]{1,0:T(8,128)(2,1)S(1)}, u32[]{:S(2)}, u32[]{:S(2)}) collective-permute-start(bf16[768,256]{1,0:T(8,128)(2,1)S(1)} %behind.4.refs_1_.refs_2_), channel_id=1, source_target_pairs={{0,4},{4,0},{8,12},{12,8},{16,20},{20,16},{24,28},{28,24},{1,5},{5... | collective-permute-start | bytes 1179656 | tf_op jit(solution)/shard_map/ppermute | solution.py:493
  72.5 13.0 %collective-permute-start.12 = (bf16[768,256]{1,0:T(8,128)(2,1)S(1)}, bf16[768,256]{1,0:T(8,128)(2,1)S(1)}, u32[]{:S(2)}, u32[]{:S(2)}) collective-permute-start(bf16[768,256]{1,0:T(8,128)(2,1)S(1)} %behind.4.refs_1_.refs_2_), channel_id=1, source_target_pairs={{0,16},{4,20},{8,0},{12,4},{16,24},{20,28},{24,8},{28,12},{1,17},{... | collective-permute-start | bytes 1179656 | tf_op jit(solution)/shard_map/ppermute | solution.py:493
  76.7 8.8 %collective-permute-start.14 = (bf16[320,256]{1,0:T(8,128)(2,1)S(1)}, bf16[320,256]{1,0:T(8,128)(2,1)S(1)}, u32[]{:S(2)}, u32[]{:S(2)}) collective-permute-start(bf16[320,256]{1,0:T(8,128)(2,1)S(1)} %behind.6.refs_3_), channel_id=1, source_target_pairs={{0,4},{4,0},{8,12},{12,8},{16,20},{20,16},{24,28},{28,24},{1,5},{5... | collective-permute-start | bytes 491528 | tf_op jit(solution)/shard_map/ppermute | solution.py:493
  83.7 11.4 %collective-permute-start.11 = (bf16[896,256]{1,0:T(8,128)(2,1)S(1)}, bf16[896,256]{1,0:T(8,128)(2,1)S(1)}, u32[]{:S(2)}, u32[]{:S(2)}) collective-permute-start(bf16[896,256]{1,0:T(8,128)(2,1)S(1)} %both.1), channel_id=1, source_target_pairs={{0,8},{4,12},{8,24},{12,28},{16,0},{20,4},{24,16},{28,20},{1,9},{5... | collective-permute-start | bytes 1376264 | tf_op jit(solution)/shard_map/ppermute | solution.py:493
  85.5 9.6 %collective-permute-start.15 = (bf16[768,256]{1,0:T(8,128)(2,1)S(1)}, bf16[768,256]{1,0:T(8,128)(2,1)S(1)}, u32[]{:S(2)}, u32[]{:S(2)}) collective-permute-start(bf16[768,256]{1,0:T(8,128)(2,1)S(1)} %behind.7.refs_6_), channel_id=1, source_target_pairs={{0,4},{4,0},{8,12},{12,8},{16,20},{20,16},{24,28},{28,24},{1,5},{5... | collective-permute-start | bytes 1179656 | tf_op jit(solution)/shard_map/ppermute | solution.py:493

commit v2 on v1

--- a/solution.py
+++ b/solution.py
@@ -10,7 +10,7 @@
 MROWS = 256
 STEP = 10
 LITTLE = 16 << 20
-CHUNK = 32
+CHUNK = 64
 PAD = 16
 POWER = 8
 TOP = 32768.0

time: 96.3 us -> 96.3 us (level)
  no operation moved by 1% of the time
where the time goes in v2:
time: 96.3 us; the launch traced here: 96.1 us
  waiting for transfers between devices  33.5 us (35%)
  Pallas kernels  24.9 us (26%)
  starting transfers between devices  21.9 us (23%)
  blocking collectives  12.3 us (13%)
  local copies, waits for them, and re-layouts  2.76 us (3%)
    ppermute x16, waiting for transfers between devices, send(): lax.ppermute(value, 'dp', [(r, at_offset(r, offset, flip)) for r in range...  33.5 us
    ppermute x16, starting transfers between devices, send(): lax.ppermute(value, 'dp', [(r, at_offset(r, offset, flip)) for r in range...  21.9 us
    all_to_all x1, blocking collectives, paired(): total = lax.all_to_all(squares, ('dp', 'section'), 0, 0, tiled=True)  12.3 us
    pallas_call x8, Pallas kernels, piece(): pl.pallas_call(lambda *refs: piece_kernel(place, per, [parts for _, parts...  10.9 us
    pallas_call x1, Pallas kernels, forward(): pl.pallas_call(lambda *refs: forward_kernel(places, rows, *refs), in_spec...  6.2 us
    pallas_call x2, Pallas kernels, update(): pl.pallas_call(lambda *refs: update_kernel(max_norm, states, *refs), grid...  3.15 us
    unnamed x14, local copies, waits for them, and re-layouts  2.75 us
    pallas_call x2, Pallas kernels, fill(): pl.pallas_call(lambda *refs: fill_kernel(moves, len(values), *refs), in_s...  2.35 us
  transfers between devices with their start and end apart: 16, of which 10 were waited for; matrix products, arithmetic and copies ran while one was open for 0% of the time, Pallas kernels for 17%

profile of v2, /device:TPU:0, one launch (start us, length us, event | category | flops | bytes accessed | tf_op | source)
XLA Modules:
  0.0 96.1 jit_solution(7288546023333277955)
XLA Ops:
  0.6 0.0 copy-start.3
  0.6 6.2 %forward.1 = (bf16[3,512,256]{2,1,0:T(8,128)(2,1)}, bf16[784,256]{1,0:T(8,128)(2,1)}) custom-call(bf16[512,2048]{1,0:T(8,128)(2,1)} %bitcast.20, bf16[512,2048]{1,0:T(8,128)(2,1)} %bitcast.29, bf16[6144,256]{1,0:T(8,128)(2,1)} %bitcast.42), custom_call_target="tpu_custom_call" | custom-call | flops 1024 | bytes 1024 | tf_op jit(solution)/shard_map/forward/pallas_call | solution.py:204
  6.9 3.0 %collective-permute-start.4 = (bf16[784,256]{1,0:T(8,128)(2,1)}, bf16[784,256]{1,0:T(8,128)(2,1)S(1)}, u32[]{:S(2)}, u32[]{:S(2)}) collective-permute-start(bf16[784,256]{1,0:T(8,128)(2,1)} %get-tuple-element.12), channel_id=1, source_target_pairs={{0,4},{4,0},{8,12},{12,8},{16,20},{20,16},{24,28},{28,24},{1,5},{5... | collective-permute-start | bytes 1204232 | tf_op jit(solution)/shard_map/ppermute | solution.py:493
  9.9 0.0 copy-done.3
  9.9 0.0 copy-start.4
  9.9 1.6 %copy-done.4 = bf16[1,512,2048]{2,1,0:T(8,128)(2,1)S(1)} copy-done((bf16[1,512,2048]{2,1,0:T(8,128)(2,1)S(1)}, bf16[1,512,2048]{2,1,0:T(8,128)(2,1)}, u32[]{:S(2)}) %copy-start.4) | copy-done | bytes 2097176
  11.5 0.0 copy-start.6
  11.5 1.1 %copy-done.6 = bf16[3,512,256]{2,1,0:T(8,128)(2,1)S(1)} copy-done((bf16[3,512,256]{2,1,0:T(8,128)(2,1)S(1)}, bf16[3,512,256]{2,1,0:T(8,128)(2,1)}, u32[]{:S(2)}) %copy-start.6) | copy-done | bytes 786456
  12.6 1.1 %piece.8.refs_3_ = bf16[528,256]{1,0:T(8,128)(2,1)S(1)} custom-call(bf16[512,2048]{1,0:T(8,128)(2,1)S(1)} %bitcast.21, bf16[512,2048]{1,0:T(8,128)(2,1)S(1)} %bitcast.30, bf16[3,512,256]{2,1,0:T(8,128)(2,1)S(1)} %copy-done.6), custom_call_target="tpu_custom_call" | custom-call | flops 2006000000 | bytes 1024 | tf_op jit(solution)/shard_map/piece/pallas_call | solution.py:313
  13.7 1.6 %collective-permute-start.2 = (bf16[528,256]{1,0:T(8,128)(2,1)S(1)}, bf16[528,256]{1,0:T(8,128)(2,1)S(1)}, u32[]{:S(2)}, u32[]{:S(2)}) collective-permute-start(bf16[528,256]{1,0:T(8,128)(2,1)S(1)} %piece.8.refs_3_), channel_id=1, source_target_pairs={{0,8},{4,12},{8,24},{12,28},{16,0},{20,4},{24,16},{28,20},{1,9},{5... | collective-permute-start | bytes 811016 | tf_op jit(solution)/shard_map/ppermute | solution.py:493
  15.3 1.1 %piece.9.refs_3_ = bf16[528,256]{1,0:T(8,128)(2,1)S(1)} custom-call(bf16[512,2048]{1,0:T(8,128)(2,1)S(1)} %bitcast.22, bf16[512,2048]{1,0:T(8,128)(2,1)S(1)} %bitcast.31, bf16[3,512,256]{2,1,0:T(8,128)(2,1)S(1)} %copy-done.6, bf16[528,256]{1,0:T(8,128)(2,1)S(1)} %piece.8.refs_3_), custom_call_target="tpu_custom_call" | custom-call | flops 2006000000 | bytes 1024 | tf_op jit(solution)/shard_map/piece/pallas_call | solution.py:313
  16.4 0.6 collective-permute-start
  17.0 1.3 %piece.12.refs_3_.refs_0_ = f32[768,256]{1,0:T(8,128)S(1)} custom-call(bf16[512,2048]{1,0:T(8,128)(2,1)S(1)} %bitcast.23, bf16[512,2048]{1,0:T(8,128)(2,1)S(1)} %bitcast.32, bf16[3,512,256]{2,1,0:T(8,128)(2,1)S(1)} %copy-done.6, bf16[528,256]{1,0:T(8,128)(2,1)S(1)} %piece.9.refs_3_), custom_call_target="tpu_custom_call" | custom-call | flops 2006000000 | bytes 1024 | tf_op jit(solution)/shard_map/piece/pallas_call | solution.py:313
  18.3 0.0 copy-start.5
  18.3 1.9 %collective-permute-done.4.refs_1_ = bf16[784,256]{1,0:T(8,128)(2,1)S(1)} collective-permute-done((bf16[784,256]{1,0:T(8,128)(2,1)}, bf16[784,256]{1,0:T(8,128)(2,1)S(1)}, u32[]{:S(2)}, u32[]{:S(2)}) %collective-permute-start.4) | collective-permute-done | bytes 401440 | tf_op jit(solution)/shard_map/ppermute | solution.py:493
  20.2 0.7 join.2
  20.9 3.2 %collective-permute-start.5 = (bf16[784,256]{1,0:T(8,128)(2,1)S(1)}, bf16[784,256]{1,0:T(8,128)(2,1)S(1)}, u32[]{:S(2)}, u32[]{:S(2)}) collective-permute-start(bf16[784,256]{1,0:T(8,128)(2,1)S(1)} %join.2), channel_id=1, source_target_pairs={{0,16},{4,20},{8,0},{12,4},{16,24},{20,28},{24,8},{28,12},{1,17},{... | collective-permute-start | bytes 1204232 | tf_op jit(solution)/shard_map/ppermute | solution.py:493
  24.1 0.0 copy-done.5
  24.1 1.6 %piece.13.refs_5_ = bf16[784,256]{1,0:T(8,128)(2,1)S(1)} custom-call(bf16[512,2048]{1,0:T(8,128)(2,1)S(1)} %bitcast.24, bf16[512,2048]{1,0:T(8,128)(2,1)S(1)} %bitcast.33, bf16[3,512,256]{2,1,0:T(8,128)(2,1)S(1)} %copy-done.6, f32[768,256]{1,0:T(8,128)S(1)} %piece.12.refs_3_.refs_0_), custom_call_target="tpu_custom_call" | custom-call | flops 2006000000 | bytes 1024 | tf_op jit(solution)/shard_map/piece/pallas_call | solution.py:313
  25.7 1.6 %collective-permute-start.6 = (bf16[784,256]{1,0:T(8,128)(2,1)S(1)}, bf16[784,256]{1,0:T(8,128)(2,1)S(1)}, u32[]{:S(2)}, u32[]{:S(2)}) collective-permute-start(bf16[784,256]{1,0:T(8,128)(2,1)S(1)} %piece.13.refs_5_), channel_id=1, source_target_pairs={{0,4},{4,0},{8,12},{12,8},{16,20},{20,16},{24,28},{28,24},{1,5},{5... | collective-permute-start | bytes 1204232 | tf_op jit(solution)/shard_map/ppermute | solution.py:493
  27.2 0.0 collective-permute-done.refs_3_.refs_4_
  27.2 1.1 %piece.10 = bf16[528,256]{1,0:T(8,128)(2,1)S(1)} custom-call(bf16[512,2048]{1,0:T(8,128)(2,1)S(1)} %bitcast.25, bf16[512,2048]{1,0:T(8,128)(2,1)S(1)} %bitcast.34, bf16[3,512,256]{2,1,0:T(8,128)(2,1)S(1)} %copy-done.6, bf16[528,256]{1,0:T(8,128)(2,1)S(1)} %collective-permute-done.refs_3_.refs_4_, bf16[528,256]{1,0:T(8,128)(2,1)S(1)} %collective-permute-done.refs_3_.refs_4_), custom_call_target="tpu_custom_call" | custom-call | flops 2006000000 | bytes 1024 | tf_op jit(solution)/shard_map/piece/pallas_call | solution.py:313
  28.4 1.0 %collective-permute-start.1 = (bf16[528,256]{1,0:T(8,128)(2,1)S(1)}, bf16[528,256]{1,0:T(8,128)(2,1)S(1)}, u32[]{:S(2)}, u32[]{:S(2)}) collective-permute-start(bf16[528,256]{1,0:T(8,128)(2,1)S(1)} %piece.10), channel_id=1, source_target_pairs={{0,8},{4,12},{8,24},{12,28},{16,0},{20,4},{24,16},{28,20},{1,9},{5... | collective-permute-start | bytes 811016 | tf_op jit(solution)/shard_map/ppermute | solution.py:493
  29.3 0.0 collective-permute-done.2.refs_5_.refs_6_.refs_3_.refs_4_
  29.3 1.6 %piece.14 = bf16[784,256]{1,0:T(8,128)(2,1)S(1)} custom-call(bf16[512,2048]{1,0:T(8,128)(2,1)S(1)} %bitcast.26, bf16[512,2048]{1,0:T(8,128)(2,1)S(1)} %bitcast.35, bf16[3,512,256]{2,1,0:T(8,128)(2,1)S(1)} %copy-done.6, bf16[528,256]{1,0:T(8,128)(2,1)S(1)} %collective-permute-done.2.refs_5_.refs_6_.refs_3_.refs_4_, ...), custom_call_target="tpu_custom_call" | custom-call | flops 2006000000 | bytes 1024 | tf_op jit(solution)/shard_map/piece/pallas_call | solution.py:313
  31.0 1.5 %collective-permute-start.3 = (bf16[784,256]{1,0:T(8,128)(2,1)S(1)}, bf16[784,256]{1,0:T(8,128)(2,1)S(1)}, u32[]{:S(2)}, u32[]{:S(2)}) collective-permute-start(bf16[784,256]{1,0:T(8,128)(2,1)S(1)} %piece.14), channel_id=1, source_target_pairs={{0,4},{4,0},{8,12},{12,8},{16,20},{20,16},{24,28},{28,24},{1,5},{5... | collective-permute-start | bytes 1204232 | tf_op jit(solution)/shard_map/ppermute | solution.py:493
  32.5 1.0 %collective-permute-done.5.refs_3_.refs_4_ = bf16[784,256]{1,0:T(8,128)(2,1)S(1)} collective-permute-done((bf16[784,256]{1,0:T(8,128)(2,1)S(1)}, bf16[784,256]{1,0:T(8,128)(2,1)S(1)}, u32[]{:S(2)}, u32[]{:S(2)}) %collective-permute-start.5) | collective-permute-done | bytes 401440 | tf_op jit(solution)/shard_map/ppermute | solution.py:493
  33.5 1.4 %piece.15.refs_0_ = f32[768,256]{1,0:T(8,128)S(1)} custom-call(bf16[512,2048]{1,0:T(8,128)(2,1)S(1)} %bitcast.27, bf16[512,2048]{1,0:T(8,128)(2,1)S(1)} %bitcast.36, bf16[3,512,256]{2,1,0:T(8,128)(2,1)S(1)} %copy-done.6, bf16[784,256]{1,0:T(8,128)(2,1)S(1)} %collective-permute-done.5.refs_3_.refs_4_, bf16[784,256]{1,0:T(8,128)(2,1)S(1)} %collective-permute-done.5.refs_3_.refs_4_), custom_call_target="tpu_custom_call" | custom-call | flops 2006000000 | bytes 1024 | tf_op jit(solution)/shard_map/piece/pallas_call | solution.py:313
  34.9 3.1 %collective-permute-done.6.refs_1_ = bf16[784,256]{1,0:T(8,128)(2,1)S(1)} collective-permute-done((bf16[784,256]{1,0:T(8,128)(2,1)S(1)}, bf16[784,256]{1,0:T(8,128)(2,1)S(1)}, u32[]{:S(2)}, u32[]{:S(2)}) %collective-permute-start.6) | collective-permute-done | bytes 401440 | tf_op jit(solution)/shard_map/ppermute | solution.py:493
  38.0 0.7 join.3
  38.6 1.6 %collective-permute-start.7 = (bf16[784,256]{1,0:T(8,128)(2,1)S(1)}, bf16[784,256]{1,0:T(8,128)(2,1)S(1)}, u32[]{:S(2)}, u32[]{:S(2)}) collective-permute-start(bf16[784,256]{1,0:T(8,128)(2,1)S(1)} %join.3), channel_id=1, source_target_pairs={{0,16},{4,20},{8,0},{12,4},{16,24},{20,28},{24,8},{28,12},{1,17},{... | collective-permute-start | bytes 1204232 | tf_op jit(solution)/shard_map/ppermute | solution.py:493
  40.3 0.0 collective-permute-done.1.refs_3_.refs_4_
  40.3 1.8 %piece.11.refs_0_ = f32[768,256]{1,0:T(8,128)S(1)} custom-call(bf16[512,2048]{1,0:T(8,128)(2,1)S(1)} %bitcast.28, bf16[512,2048]{1,0:T(8,128)(2,1)S(1)} %bitcast.37, bf16[3,512,256]{2,1,0:T(8,128)(2,1)S(1)} %copy-done.6, bf16[528,256]{1,0:T(8,128)(2,1)S(1)} %collective-permute-done.1.refs_3_.refs_4_, ...), custom_call_target="tpu_custom_call" | custom-call | flops 2006000000 | bytes 1024 | tf_op jit(solution)/shard_map/piece/pallas_call | solution.py:313
  42.1 0.0 copy-start
  42.1 0.0 copy-start.1
  42.1 0.0 copy-start.2
  42.1 1.0 %collective-permute-done.3.refs_1_ = bf16[784,256]{1,0:T(8,128)(2,1)S(1)} collective-permute-done((bf16[784,256]{1,0:T(8,128)(2,1)S(1)}, bf16[784,256]{1,0:T(8,128)(2,1)S(1)}, u32[]{:S(2)}, u32[]{:S(2)}) %collective-permute-start.3) | collective-permute-done | bytes 401440 | tf_op jit(solution)/shard_map/ppermute | solution.py:493
  43.1 3.7 %collective-permute-done.7.refs_2_ = bf16[784,256]{1,0:T(8,128)(2,1)S(1)} collective-permute-done((bf16[784,256]{1,0:T(8,128)(2,1)S(1)}, bf16[784,256]{1,0:T(8,128)(2,1)S(1)}, u32[]{:S(2)}, u32[]{:S(2)}) %collective-permute-start.7) | collective-permute-done | bytes 401440 | tf_op jit(solution)/shard_map/ppermute | solution.py:493
  46.8 0.8 finish.1
  47.6 12.3 %all_to_all.11 = f32[32,1,128]{2,1,0:T(1,128)S(1)} all-to-all(f32[32,1,128]{2,1,0:T(1,128)S(1)} %bitcast.40), channel_id=1, replica_groups=mesh['dp'=8,'section'=4] {'dp','section'}, dimensions={0} | all-to-all | bytes 32768 | tf_op jit(solution)/shard_map/all_to_all | solution.py:529
  60.0 0.0 copy-done
  60.0 0.0 copy-done.1
  60.0 0.0 copy-done.2
  60.0 0.9 update.1.own_ref.refs_0_
  60.8 0.6 collective-permute-start.9
  61.5 0.6 collective-permute-start.8
  62.1 1.5 %collective-permute-start.13 = (bf16[320,256]{1,0:T(8,128)(2,1)S(1)}, bf16[320,256]{1,0:T(8,128)(2,1)S(1)}, u32[]{:S(2)}, u32[]{:S(2)}) collective-permute-start(bf16[320,256]{1,0:T(8,128)(2,1)S(1)} %slice.4), channel_id=1, source_target_pairs={{0,8},{4,12},{8,24},{12,28},{16,0},{20,4},{24,16},{28,20},{1,9},{5... | collective-permute-start | bytes 491528 | tf_op jit(solution)/shard_map/ppermute | solution.py:493
  63.5 8.8 %collective-permute-done.9.refs_0_ = bf16[768,256]{1,0:T(8,128)(2,1)S(1)} collective-permute-done((bf16[768,256]{1,0:T(8,128)(2,1)S(1)}, bf16[768,256]{1,0:T(8,128)(2,1)S(1)}, u32[]{:S(2)}, u32[]{:S(2)}) %collective-permute-start.9) | collective-permute-done | bytes 393248 | tf_op jit(solution)/shard_map/ppermute | solution.py:493
  72.3 0.0 collective-permute-done.8.refs_1_.other_ref
  72.3 0.3 collective-permute-start.10
  72.6 2.4 %collective-permute-start.12 = (bf16[768,256]{1,0:T(8,128)(2,1)S(1)}, bf16[768,256]{1,0:T(8,128)(2,1)S(1)}, u32[]{:S(2)}, u32[]{:S(2)}) collective-permute-start(bf16[768,256]{1,0:T(8,128)(2,1)S(1)} %behind.4.refs_1_.refs_2_), channel_id=1, source_target_pairs={{0,16},{4,20},{8,0},{12,4},{16,24},{20,28},{24,8},{28,12},{1,17},{... | collective-permute-start | bytes 1179656 | tf_op jit(solution)/shard_map/ppermute | solution.py:493
  75.0 1.8 %collective-permute-done.13.refs_0_ = bf16[320,256]{1,0:T(8,128)(2,1)S(1)} collective-permute-done((bf16[320,256]{1,0:T(8,128)(2,1)S(1)}, bf16[320,256]{1,0:T(8,128)(2,1)S(1)}, u32[]{:S(2)}, u32[]{:S(2)}) %collective-permute-start.13) | collective-permute-done | bytes 163872 | tf_op jit(solution)/shard_map/ppermute | solution.py:493
  76.8 0.1 collective-permute-start.14
  76.8 6.8 %collective-permute-done.10.after_ref.refs_1_.refs_4_ = bf16[768,256]{1,0:T(8,128)(2,1)S(1)} collective-permute-done((bf16[768,256]{1,0:T(8,128)(2,1)S(1)}, bf16[768,256]{1,0:T(8,128)(2,1)S(1)}, u32[]{:S(2)}, u32[]{:S(2)}) %collective-permute-start.10) | collective-permute-done | bytes 393248 | tf_op jit(solution)/shard_map/ppermute | solution.py:493
  83.7 0.1 both.1
  83.7 1.4 %collective-permute-start.11 = (bf16[896,256]{1,0:T(8,128)(2,1)S(1)}, bf16[896,256]{1,0:T(8,128)(2,1)S(1)}, u32[]{:S(2)}, u32[]{:S(2)}) collective-permute-start(bf16[896,256]{1,0:T(8,128)(2,1)S(1)} %both.1), channel_id=1, source_target_pairs={{0,8},{4,12},{8,24},{12,28},{16,0},{20,4},{24,16},{28,20},{1,9},{5... | collective-permute-start | bytes 1376264 | tf_op jit(solution)/shard_map/ppermute | solution.py:493
  85.1 0.4 collective-permute-done.12.refs_0_
  85.6 0.0 collective-permute-done.14.refs_1_.refs_5_
  85.6 0.9 collective-permute-start.15
  86.5 2.3 %states.1 = (f32[768,256]{1,0:T(8,128)}, f32[768,256]{1,0:T(8,128)}, f32[768,256]{1,0:T(8,128)}) custom-call(f32[32,128]{1,0:T(8,128)S(1)} %bitcast.39, f32[768,256]{1,0:T(8,128)S(1)} %get-tuple-element.14.refs_1_, f32[768,256]{1,0:T(8,128)S(1)} %bitcast.15, f32[768,256]{1,0:T(8,128)S(1)} %bitcast.17, f32[768,256]{1,0:T(8,128)S(1)} %bitcast.19), custom_call_target="tpu_custom_call" | custom-call | flops 1024 | bytes 1024 | tf_op jit(solution)/shard_map/states/pallas_call | solution.py:404
  88.8 1.4 %fill.2.refs_2_ = bf16[6144,256]{1,0:T(8,128)(2,1)} custom-call(bf16[768,256]{1,0:T(8,128)(2,1)S(1)} %update.1.own_ref.refs_0_, bf16[768,256]{1,0:T(8,128)(2,1)S(1)} %collective-permute-done.8.refs_1_.other_ref, bf16[768,256]{1,0:T(8,128)(2,1)S(1)} %behind.4.refs_1_.refs_2_, bf16[320,256]{1,0:T(8,128)(2,1)S(1)} %behind.6.refs_3_, ...), custom_call_target="tpu_custom_call" | custom-call | flops 1024 | bytes 1024 | tf_op jit(solution)/shard_map/fill/pallas_call | solution.py:466
  90.2 5.0 %collective-permute-done.15.refs_1_ = bf16[768,256]{1,0:T(8,128)(2,1)S(1)} collective-permute-done((bf16[768,256]{1,0:T(8,128)(2,1)S(1)}, bf16[768,256]{1,0:T(8,128)(2,1)S(1)}, u32[]{:S(2)}, u32[]{:S(2)}) %collective-permute-start.15) | collective-permute-done | bytes 393248 | tf_op jit(solution)/shard_map/ppermute | solution.py:493
  95.2 0.0 collective-permute-done.11.refs_0_
  95.2 0.9 fill.3
  (5 shorter events, 0.0 us)
Async XLA Ops:
  0.6 9.2 %copy-start.3 = (bf16[1,512,2048]{2,1,0:T(8,128)(2,1)S(1)}, bf16[1,512,2048]{2,1,0:T(8,128)(2,1)}, u32[]{:S(2)}) copy-start(bf16[1,512,2048]{2,1,0:T(8,128)(2,1)} %param.7) | copy-start | bytes 6291460
  6.9 13.3 %collective-permute-start.4 = (bf16[784,256]{1,0:T(8,128)(2,1)}, bf16[784,256]{1,0:T(8,128)(2,1)S(1)}, u32[]{:S(2)}, u32[]{:S(2)}) collective-permute-start(bf16[784,256]{1,0:T(8,128)(2,1)} %get-tuple-element.12), channel_id=1, source_target_pairs={{0,4},{4,0},{8,12},{12,8},{16,20},{20,16},{24,28},{28,24},{1,5},{5... | collective-permute-start | bytes 1204232 | tf_op jit(solution)/shard_map/ppermute | solution.py:493
  9.9 1.6 %copy-start.4 = (bf16[1,512,2048]{2,1,0:T(8,128)(2,1)S(1)}, bf16[1,512,2048]{2,1,0:T(8,128)(2,1)}, u32[]{:S(2)}) copy-start(bf16[1,512,2048]{2,1,0:T(8,128)(2,1)} %param.8) | copy-start | bytes 6291460
  11.5 1.1 %copy-start.6 = (bf16[3,512,256]{2,1,0:T(8,128)(2,1)S(1)}, bf16[3,512,256]{2,1,0:T(8,128)(2,1)}, u32[]{:S(2)}) copy-start(bf16[3,512,256]{2,1,0:T(8,128)(2,1)} %get-tuple-element.11.refs_2_) | copy-start | bytes 2359300
  13.7 15.7 %collective-permute-start.2 = (bf16[528,256]{1,0:T(8,128)(2,1)S(1)}, bf16[528,256]{1,0:T(8,128)(2,1)S(1)}, u32[]{:S(2)}, u32[]{:S(2)}) collective-permute-start(bf16[528,256]{1,0:T(8,128)(2,1)S(1)} %piece.8.refs_3_), channel_id=1, source_target_pairs={{0,8},{4,12},{8,24},{12,28},{16,0},{20,4},{24,16},{28,20},{1,9},{5... | collective-permute-start | bytes 811016 | tf_op jit(solution)/shard_map/ppermute | solution.py:493
  16.4 10.9 %collective-permute-start = (bf16[528,256]{1,0:T(8,128)(2,1)S(1)}, bf16[528,256]{1,0:T(8,128)(2,1)S(1)}, u32[]{:S(2)}, u32[]{:S(2)}) collective-permute-start(bf16[528,256]{1,0:T(8,128)(2,1)S(1)} %piece.9.refs_3_), channel_id=1, source_target_pairs={{0,4},{4,0},{8,12},{12,8},{16,20},{20,16},{24,28},{28,24},{1,5},{5... | collective-permute-start | bytes 811016 | tf_op jit(solution)/shard_map/ppermute | solution.py:493
  18.3 5.8 %copy-start.5 = (bf16[1,512,2048]{2,1,0:T(8,128)(2,1)S(1)}, bf16[1,512,2048]{2,1,0:T(8,128)(2,1)}, u32[]{:S(2)}) copy-start(bf16[1,512,2048]{2,1,0:T(8,128)(2,1)} %param.8) | copy-start | bytes 6291460
  20.9 12.6 %collective-permute-start.5 = (bf16[784,256]{1,0:T(8,128)(2,1)S(1)}, bf16[784,256]{1,0:T(8,128)(2,1)S(1)}, u32[]{:S(2)}, u32[]{:S(2)}) collective-permute-start(bf16[784,256]{1,0:T(8,128)(2,1)S(1)} %join.2), channel_id=1, source_target_pairs={{0,16},{4,20},{8,0},{12,4},{16,24},{20,28},{24,8},{28,12},{1,17},{... | collective-permute-start | bytes 1204232 | tf_op jit(solution)/shard_map/ppermute | solution.py:493
  25.7 12.3 %collective-permute-start.6 = (bf16[784,256]{1,0:T(8,128)(2,1)S(1)}, bf16[784,256]{1,0:T(8,128)(2,1)S(1)}, u32[]{:S(2)}, u32[]{:S(2)}) collective-permute-start(bf16[784,256]{1,0:T(8,128)(2,1)S(1)} %piece.13.refs_5_), channel_id=1, source_target_pairs={{0,4},{4,0},{8,12},{12,8},{16,20},{20,16},{24,28},{28,24},{1,5},{5... | collective-permute-start | bytes 1204232 | tf_op jit(solution)/shard_map/ppermute | solution.py:493
  28.4 11.9 %collective-permute-start.1 = (bf16[528,256]{1,0:T(8,128)(2,1)S(1)}, bf16[528,256]{1,0:T(8,128)(2,1)S(1)}, u32[]{:S(2)}, u32[]{:S(2)}) collective-permute-start(bf16[528,256]{1,0:T(8,128)(2,1)S(1)} %piece.10), channel_id=1, source_target_pairs={{0,8},{4,12},{8,24},{12,28},{16,0},{20,4},{24,16},{28,20},{1,9},{5... | collective-permute-start | bytes 811016 | tf_op jit(solution)/shard_map/ppermute | solution.py:493
  31.0 12.1 %collective-permute-start.3 = (bf16[784,256]{1,0:T(8,128)(2,1)S(1)}, bf16[784,256]{1,0:T(8,128)(2,1)S(1)}, u32[]{:S(2)}, u32[]{:S(2)}) collective-permute-start(bf16[784,256]{1,0:T(8,128)(2,1)S(1)} %piece.14), channel_id=1, source_target_pairs={{0,4},{4,0},{8,12},{12,8},{16,20},{20,16},{24,28},{28,24},{1,5},{5... | collective-permute-start | bytes 1204232 | tf_op jit(solution)/shard_map/ppermute | solution.py:493
  38.6 8.2 %collective-permute-start.7 = (bf16[784,256]{1,0:T(8,128)(2,1)S(1)}, bf16[784,256]{1,0:T(8,128)(2,1)S(1)}, u32[]{:S(2)}, u32[]{:S(2)}) collective-permute-start(bf16[784,256]{1,0:T(8,128)(2,1)S(1)} %join.3), channel_id=1, source_target_pairs={{0,16},{4,20},{8,0},{12,4},{16,24},{20,28},{24,8},{28,12},{1,17},{... | collective-permute-start | bytes 1204232 | tf_op jit(solution)/shard_map/ppermute | solution.py:493
  42.1 17.9 %copy-start = (f32[1,768,256]{2,1,0:T(8,128)S(1)}, f32[1,768,256]{2,1,0:T(8,128)}, u32[]{:S(2)}) copy-start(f32[1,768,256]{2,1,0:T(8,128)} %param.9) | copy-start | bytes 2359300
  42.1 17.9 %copy-start.1 = (f32[1,768,256]{2,1,0:T(8,128)S(1)}, f32[1,768,256]{2,1,0:T(8,128)}, u32[]{:S(2)}) copy-start(f32[1,768,256]{2,1,0:T(8,128)} %param.10) | copy-start | bytes 2359300
  42.1 17.9 %copy-start.2 = (f32[1,768,256]{2,1,0:T(8,128)S(1)}, f32[1,768,256]{2,1,0:T(8,128)}, u32[]{:S(2)}) copy-start(f32[1,768,256]{2,1,0:T(8,128)} %param.11) | copy-start | bytes 2359300
  60.8 11.5 %collective-permute-start.9 = (bf16[768,256]{1,0:T(8,128)(2,1)S(1)}, bf16[768,256]{1,0:T(8,128)(2,1)S(1)}, u32[]{:S(2)}, u32[]{:S(2)}) collective-permute-start(bf16[768,256]{1,0:T(8,128)(2,1)S(1)} %update.1.own_ref.refs_0_), channel_id=1, source_target_pairs={{0,16},{4,20},{8,0},{12,4},{16,24},{20,28},{24,8},{28,12},{1,17},{... | collective-permute-start | bytes 1179656 | tf_op jit(solution)/shard_map/ppermute | solution.py:493
  61.5 10.8 %collective-permute-start.8 = (bf16[768,256]{1,0:T(8,128)(2,1)S(1)}, bf16[768,256]{1,0:T(8,128)(2,1)S(1)}, u32[]{:S(2)}, u32[]{:S(2)}) collective-permute-start(bf16[768,256]{1,0:T(8,128)(2,1)S(1)} %update.1.own_ref.refs_0_), channel_id=1, source_target_pairs={{0,4},{4,0},{8,12},{12,8},{16,20},{20,16},{24,28},{28,24},{1,5},{5... | collective-permute-start | bytes 1179656 | tf_op jit(solution)/shard_map/ppermute | solution.py:493
  62.1 14.7 %collective-permute-start.13 = (bf16[320,256]{1,0:T(8,128)(2,1)S(1)}, bf16[320,256]{1,0:T(8,128)(2,1)S(1)}, u32[]{:S(2)}, u32[]{:S(2)}) collective-permute-start(bf16[320,256]{1,0:T(8,128)(2,1)S(1)} %slice.4), channel_id=1, source_target_pairs={{0,8},{4,12},{8,24},{12,28},{16,0},{20,4},{24,16},{28,20},{1,9},{5... | collective-permute-start | bytes 491528 | tf_op jit(solution)/shard_map/ppermute | solution.py:493
  72.3 11.4 %collective-permute-start.10 = (bf16[768,256]{1,0:T(8,128)(2,1)S(1)}, bf16[768,256]{1,0:T(8,128)(2,1)S(1)}, u32[]{:S(2)}, u32[]{:S(2)}) collective-permute-start(bf16[768,256]{1,0:T(8,128)(2,1)S(1)} %behind.4.refs_1_.refs_2_), channel_id=1, source_target_pairs={{0,4},{4,0},{8,12},{12,8},{16,20},{20,16},{24,28},{28,24},{1,5},{5... | collective-permute-start | bytes 1179656 | tf_op jit(solution)/shard_map/ppermute | solution.py:493
  72.6 13.0 %collective-permute-start.12 = (bf16[768,256]{1,0:T(8,128)(2,1)S(1)}, bf16[768,256]{1,0:T(8,128)(2,1)S(1)}, u32[]{:S(2)}, u32[]{:S(2)}) collective-permute-start(bf16[768,256]{1,0:T(8,128)(2,1)S(1)} %behind.4.refs_1_.refs_2_), channel_id=1, source_target_pairs={{0,16},{4,20},{8,0},{12,4},{16,24},{20,28},{24,8},{28,12},{1,17},{... | collective-permute-start | bytes 1179656 | tf_op jit(solution)/shard_map/ppermute | solution.py:493
  76.8 8.8 %collective-permute-start.14 = (bf16[320,256]{1,0:T(8,128)(2,1)S(1)}, bf16[320,256]{1,0:T(8,128)(2,1)S(1)}, u32[]{:S(2)}, u32[]{:S(2)}) collective-permute-start(bf16[320,256]{1,0:T(8,128)(2,1)S(1)} %behind.6.refs_3_), channel_id=1, source_target_pairs={{0,4},{4,0},{8,12},{12,8},{16,20},{20,16},{24,28},{28,24},{1,5},{5... | collective-permute-start | bytes 491528 | tf_op jit(solution)/shard_map/ppermute | solution.py:493
  83.7 11.4 %collective-permute-start.11 = (bf16[896,256]{1,0:T(8,128)(2,1)S(1)}, bf16[896,256]{1,0:T(8,128)(2,1)S(1)}, u32[]{:S(2)}, u32[]{:S(2)}) collective-permute-start(bf16[896,256]{1,0:T(8,128)(2,1)S(1)} %both.1), channel_id=1, source_target_pairs={{0,8},{4,12},{8,24},{12,28},{16,0},{20,4},{24,16},{28,20},{1,9},{5... | collective-permute-start | bytes 1376264 | tf_op jit(solution)/shard_map/ppermute | solution.py:493
  85.6 9.6 %collective-permute-start.15 = (bf16[768,256]{1,0:T(8,128)(2,1)S(1)}, bf16[768,256]{1,0:T(8,128)(2,1)S(1)}, u32[]{:S(2)}, u32[]{:S(2)}) collective-permute-start(bf16[768,256]{1,0:T(8,128)(2,1)S(1)} %behind.7.refs_6_), channel_id=1, source_target_pairs={{0,4},{4,0},{8,12},{12,8},{16,20},{20,16},{24,28},{28,24},{1,5},{5... | collective-permute-start | bytes 1179656 | tf_op jit(solution)/shard_map/ppermute | solution.py:493

commit v3 on v1

--- a/solution.py
+++ b/solution.py
@@ -20,7 +20,7 @@
     return pl.CostEstimate(flops=int(micros * 1.18e9), bytes_accessed=1024, transcendentals=0)
 
 
-PIECE = cost_of(1.7)
+PIECE = cost_of(1.2)
 CHEAP = pl.CostEstimate(flops=1024, bytes_accessed=1024, transcendentals=0)
 
 
@@ -517,11 +517,12 @@
     own_far = made(at(*[(2, 0, b) for b in every]), after=message, last=True)
     message = made(at(*[(1, 1, b) for b in every]), after=own_far)
     cross_next = send(message, 0, 1)
+    own_back = made(at(*[(-1, 0, b) for b in most]), after=message, last=True)
+    by_ring = send(join(own_far, cross_far, rows), 1)
+    message = join(own_back, cross_back, rows)
+    from_ahead = send(message, -1)
     message = made(at(*[(0, 1, b) for b in every]), [(ahead, [None] * end + [1])], after=message)
     cross_own = send(message, 0, 1)
-
-    by_ring = send(join(own_far, cross_far, rows), 1)
-    from_ahead = send(made(at(*[(-1, 0, b) for b in most]), [(cross_back, most)]), -1)
     from_behind = send(join(made(at(*[(1, 0, b) for b in every]), [(by_ring, every)], last=True), cross_next, rows), 1)
     partial = made(at(*[(0, 0, b) for b in every]), [(from_ahead, most + [None]), (ahead, [None] * end + [0])], last=True)
     shard, squares = finish(partial, [cross_own, from_behind], rows, n * lax.axis_size("section"))

time: 96.3 us -> 95.9 us (level)
  no operation moved by 1% of the time
where the time goes in v3:
time: 95.9 us; the launch traced here: 95.7 us
  waiting for transfers between devices  34.1 us (36%)
  Pallas kernels  25 us (26%)
  starting transfers between devices  21 us (22%)
  blocking collectives  12 us (13%)
  local copies, waits for them, and re-layouts  2.76 us (3%)
    ppermute x16, waiting for transfers between devices, send(): lax.ppermute(value, 'dp', [(r, at_offset(r, offset, flip)) for r in range...  34.1 us
    ppermute x16, starting transfers between devices, send(): lax.ppermute(value, 'dp', [(r, at_offset(r, offset, flip)) for r in range...  21 us
    all_to_all x1, blocking collectives, paired(): total = lax.all_to_all(squares, ('dp', 'section'), 0, 0, tiled=True)  12 us
    pallas_call x8, Pallas kernels, piece(): pl.pallas_call(lambda *refs: piece_kernel(place, per, [parts for _, parts...  10.7 us
    pallas_call x1, Pallas kernels, forward(): pl.pallas_call(lambda *refs: forward_kernel(places, rows, *refs), in_spec...  6.21 us
    pallas_call x2, Pallas kernels, update(): pl.pallas_call(lambda *refs: update_kernel(max_norm, states, *refs), grid...  3.07 us
    unnamed x14, local copies, waits for them, and re-layouts  2.75 us
    pallas_call x2, Pallas kernels, fill(): pl.pallas_call(lambda *refs: fill_kernel(moves, len(values), *refs), in_s...  2.35 us
  transfers between devices with their start and end apart: 16, of which 10 were waited for; matrix products, arithmetic and copies ran while one was open for 0% of the time, Pallas kernels for 17%

profile of v3, /device:TPU:0, one launch (start us, length us, event | category | flops | bytes accessed | tf_op | source)
XLA Modules:
  0.0 95.7 jit_solution(16608503807627516310)
XLA Ops:
  0.6 0.0 copy-start
  0.6 6.2 %forward.1 = (bf16[3,512,256]{2,1,0:T(8,128)(2,1)}, bf16[784,256]{1,0:T(8,128)(2,1)}) custom-call(bf16[512,2048]{1,0:T(8,128)(2,1)} %bitcast.14, bf16[512,2048]{1,0:T(8,128)(2,1)} %bitcast.23, bf16[6144,256]{1,0:T(8,128)(2,1)} %bitcast.42), custom_call_target="tpu_custom_call" | custom-call | flops 1024 | bytes 1024 | tf_op jit(solution)/shard_map/forward/pallas_call | solution.py:204
  6.9 3.0 %collective-permute-start.4 = (bf16[784,256]{1,0:T(8,128)(2,1)}, bf16[784,256]{1,0:T(8,128)(2,1)S(1)}, u32[]{:S(2)}, u32[]{:S(2)}) collective-permute-start(bf16[784,256]{1,0:T(8,128)(2,1)} %get-tuple-element.12), channel_id=1, source_target_pairs={{0,4},{4,0},{8,12},{12,8},{16,20},{20,16},{24,28},{28,24},{1,5},{5... | collective-permute-start | bytes 1204232 | tf_op jit(solution)/shard_map/ppermute | solution.py:493
  9.9 0.0 copy-done
  9.9 0.0 copy-start.1
  9.9 1.6 %copy-done.1 = bf16[1,512,2048]{2,1,0:T(8,128)(2,1)S(1)} copy-done((bf16[1,512,2048]{2,1,0:T(8,128)(2,1)S(1)}, bf16[1,512,2048]{2,1,0:T(8,128)(2,1)}, u32[]{:S(2)}) %copy-start.1) | copy-done | bytes 2097176
  11.5 1.1 %copy-done.3 = bf16[3,512,256]{2,1,0:T(8,128)(2,1)S(1)} copy-done((bf16[3,512,256]{2,1,0:T(8,128)(2,1)S(1)}, bf16[3,512,256]{2,1,0:T(8,128)(2,1)}, u32[]{:S(2)}) %copy-start.3) | copy-done | bytes 786456
  12.6 1.1 %piece.8.refs_3_ = bf16[528,256]{1,0:T(8,128)(2,1)S(1)} custom-call(bf16[512,2048]{1,0:T(8,128)(2,1)S(1)} %bitcast.15, bf16[512,2048]{1,0:T(8,128)(2,1)S(1)} %bitcast.24, bf16[3,512,256]{2,1,0:T(8,128)(2,1)S(1)} %copy-done.3), custom_call_target="tpu_custom_call" | custom-call | flops 1416000000 | bytes 1024 | tf_op jit(solution)/shard_map/piece/pallas_call | solution.py:313
  13.7 1.6 %collective-permute-start.2 = (bf16[528,256]{1,0:T(8,128)(2,1)S(1)}, bf16[528,256]{1,0:T(8,128)(2,1)S(1)}, u32[]{:S(2)}, u32[]{:S(2)}) collective-permute-start(bf16[528,256]{1,0:T(8,128)(2,1)S(1)} %piece.8.refs_3_), channel_id=1, source_target_pairs={{0,8},{4,12},{8,24},{12,28},{16,0},{20,4},{24,16},{28,20},{1,9},{5... | collective-permute-start | bytes 811016 | tf_op jit(solution)/shard_map/ppermute | solution.py:493
  15.3 1.1 %piece.9.refs_3_ = bf16[528,256]{1,0:T(8,128)(2,1)S(1)} custom-call(bf16[512,2048]{1,0:T(8,128)(2,1)S(1)} %bitcast.16, bf16[512,2048]{1,0:T(8,128)(2,1)S(1)} %bitcast.25, bf16[3,512,256]{2,1,0:T(8,128)(2,1)S(1)} %copy-done.3, bf16[528,256]{1,0:T(8,128)(2,1)S(1)} %piece.8.refs_3_), custom_call_target="tpu_custom_call" | custom-call | flops 1416000000 | bytes 1024 | tf_op jit(solution)/shard_map/piece/pallas_call | solution.py:313
  16.3 0.6 collective-permute-start
  17.0 1.3 %piece.10.refs_3_.refs_0_ = f32[768,256]{1,0:T(8,128)S(1)} custom-call(bf16[512,2048]{1,0:T(8,128)(2,1)S(1)} %bitcast.17, bf16[512,2048]{1,0:T(8,128)(2,1)S(1)} %bitcast.26, bf16[3,512,256]{2,1,0:T(8,128)(2,1)S(1)} %copy-done.3, bf16[528,256]{1,0:T(8,128)(2,1)S(1)} %piece.9.refs_3_), custom_call_target="tpu_custom_call" | custom-call | flops 1416000000 | bytes 1024 | tf_op jit(solution)/shard_map/piece/pallas_call | solution.py:313
  18.3 0.0 copy-start.2
  18.3 1.9 %collective-permute-done.4.refs_1_ = bf16[784,256]{1,0:T(8,128)(2,1)S(1)} collective-permute-done((bf16[784,256]{1,0:T(8,128)(2,1)}, bf16[784,256]{1,0:T(8,128)(2,1)S(1)}, u32[]{:S(2)}, u32[]{:S(2)}) %collective-permute-start.4) | collective-permute-done | bytes 401440 | tf_op jit(solution)/shard_map/ppermute | solution.py:493
  20.2 0.7 join.4
  20.9 3.2 %collective-permute-start.5 = (bf16[784,256]{1,0:T(8,128)(2,1)S(1)}, bf16[784,256]{1,0:T(8,128)(2,1)S(1)}, u32[]{:S(2)}, u32[]{:S(2)}) collective-permute-start(bf16[784,256]{1,0:T(8,128)(2,1)S(1)} %join.4), channel_id=1, source_target_pairs={{0,16},{4,20},{8,0},{12,4},{16,24},{20,28},{24,8},{28,12},{1,17},{... | collective-permute-start | bytes 1204232 | tf_op jit(solution)/shard_map/ppermute | solution.py:493
  24.1 0.0 copy-done.2
  24.1 1.6 %piece.11.refs_3_ = bf16[784,256]{1,0:T(8,128)(2,1)S(1)} custom-call(bf16[512,2048]{1,0:T(8,128)(2,1)S(1)} %bitcast.18, bf16[512,2048]{1,0:T(8,128)(2,1)S(1)} %bitcast.27, bf16[3,512,256]{2,1,0:T(8,128)(2,1)S(1)} %copy-done.3, f32[768,256]{1,0:T(8,128)S(1)} %piece.10.refs_3_.refs_0_), custom_call_target="tpu_custom_call" | custom-call | flops 1416000000 | bytes 1024 | tf_op jit(solution)/shard_map/piece/pallas_call | solution.py:313
  25.7 1.6 %collective-permute-start.6 = (bf16[784,256]{1,0:T(8,128)(2,1)S(1)}, bf16[784,256]{1,0:T(8,128)(2,1)S(1)}, u32[]{:S(2)}, u32[]{:S(2)}) collective-permute-start(bf16[784,256]{1,0:T(8,128)(2,1)S(1)} %piece.11.refs_3_), channel_id=1, source_target_pairs={{0,4},{4,0},{8,12},{12,8},{16,20},{20,16},{24,28},{28,24},{1,5},{5... | collective-permute-start | bytes 1204232 | tf_op jit(solution)/shard_map/ppermute | solution.py:493
  27.2 0.9 piece.12.refs_0_
  28.1 0.0 collective-permute-done.refs_1_
  28.1 0.5 join.3.refs_5_
  28.6 0.1 collective-permute-start.1
  28.7 0.0 collective-permute-done.2.refs_5_.refs_6_.refs_3_.refs_4_
  28.7 1.7 %piece.14 = bf16[784,256]{1,0:T(8,128)(2,1)S(1)} custom-call(bf16[512,2048]{1,0:T(8,128)(2,1)S(1)} %bitcast.20, bf16[512,2048]{1,0:T(8,128)(2,1)S(1)} %bitcast.29, bf16[3,512,256]{2,1,0:T(8,128)(2,1)S(1)} %copy-done.3, bf16[528,256]{1,0:T(8,128)(2,1)S(1)} %collective-permute-done.2.refs_5_.refs_6_.refs_3_.refs_4_, ...), custom_call_target="tpu_custom_call" | custom-call | flops 1416000000 | bytes 1024 | tf_op jit(solution)/shard_map/piece/pallas_call | solution.py:313
  30.4 1.5 %collective-permute-start.3 = (bf16[784,256]{1,0:T(8,128)(2,1)S(1)}, bf16[784,256]{1,0:T(8,128)(2,1)S(1)}, u32[]{:S(2)}, u32[]{:S(2)}) collective-permute-start(bf16[784,256]{1,0:T(8,128)(2,1)S(1)} %piece.14), channel_id=1, source_target_pairs={{0,4},{4,0},{8,12},{12,8},{16,20},{20,16},{24,28},{28,24},{1,5},{5... | collective-permute-start | bytes 1204232 | tf_op jit(solution)/shard_map/ppermute | solution.py:493
  31.9 1.6 %collective-permute-done.5.refs_3_.refs_4_ = bf16[784,256]{1,0:T(8,128)(2,1)S(1)} collective-permute-done((bf16[784,256]{1,0:T(8,128)(2,1)S(1)}, bf16[784,256]{1,0:T(8,128)(2,1)S(1)}, u32[]{:S(2)}, u32[]{:S(2)}) %collective-permute-start.5) | collective-permute-done | bytes 401440 | tf_op jit(solution)/shard_map/ppermute | solution.py:493
  33.5 1.4 %piece.15.refs_0_ = f32[768,256]{1,0:T(8,128)S(1)} custom-call(bf16[512,2048]{1,0:T(8,128)(2,1)S(1)} %bitcast.21, bf16[512,2048]{1,0:T(8,128)(2,1)S(1)} %bitcast.30, bf16[3,512,256]{2,1,0:T(8,128)(2,1)S(1)} %copy-done.3, bf16[784,256]{1,0:T(8,128)(2,1)S(1)} %collective-permute-done.5.refs_3_.refs_4_, bf16[784,256]{1,0:T(8,128)(2,1)S(1)} %collective-permute-done.5.refs_3_.refs_4_), custom_call_target="tpu_custom_call" | custom-call | flops 1416000000 | bytes 1024 | tf_op jit(solution)/shard_map/piece/pallas_call | solution.py:313
  34.9 3.1 %collective-permute-done.6.refs_1_ = bf16[784,256]{1,0:T(8,128)(2,1)S(1)} collective-permute-done((bf16[784,256]{1,0:T(8,128)(2,1)S(1)}, bf16[784,256]{1,0:T(8,128)(2,1)S(1)}, u32[]{:S(2)}, u32[]{:S(2)}) %collective-permute-start.6) | collective-permute-done | bytes 401440 | tf_op jit(solution)/shard_map/ppermute | solution.py:493
  38.0 0.7 join.5
  38.6 1.6 %collective-permute-start.7 = (bf16[784,256]{1,0:T(8,128)(2,1)S(1)}, bf16[784,256]{1,0:T(8,128)(2,1)S(1)}, u32[]{:S(2)}, u32[]{:S(2)}) collective-permute-start(bf16[784,256]{1,0:T(8,128)(2,1)S(1)} %join.5), channel_id=1, source_target_pairs={{0,16},{4,20},{8,0},{12,4},{16,24},{20,28},{24,8},{28,12},{1,17},{... | collective-permute-start | bytes 1204232 | tf_op jit(solution)/shard_map/ppermute | solution.py:493
  40.3 0.0 collective-permute-done.1.refs_3_.refs_4_
  40.3 1.8 %piece.13.refs_0_ = f32[768,256]{1,0:T(8,128)S(1)} custom-call(bf16[512,2048]{1,0:T(8,128)(2,1)S(1)} %bitcast.22, bf16[512,2048]{1,0:T(8,128)(2,1)S(1)} %bitcast.31, bf16[3,512,256]{2,1,0:T(8,128)(2,1)S(1)} %copy-done.3, bf16[528,256]{1,0:T(8,128)(2,1)S(1)} %collective-permute-done.1.refs_3_.refs_4_, ...), custom_call_target="tpu_custom_call" | custom-call | flops 1416000000 | bytes 1024 | tf_op jit(solution)/shard_map/piece/pallas_call | solution.py:313
  42.1 0.0 copy-start.4
  42.1 0.0 copy-start.5
  42.1 0.0 copy-start.6
  42.1 1.0 collective-permute-done.3.refs_1_
  43.1 3.7 %collective-permute-done.7.refs_2_ = bf16[784,256]{1,0:T(8,128)(2,1)S(1)} collective-permute-done((bf16[784,256]{1,0:T(8,128)(2,1)S(1)}, bf16[784,256]{1,0:T(8,128)(2,1)S(1)}, u32[]{:S(2)}, u32[]{:S(2)}) %collective-permute-start.7) | collective-permute-done | bytes 401440 | tf_op jit(solution)/shard_map/ppermute | solution.py:493
  46.8 0.8 finish.1
  47.6 12.0 %all_to_all.11 = f32[32,1,128]{2,1,0:T(1,128)S(1)} all-to-all(f32[32,1,128]{2,1,0:T(1,128)S(1)} %bitcast.40), channel_id=1, replica_groups=mesh['dp'=8,'section'=4] {'dp','section'}, dimensions={0} | all-to-all | bytes 32768 | tf_op jit(solution)/shard_map/all_to_all | solution.py:530
  59.6 0.0 copy-done.4
  59.6 0.0 copy-done.5
  59.6 0.0 copy-done.6
  59.6 0.8 update.1.own_ref.refs_0_
  60.5 0.6 collective-permute-start.9
  61.1 0.6 collective-permute-start.8
  61.7 1.5 %collective-permute-start.13 = (bf16[320,256]{1,0:T(8,128)(2,1)S(1)}, bf16[320,256]{1,0:T(8,128)(2,1)S(1)}, u32[]{:S(2)}, u32[]{:S(2)}) collective-permute-start(bf16[320,256]{1,0:T(8,128)(2,1)S(1)} %slice.4), channel_id=1, source_target_pairs={{0,8},{4,12},{8,24},{12,28},{16,0},{20,4},{24,16},{28,20},{1,9},{5... | collective-permute-start | bytes 491528 | tf_op jit(solution)/shard_map/ppermute | solution.py:493
  63.2 8.8 %collective-permute-done.9.refs_0_ = bf16[768,256]{1,0:T(8,128)(2,1)S(1)} collective-permute-done((bf16[768,256]{1,0:T(8,128)(2,1)S(1)}, bf16[768,256]{1,0:T(8,128)(2,1)S(1)}, u32[]{:S(2)}, u32[]{:S(2)}) %collective-permute-start.9) | collective-permute-done | bytes 393248 | tf_op jit(solution)/shard_map/ppermute | solution.py:493
  71.9 0.0 collective-permute-done.8.refs_1_.other_ref
  71.9 0.3 collective-permute-start.10
  72.2 2.4 %collective-permute-start.12 = (bf16[768,256]{1,0:T(8,128)(2,1)S(1)}, bf16[768,256]{1,0:T(8,128)(2,1)S(1)}, u32[]{:S(2)}, u32[]{:S(2)}) collective-permute-start(bf16[768,256]{1,0:T(8,128)(2,1)S(1)} %behind.4.refs_1_.refs_2_), channel_id=1, source_target_pairs={{0,16},{4,20},{8,0},{12,4},{16,24},{20,28},{24,8},{28,12},{1,17},{... | collective-permute-start | bytes 1179656 | tf_op jit(solution)/shard_map/ppermute | solution.py:493
  74.6 1.8 %collective-permute-done.13.refs_0_ = bf16[320,256]{1,0:T(8,128)(2,1)S(1)} collective-permute-done((bf16[320,256]{1,0:T(8,128)(2,1)S(1)}, bf16[320,256]{1,0:T(8,128)(2,1)S(1)}, u32[]{:S(2)}, u32[]{:S(2)}) %collective-permute-start.13) | collective-permute-done | bytes 163872 | tf_op jit(solution)/shard_map/ppermute | solution.py:493
  76.4 0.1 collective-permute-start.14
  76.4 6.8 %collective-permute-done.10.after_ref.refs_1_.refs_4_ = bf16[768,256]{1,0:T(8,128)(2,1)S(1)} collective-permute-done((bf16[768,256]{1,0:T(8,128)(2,1)S(1)}, bf16[768,256]{1,0:T(8,128)(2,1)S(1)}, u32[]{:S(2)}, u32[]{:S(2)}) %collective-permute-start.10) | collective-permute-done | bytes 393248 | tf_op jit(solution)/shard_map/ppermute | solution.py:493
  83.3 0.1 both.1
  83.4 1.4 %collective-permute-start.11 = (bf16[896,256]{1,0:T(8,128)(2,1)S(1)}, bf16[896,256]{1,0:T(8,128)(2,1)S(1)}, u32[]{:S(2)}, u32[]{:S(2)}) collective-permute-start(bf16[896,256]{1,0:T(8,128)(2,1)S(1)} %both.1), channel_id=1, source_target_pairs={{0,8},{4,12},{8,24},{12,28},{16,0},{20,4},{24,16},{28,20},{1,9},{5... | collective-permute-start | bytes 1376264 | tf_op jit(solution)/shard_map/ppermute | solution.py:493
  84.7 0.4 collective-permute-done.12.refs_0_
  85.2 0.0 collective-permute-done.14.refs_1_.refs_5_
  85.2 0.9 collective-permute-start.15
  86.1 2.3 %states.1 = (f32[768,256]{1,0:T(8,128)}, f32[768,256]{1,0:T(8,128)}, f32[768,256]{1,0:T(8,128)}) custom-call(f32[32,128]{1,0:T(8,128)S(1)} %bitcast.39, f32[768,256]{1,0:T(8,128)S(1)} %get-tuple-element.14.refs_1_, f32[768,256]{1,0:T(8,128)S(1)} %bitcast.33, f32[768,256]{1,0:T(8,128)S(1)} %bitcast.35, f32[768,256]{1,0:T(8,128)S(1)} %bitcast.37), custom_call_target="tpu_custom_call" | custom-call | flops 1024 | bytes 1024 | tf_op jit(solution)/shard_map/states/pallas_call | solution.py:404
  88.4 1.4 %fill.2.refs_2_ = bf16[6144,256]{1,0:T(8,128)(2,1)} custom-call(bf16[768,256]{1,0:T(8,128)(2,1)S(1)} %update.1.own_ref.refs_0_, bf16[768,256]{1,0:T(8,128)(2,1)S(1)} %collective-permute-done.8.refs_1_.other_ref, bf16[768,256]{1,0:T(8,128)(2,1)S(1)} %behind.4.refs_1_.refs_2_, bf16[320,256]{1,0:T(8,128)(2,1)S(1)} %behind.6.refs_3_, ...), custom_call_target="tpu_custom_call" | custom-call | flops 1024 | bytes 1024 | tf_op jit(solution)/shard_map/fill/pallas_call | solution.py:466
  89.8 5.0 %collective-permute-done.15.refs_1_ = bf16[768,256]{1,0:T(8,128)(2,1)S(1)} collective-permute-done((bf16[768,256]{1,0:T(8,128)(2,1)S(1)}, bf16[768,256]{1,0:T(8,128)(2,1)S(1)}, u32[]{:S(2)}, u32[]{:S(2)}) %collective-permute-start.15) | collective-permute-done | bytes 393248 | tf_op jit(solution)/shard_map/ppermute | solution.py:493
  94.8 0.0 collective-permute-done.11.refs_0_
  94.8 0.9 fill.3
  (6 shorter events, 0.0 us)
Async XLA Ops:
  0.6 9.2 %copy-start = (bf16[1,512,2048]{2,1,0:T(8,128)(2,1)S(1)}, bf16[1,512,2048]{2,1,0:T(8,128)(2,1)}, u32[]{:S(2)}) copy-start(bf16[1,512,2048]{2,1,0:T(8,128)(2,1)} %param.7) | copy-start | bytes 6291460
  6.9 13.3 %collective-permute-start.4 = (bf16[784,256]{1,0:T(8,128)(2,1)}, bf16[784,256]{1,0:T(8,128)(2,1)S(1)}, u32[]{:S(2)}, u32[]{:S(2)}) collective-permute-start(bf16[784,256]{1,0:T(8,128)(2,1)} %get-tuple-element.12), channel_id=1, source_target_pairs={{0,4},{4,0},{8,12},{12,8},{16,20},{20,16},{24,28},{28,24},{1,5},{5... | collective-permute-start | bytes 1204232 | tf_op jit(solution)/shard_map/ppermute | solution.py:493
  9.9 1.6 %copy-start.1 = (bf16[1,512,2048]{2,1,0:T(8,128)(2,1)S(1)}, bf16[1,512,2048]{2,1,0:T(8,128)(2,1)}, u32[]{:S(2)}) copy-start(bf16[1,512,2048]{2,1,0:T(8,128)(2,1)} %param.8) | copy-start | bytes 6291460
  11.5 1.1 %copy-start.3 = (bf16[3,512,256]{2,1,0:T(8,128)(2,1)S(1)}, bf16[3,512,256]{2,1,0:T(8,128)(2,1)}, u32[]{:S(2)}) copy-start(bf16[3,512,256]{2,1,0:T(8,128)(2,1)} %get-tuple-element.11.refs_2_) | copy-start | bytes 2359300
  13.7 15.1 %collective-permute-start.2 = (bf16[528,256]{1,0:T(8,128)(2,1)S(1)}, bf16[528,256]{1,0:T(8,128)(2,1)S(1)}, u32[]{:S(2)}, u32[]{:S(2)}) collective-permute-start(bf16[528,256]{1,0:T(8,128)(2,1)S(1)} %piece.8.refs_3_), channel_id=1, source_target_pairs={{0,8},{4,12},{8,24},{12,28},{16,0},{20,4},{24,16},{28,20},{1,9},{5... | collective-permute-start | bytes 811016 | tf_op jit(solution)/shard_map/ppermute | solution.py:493
  16.3 11.8 %collective-permute-start = (bf16[528,256]{1,0:T(8,128)(2,1)S(1)}, bf16[528,256]{1,0:T(8,128)(2,1)S(1)}, u32[]{:S(2)}, u32[]{:S(2)}) collective-permute-start(bf16[528,256]{1,0:T(8,128)(2,1)S(1)} %piece.9.refs_3_), channel_id=1, source_target_pairs={{0,4},{4,0},{8,12},{12,8},{16,20},{20,16},{24,28},{28,24},{1,5},{5... | collective-permute-start | bytes 811016 | tf_op jit(solution)/shard_map/ppermute | solution.py:493
  18.3 5.8 %copy-start.2 = (bf16[1,512,2048]{2,1,0:T(8,128)(2,1)S(1)}, bf16[1,512,2048]{2,1,0:T(8,128)(2,1)}, u32[]{:S(2)}) copy-start(bf16[1,512,2048]{2,1,0:T(8,128)(2,1)} %param.8) | copy-start | bytes 6291460
  20.9 12.6 %collective-permute-start.5 = (bf16[784,256]{1,0:T(8,128)(2,1)S(1)}, bf16[784,256]{1,0:T(8,128)(2,1)S(1)}, u32[]{:S(2)}, u32[]{:S(2)}) collective-permute-start(bf16[784,256]{1,0:T(8,128)(2,1)S(1)} %join.4), channel_id=1, source_target_pairs={{0,16},{4,20},{8,0},{12,4},{16,24},{20,28},{24,8},{28,12},{1,17},{... | collective-permute-start | bytes 1204232 | tf_op jit(solution)/shard_map/ppermute | solution.py:493
  25.7 12.3 %collective-permute-start.6 = (bf16[784,256]{1,0:T(8,128)(2,1)S(1)}, bf16[784,256]{1,0:T(8,128)(2,1)S(1)}, u32[]{:S(2)}, u32[]{:S(2)}) collective-permute-start(bf16[784,256]{1,0:T(8,128)(2,1)S(1)} %piece.11.refs_3_), channel_id=1, source_target_pairs={{0,4},{4,0},{8,12},{12,8},{16,20},{20,16},{24,28},{28,24},{1,5},{5... | collective-permute-start | bytes 1204232 | tf_op jit(solution)/shard_map/ppermute | solution.py:493
  28.6 11.7 %collective-permute-start.1 = (bf16[528,256]{1,0:T(8,128)(2,1)S(1)}, bf16[528,256]{1,0:T(8,128)(2,1)S(1)}, u32[]{:S(2)}, u32[]{:S(2)}) collective-permute-start(bf16[528,256]{1,0:T(8,128)(2,1)S(1)} %join.3.refs_5_), channel_id=1, source_target_pairs={{0,8},{4,12},{8,24},{12,28},{16,0},{20,4},{24,16},{28,20},{1,9},{5... | collective-permute-start | bytes 811016 | tf_op jit(solution)/shard_map/ppermute | solution.py:493
  30.4 12.7 %collective-permute-start.3 = (bf16[784,256]{1,0:T(8,128)(2,1)S(1)}, bf16[784,256]{1,0:T(8,128)(2,1)S(1)}, u32[]{:S(2)}, u32[]{:S(2)}) collective-permute-start(bf16[784,256]{1,0:T(8,128)(2,1)S(1)} %piece.14), channel_id=1, source_target_pairs={{0,4},{4,0},{8,12},{12,8},{16,20},{20,16},{24,28},{28,24},{1,5},{5... | collective-permute-start | bytes 1204232 | tf_op jit(solution)/shard_map/ppermute | solution.py:493
  38.6 8.2 %collective-permute-start.7 = (bf16[784,256]{1,0:T(8,128)(2,1)S(1)}, bf16[784,256]{1,0:T(8,128)(2,1)S(1)}, u32[]{:S(2)}, u32[]{:S(2)}) collective-permute-start(bf16[784,256]{1,0:T(8,128)(2,1)S(1)} %join.5), channel_id=1, source_target_pairs={{0,16},{4,20},{8,0},{12,4},{16,24},{20,28},{24,8},{28,12},{1,17},{... | collective-permute-start | bytes 1204232 | tf_op jit(solution)/shard_map/ppermute | solution.py:493
  42.1 17.6 %copy-start.4 = (f32[1,768,256]{2,1,0:T(8,128)S(1)}, f32[1,768,256]{2,1,0:T(8,128)}, u32[]{:S(2)}) copy-start(f32[1,768,256]{2,1,0:T(8,128)} %param.9) | copy-start | bytes 2359300
  42.1 17.6 %copy-start.5 = (f32[1,768,256]{2,1,0:T(8,128)S(1)}, f32[1,768,256]{2,1,0:T(8,128)}, u32[]{:S(2)}) copy-start(f32[1,768,256]{2,1,0:T(8,128)} %param.10) | copy-start | bytes 2359300
  42.1 17.5 %copy-start.6 = (f32[1,768,256]{2,1,0:T(8,128)S(1)}, f32[1,768,256]{2,1,0:T(8,128)}, u32[]{:S(2)}) copy-start(f32[1,768,256]{2,1,0:T(8,128)} %param.11) | copy-start | bytes 2359300
  60.5 11.5 %collective-permute-start.9 = (bf16[768,256]{1,0:T(8,128)(2,1)S(1)}, bf16[768,256]{1,0:T(8,128)(2,1)S(1)}, u32[]{:S(2)}, u32[]{:S(2)}) collective-permute-start(bf16[768,256]{1,0:T(8,128)(2,1)S(1)} %update.1.own_ref.refs_0_), channel_id=1, source_target_pairs={{0,16},{4,20},{8,0},{12,4},{16,24},{20,28},{24,8},{28,12},{1,17},{... | collective-permute-start | bytes 1179656 | tf_op jit(solution)/shard_map/ppermute | solution.py:493
  61.1 10.8 %collective-permute-start.8 = (bf16[768,256]{1,0:T(8,128)(2,1)S(1)}, bf16[768,256]{1,0:T(8,128)(2,1)S(1)}, u32[]{:S(2)}, u32[]{:S(2)}) collective-permute-start(bf16[768,256]{1,0:T(8,128)(2,1)S(1)} %update.1.own_ref.refs_0_), channel_id=1, source_target_pairs={{0,4},{4,0},{8,12},{12,8},{16,20},{20,16},{24,28},{28,24},{1,5},{5... | collective-permute-start | bytes 1179656 | tf_op jit(solution)/shard_map/ppermute | solution.py:493
  61.7 14.7 %collective-permute-start.13 = (bf16[320,256]{1,0:T(8,128)(2,1)S(1)}, bf16[320,256]{1,0:T(8,128)(2,1)S(1)}, u32[]{:S(2)}, u32[]{:S(2)}) collective-permute-start(bf16[320,256]{1,0:T(8,128)(2,1)S(1)} %slice.4), channel_id=1, source_target_pairs={{0,8},{4,12},{8,24},{12,28},{16,0},{20,4},{24,16},{28,20},{1,9},{5... | collective-permute-start | bytes 491528 | tf_op jit(solution)/shard_map/ppermute | solution.py:493
  71.9 11.4 %collective-permute-start.10 = (bf16[768,256]{1,0:T(8,128)(2,1)S(1)}, bf16[768,256]{1,0:T(8,128)(2,1)S(1)}, u32[]{:S(2)}, u32[]{:S(2)}) collective-permute-start(bf16[768,256]{1,0:T(8,128)(2,1)S(1)} %behind.4.refs_1_.refs_2_), channel_id=1, source_target_pairs={{0,4},{4,0},{8,12},{12,8},{16,20},{20,16},{24,28},{28,24},{1,5},{5... | collective-permute-start | bytes 1179656 | tf_op jit(solution)/shard_map/ppermute | solution.py:493
  72.2 13.0 %collective-permute-start.12 = (bf16[768,256]{1,0:T(8,128)(2,1)S(1)}, bf16[768,256]{1,0:T(8,128)(2,1)S(1)}, u32[]{:S(2)}, u32[]{:S(2)}) collective-permute-start(bf16[768,256]{1,0:T(8,128)(2,1)S(1)} %behind.4.refs_1_.refs_2_), channel_id=1, source_target_pairs={{0,16},{4,20},{8,0},{12,4},{16,24},{20,28},{24,8},{28,12},{1,17},{... | collective-permute-start | bytes 1179656 | tf_op jit(solution)/shard_map/ppermute | solution.py:493
  76.4 8.8 %collective-permute-start.14 = (bf16[320,256]{1,0:T(8,128)(2,1)S(1)}, bf16[320,256]{1,0:T(8,128)(2,1)S(1)}, u32[]{:S(2)}, u32[]{:S(2)}) collective-permute-start(bf16[320,256]{1,0:T(8,128)(2,1)S(1)} %behind.6.refs_3_), channel_id=1, source_target_pairs={{0,4},{4,0},{8,12},{12,8},{16,20},{20,16},{24,28},{28,24},{1,5},{5... | collective-permute-start | bytes 491528 | tf_op jit(solution)/shard_map/ppermute | solution.py:493
  83.4 11.4 %collective-permute-start.11 = (bf16[896,256]{1,0:T(8,128)(2,1)S(1)}, bf16[896,256]{1,0:T(8,128)(2,1)S(1)}, u32[]{:S(2)}, u32[]{:S(2)}) collective-permute-start(bf16[896,256]{1,0:T(8,128)(2,1)S(1)} %both.1), channel_id=1, source_target_pairs={{0,8},{4,12},{8,24},{12,28},{16,0},{20,4},{24,16},{28,20},{1,9},{5... | collective-permute-start | bytes 1376264 | tf_op jit(solution)/shard_map/ppermute | solution.py:493
  85.2 9.6 %collective-permute-start.15 = (bf16[768,256]{1,0:T(8,128)(2,1)S(1)}, bf16[768,256]{1,0:T(8,128)(2,1)S(1)}, u32[]{:S(2)}, u32[]{:S(2)}) collective-permute-start(bf16[768,256]{1,0:T(8,128)(2,1)S(1)} %behind.7.refs_6_), channel_id=1, source_target_pairs={{0,4},{4,0},{8,12},{12,8},{16,20},{20,16},{24,28},{28,24},{1,5},{5... | collective-permute-start | bytes 1179656 | tf_op jit(solution)/shard_map/ppermute | solution.py:493

commit v4 on v3

--- a/solution.py
+++ b/solution.py
@@ -532,7 +532,7 @@
     states = (shard, master[0], moment1[0], moment2[0], max_norm)
     (own,) = update(total, *states, shard_rows, False)
 
-    cut = shard_rows * 7 // 12 // PAD * PAD
+    cut = shard_rows * 5 // 8 // PAD * PAD
     other = send(own, 0, 1)
     behind = behind_of(send(own, 1), other)
     tail = send(own[cut:], -1)

time: 95.9 us -> 95.8 us (level)
  transfers between devices with their start and end apart: 16 -> 16, of which waited for: 10 -> 11; matrix products, arithmetic and copies ran while one was open for 0% -> 0% of each run, Pallas kernels for 17% -> 17%
where the time goes in v4:
time: 95.8 us; the launch traced here: 95.6 us
  waiting for transfers between devices  33.8 us (35%)
  Pallas kernels  25 us (26%)
  starting transfers between devices  21.2 us (22%)
  blocking collectives  12 us (13%)
  local copies, waits for them, and re-layouts  2.76 us (3%)
    ppermute x16, waiting for transfers between devices, send(): lax.ppermute(value, 'dp', [(r, at_offset(r, offset, flip)) for r in range...  33.8 us
    ppermute x16, starting transfers between devices, send(): lax.ppermute(value, 'dp', [(r, at_offset(r, offset, flip)) for r in range...  21.2 us
    all_to_all x1, blocking collectives, paired(): total = lax.all_to_all(squares, ('dp', 'section'), 0, 0, tiled=True)  12 us
    pallas_call x8, Pallas kernels, piece(): pl.pallas_call(lambda *refs: piece_kernel(place, per, [parts for _, parts...  10.7 us
    pallas_call x1, Pallas kernels, forward(): pl.pallas_call(lambda *refs: forward_kernel(places, rows, *refs), in_spec...  6.21 us
    pallas_call x2, Pallas kernels, update(): pl.pallas_call(lambda *refs: update_kernel(max_norm, states, *refs), grid...  3.07 us
    unnamed x14, local copies, waits for them, and re-layouts  2.75 us
    pallas_call x2, Pallas kernels, fill(): pl.pallas_call(lambda *refs: fill_kernel(moves, len(values), *refs), in_s...  2.35 us
  transfers between devices with their start and end apart: 16, of which 11 were waited for; matrix products, arithmetic and copies ran while one was open for 0% of the time, Pallas kernels for 17%

profile of v4, /device:TPU:0, one launch (start us, length us, event | category | flops | bytes accessed | tf_op | source)
XLA Modules:
  0.0 95.6 jit_solution(15090960075622723625)
XLA Ops:
  0.6 0.0 copy-start
  0.6 6.2 %forward.1 = (bf16[3,512,256]{2,1,0:T(8,128)(2,1)}, bf16[784,256]{1,0:T(8,128)(2,1)}) custom-call(bf16[512,2048]{1,0:T(8,128)(2,1)} %bitcast.14, bf16[512,2048]{1,0:T(8,128)(2,1)} %bitcast.23, bf16[6144,256]{1,0:T(8,128)(2,1)} %bitcast.42), custom_call_target="tpu_custom_call" | custom-call | flops 1024 | bytes 1024 | tf_op jit(solution)/shard_map/forward/pallas_call | solution.py:204
  6.9 3.0 %collective-permute-start.4 = (bf16[784,256]{1,0:T(8,128)(2,1)}, bf16[784,256]{1,0:T(8,128)(2,1)S(1)}, u32[]{:S(2)}, u32[]{:S(2)}) collective-permute-start(bf16[784,256]{1,0:T(8,128)(2,1)} %get-tuple-element.12), channel_id=1, source_target_pairs={{0,4},{4,0},{8,12},{12,8},{16,20},{20,16},{24,28},{28,24},{1,5},{5... | collective-permute-start | bytes 1204232 | tf_op jit(solution)/shard_map/ppermute | solution.py:493
  9.9 0.0 copy-done
  9.9 0.0 copy-start.1
  9.9 1.6 %copy-done.1 = bf16[1,512,2048]{2,1,0:T(8,128)(2,1)S(1)} copy-done((bf16[1,512,2048]{2,1,0:T(8,128)(2,1)S(1)}, bf16[1,512,2048]{2,1,0:T(8,128)(2,1)}, u32[]{:S(2)}) %copy-start.1) | copy-done | bytes 2097176
  11.5 1.1 %copy-done.3 = bf16[3,512,256]{2,1,0:T(8,128)(2,1)S(1)} copy-done((bf16[3,512,256]{2,1,0:T(8,128)(2,1)S(1)}, bf16[3,512,256]{2,1,0:T(8,128)(2,1)}, u32[]{:S(2)}) %copy-start.3) | copy-done | bytes 786456
  12.6 1.1 %piece.8.refs_3_ = bf16[528,256]{1,0:T(8,128)(2,1)S(1)} custom-call(bf16[512,2048]{1,0:T(8,128)(2,1)S(1)} %bitcast.15, bf16[512,2048]{1,0:T(8,128)(2,1)S(1)} %bitcast.24, bf16[3,512,256]{2,1,0:T(8,128)(2,1)S(1)} %copy-done.3), custom_call_target="tpu_custom_call" | custom-call | flops 1416000000 | bytes 1024 | tf_op jit(solution)/shard_map/piece/pallas_call | solution.py:313
  13.7 1.6 %collective-permute-start.2 = (bf16[528,256]{1,0:T(8,128)(2,1)S(1)}, bf16[528,256]{1,0:T(8,128)(2,1)S(1)}, u32[]{:S(2)}, u32[]{:S(2)}) collective-permute-start(bf16[528,256]{1,0:T(8,128)(2,1)S(1)} %piece.8.refs_3_), channel_id=1, source_target_pairs={{0,8},{4,12},{8,24},{12,28},{16,0},{20,4},{24,16},{28,20},{1,9},{5... | collective-permute-start | bytes 811016 | tf_op jit(solution)/shard_map/ppermute | solution.py:493
  15.3 1.1 %piece.9.refs_3_ = bf16[528,256]{1,0:T(8,128)(2,1)S(1)} custom-call(bf16[512,2048]{1,0:T(8,128)(2,1)S(1)} %bitcast.16, bf16[512,2048]{1,0:T(8,128)(2,1)S(1)} %bitcast.25, bf16[3,512,256]{2,1,0:T(8,128)(2,1)S(1)} %copy-done.3, bf16[528,256]{1,0:T(8,128)(2,1)S(1)} %piece.8.refs_3_), custom_call_target="tpu_custom_call" | custom-call | flops 1416000000 | bytes 1024 | tf_op jit(solution)/shard_map/piece/pallas_call | solution.py:313
  16.3 0.6 collective-permute-start
  17.0 1.3 %piece.10.refs_3_.refs_0_ = f32[768,256]{1,0:T(8,128)S(1)} custom-call(bf16[512,2048]{1,0:T(8,128)(2,1)S(1)} %bitcast.17, bf16[512,2048]{1,0:T(8,128)(2,1)S(1)} %bitcast.26, bf16[3,512,256]{2,1,0:T(8,128)(2,1)S(1)} %copy-done.3, bf16[528,256]{1,0:T(8,128)(2,1)S(1)} %piece.9.refs_3_), custom_call_target="tpu_custom_call" | custom-call | flops 1416000000 | bytes 1024 | tf_op jit(solution)/shard_map/piece/pallas_call | solution.py:313
  18.3 0.0 copy-start.2
  18.3 1.9 %collective-permute-done.4.refs_1_ = bf16[784,256]{1,0:T(8,128)(2,1)S(1)} collective-permute-done((bf16[784,256]{1,0:T(8,128)(2,1)}, bf16[784,256]{1,0:T(8,128)(2,1)S(1)}, u32[]{:S(2)}, u32[]{:S(2)}) %collective-permute-start.4) | collective-permute-done | bytes 401440 | tf_op jit(solution)/shard_map/ppermute | solution.py:493
  20.2 0.7 join.4
  20.9 3.2 %collective-permute-start.5 = (bf16[784,256]{1,0:T(8,128)(2,1)S(1)}, bf16[784,256]{1,0:T(8,128)(2,1)S(1)}, u32[]{:S(2)}, u32[]{:S(2)}) collective-permute-start(bf16[784,256]{1,0:T(8,128)(2,1)S(1)} %join.4), channel_id=1, source_target_pairs={{0,16},{4,20},{8,0},{12,4},{16,24},{20,28},{24,8},{28,12},{1,17},{... | collective-permute-start | bytes 1204232 | tf_op jit(solution)/shard_map/ppermute | solution.py:493
  24.1 0.0 copy-done.2
  24.1 1.6 %piece.11.refs_3_ = bf16[784,256]{1,0:T(8,128)(2,1)S(1)} custom-call(bf16[512,2048]{1,0:T(8,128)(2,1)S(1)} %bitcast.18, bf16[512,2048]{1,0:T(8,128)(2,1)S(1)} %bitcast.27, bf16[3,512,256]{2,1,0:T(8,128)(2,1)S(1)} %copy-done.3, f32[768,256]{1,0:T(8,128)S(1)} %piece.10.refs_3_.refs_0_), custom_call_target="tpu_custom_call" | custom-call | flops 1416000000 | bytes 1024 | tf_op jit(solution)/shard_map/piece/pallas_call | solution.py:313
  25.7 1.6 %collective-permute-start.6 = (bf16[784,256]{1,0:T(8,128)(2,1)S(1)}, bf16[784,256]{1,0:T(8,128)(2,1)S(1)}, u32[]{:S(2)}, u32[]{:S(2)}) collective-permute-start(bf16[784,256]{1,0:T(8,128)(2,1)S(1)} %piece.11.refs_3_), channel_id=1, source_target_pairs={{0,4},{4,0},{8,12},{12,8},{16,20},{20,16},{24,28},{28,24},{1,5},{5... | collective-permute-start | bytes 1204232 | tf_op jit(solution)/shard_map/ppermute | solution.py:493
  27.2 0.9 piece.12.refs_0_
  28.1 0.0 collective-permute-done.refs_1_
  28.1 0.5 join.3.refs_5_
  28.6 0.1 collective-permute-start.1
  28.7 0.0 collective-permute-done.2.refs_5_.refs_6_.refs_3_.refs_4_
  28.7 1.7 %piece.14 = bf16[784,256]{1,0:T(8,128)(2,1)S(1)} custom-call(bf16[512,2048]{1,0:T(8,128)(2,1)S(1)} %bitcast.20, bf16[512,2048]{1,0:T(8,128)(2,1)S(1)} %bitcast.29, bf16[3,512,256]{2,1,0:T(8,128)(2,1)S(1)} %copy-done.3, bf16[528,256]{1,0:T(8,128)(2,1)S(1)} %collective-permute-done.2.refs_5_.refs_6_.refs_3_.refs_4_, ...), custom_call_target="tpu_custom_call" | custom-call | flops 1416000000 | bytes 1024 | tf_op jit(solution)/shard_map/piece/pallas_call | solution.py:313
  30.4 1.5 %collective-permute-start.3 = (bf16[784,256]{1,0:T(8,128)(2,1)S(1)}, bf16[784,256]{1,0:T(8,128)(2,1)S(1)}, u32[]{:S(2)}, u32[]{:S(2)}) collective-permute-start(bf16[784,256]{1,0:T(8,128)(2,1)S(1)} %piece.14), channel_id=1, source_target_pairs={{0,4},{4,0},{8,12},{12,8},{16,20},{20,16},{24,28},{28,24},{1,5},{5... | collective-permute-start | bytes 1204232 | tf_op jit(solution)/shard_map/ppermute | solution.py:493
  31.9 1.6 %collective-permute-done.5.refs_3_.refs_4_ = bf16[784,256]{1,0:T(8,128)(2,1)S(1)} collective-permute-done((bf16[784,256]{1,0:T(8,128)(2,1)S(1)}, bf16[784,256]{1,0:T(8,128)(2,1)S(1)}, u32[]{:S(2)}, u32[]{:S(2)}) %collective-permute-start.5) | collective-permute-done | bytes 401440 | tf_op jit(solution)/shard_map/ppermute | solution.py:493
  33.5 1.4 %piece.15.refs_0_ = f32[768,256]{1,0:T(8,128)S(1)} custom-call(bf16[512,2048]{1,0:T(8,128)(2,1)S(1)} %bitcast.21, bf16[512,2048]{1,0:T(8,128)(2,1)S(1)} %bitcast.30, bf16[3,512,256]{2,1,0:T(8,128)(2,1)S(1)} %copy-done.3, bf16[784,256]{1,0:T(8,128)(2,1)S(1)} %collective-permute-done.5.refs_3_.refs_4_, bf16[784,256]{1,0:T(8,128)(2,1)S(1)} %collective-permute-done.5.refs_3_.refs_4_), custom_call_target="tpu_custom_call" | custom-call | flops 1416000000 | bytes 1024 | tf_op jit(solution)/shard_map/piece/pallas_call | solution.py:313
  34.9 3.1 %collective-permute-done.6.refs_1_ = bf16[784,256]{1,0:T(8,128)(2,1)S(1)} collective-permute-done((bf16[784,256]{1,0:T(8,128)(2,1)S(1)}, bf16[784,256]{1,0:T(8,128)(2,1)S(1)}, u32[]{:S(2)}, u32[]{:S(2)}) %collective-permute-start.6) | collective-permute-done | bytes 401440 | tf_op jit(solution)/shard_map/ppermute | solution.py:493
  38.0 0.7 join.5
  38.6 1.6 %collective-permute-start.7 = (bf16[784,256]{1,0:T(8,128)(2,1)S(1)}, bf16[784,256]{1,0:T(8,128)(2,1)S(1)}, u32[]{:S(2)}, u32[]{:S(2)}) collective-permute-start(bf16[784,256]{1,0:T(8,128)(2,1)S(1)} %join.5), channel_id=1, source_target_pairs={{0,16},{4,20},{8,0},{12,4},{16,24},{20,28},{24,8},{28,12},{1,17},{... | collective-permute-start | bytes 1204232 | tf_op jit(solution)/shard_map/ppermute | solution.py:493
  40.3 0.0 collective-permute-done.1.refs_3_.refs_4_
  40.3 1.8 %piece.13.refs_0_ = f32[768,256]{1,0:T(8,128)S(1)} custom-call(bf16[512,2048]{1,0:T(8,128)(2,1)S(1)} %bitcast.22, bf16[512,2048]{1,0:T(8,128)(2,1)S(1)} %bitcast.31, bf16[3,512,256]{2,1,0:T(8,128)(2,1)S(1)} %copy-done.3, bf16[528,256]{1,0:T(8,128)(2,1)S(1)} %collective-permute-done.1.refs_3_.refs_4_, ...), custom_call_target="tpu_custom_call" | custom-call | flops 1416000000 | bytes 1024 | tf_op jit(solution)/shard_map/piece/pallas_call | solution.py:313
  42.1 0.0 copy-start.4
  42.1 0.0 copy-start.5
  42.1 0.0 copy-start.6
  42.1 1.0 collective-permute-done.3.refs_1_
  43.1 3.7 %collective-permute-done.7.refs_2_ = bf16[784,256]{1,0:T(8,128)(2,1)S(1)} collective-permute-done((bf16[784,256]{1,0:T(8,128)(2,1)S(1)}, bf16[784,256]{1,0:T(8,128)(2,1)S(1)}, u32[]{:S(2)}, u32[]{:S(2)}) %collective-permute-start.7) | collective-permute-done | bytes 401440 | tf_op jit(solution)/shard_map/ppermute | solution.py:493
  46.8 0.8 finish.1
  47.6 12.0 %all_to_all.11 = f32[32,1,128]{2,1,0:T(1,128)S(1)} all-to-all(f32[32,1,128]{2,1,0:T(1,128)S(1)} %bitcast.40), channel_id=1, replica_groups=mesh['dp'=8,'section'=4] {'dp','section'}, dimensions={0} | all-to-all | bytes 32768 | tf_op jit(solution)/shard_map/all_to_all | solution.py:530
  59.6 0.0 copy-done.4
  59.6 0.0 copy-done.5
  59.6 0.0 copy-done.6
  59.6 0.8 update.1.own_ref.refs_0_
  60.5 0.6 collective-permute-start.9
  61.1 0.6 collective-permute-start.8
  61.7 1.5 %collective-permute-start.13 = (bf16[288,256]{1,0:T(8,128)(2,1)S(1)}, bf16[288,256]{1,0:T(8,128)(2,1)S(1)}, u32[]{:S(2)}, u32[]{:S(2)}) collective-permute-start(bf16[288,256]{1,0:T(8,128)(2,1)S(1)} %slice.4), channel_id=1, source_target_pairs={{0,8},{4,12},{8,24},{12,28},{16,0},{20,4},{24,16},{28,20},{1,9},{5... | collective-permute-start | bytes 442376 | tf_op jit(solution)/shard_map/ppermute | solution.py:493
  63.2 8.8 %collective-permute-done.9.refs_0_ = bf16[768,256]{1,0:T(8,128)(2,1)S(1)} collective-permute-done((bf16[768,256]{1,0:T(8,128)(2,1)S(1)}, bf16[768,256]{1,0:T(8,128)(2,1)S(1)}, u32[]{:S(2)}, u32[]{:S(2)}) %collective-permute-start.9) | collective-permute-done | bytes 393248 | tf_op jit(solution)/shard_map/ppermute | solution.py:493
  71.9 0.0 collective-permute-done.8.refs_1_.other_ref
  71.9 0.3 collective-permute-start.10
  72.2 2.4 %collective-permute-start.12 = (bf16[768,256]{1,0:T(8,128)(2,1)S(1)}, bf16[768,256]{1,0:T(8,128)(2,1)S(1)}, u32[]{:S(2)}, u32[]{:S(2)}) collective-permute-start(bf16[768,256]{1,0:T(8,128)(2,1)S(1)} %behind.4.refs_1_.refs_2_), channel_id=1, source_target_pairs={{0,16},{4,20},{8,0},{12,4},{16,24},{20,28},{24,8},{28,12},{1,17},{... | collective-permute-start | bytes 1179656 | tf_op jit(solution)/shard_map/ppermute | solution.py:493
  74.6 1.1 %collective-permute-done.13.refs_0_ = bf16[288,256]{1,0:T(8,128)(2,1)S(1)} collective-permute-done((bf16[288,256]{1,0:T(8,128)(2,1)S(1)}, bf16[288,256]{1,0:T(8,128)(2,1)S(1)}, u32[]{:S(2)}, u32[]{:S(2)}) %collective-permute-start.13) | collective-permute-done | bytes 147488 | tf_op jit(solution)/shard_map/ppermute | solution.py:493
  75.7 0.4 collective-permute-start.14
  76.1 7.0 %collective-permute-done.10.after_ref.refs_1_.refs_4_ = bf16[768,256]{1,0:T(8,128)(2,1)S(1)} collective-permute-done((bf16[768,256]{1,0:T(8,128)(2,1)S(1)}, bf16[768,256]{1,0:T(8,128)(2,1)S(1)}, u32[]{:S(2)}, u32[]{:S(2)}) %collective-permute-start.10) | collective-permute-done | bytes 393248 | tf_op jit(solution)/shard_map/ppermute | solution.py:493
  83.1 0.1 both.1
  83.2 1.4 %collective-permute-start.11 = (bf16[960,256]{1,0:T(8,128)(2,1)S(1)}, bf16[960,256]{1,0:T(8,128)(2,1)S(1)}, u32[]{:S(2)}, u32[]{:S(2)}) collective-permute-start(bf16[960,256]{1,0:T(8,128)(2,1)S(1)} %both.1), channel_id=1, source_target_pairs={{0,8},{4,12},{8,24},{12,28},{16,0},{20,4},{24,16},{28,20},{1,9},{5... | collective-permute-start | bytes 1474568 | tf_op jit(solution)/shard_map/ppermute | solution.py:493
  84.6 0.0 collective-permute-done.12.refs_0_
  84.6 0.1 collective-permute-done.14.refs_1_.refs_5_
  84.7 0.7 collective-permute-start.15
  85.4 2.3 %states.1 = (f32[768,256]{1,0:T(8,128)}, f32[768,256]{1,0:T(8,128)}, f32[768,256]{1,0:T(8,128)}) custom-call(f32[32,128]{1,0:T(8,128)S(1)} %bitcast.39, f32[768,256]{1,0:T(8,128)S(1)} %get-tuple-element.14.refs_1_, f32[768,256]{1,0:T(8,128)S(1)} %bitcast.33, f32[768,256]{1,0:T(8,128)S(1)} %bitcast.35, f32[768,256]{1,0:T(8,128)S(1)} %bitcast.37), custom_call_target="tpu_custom_call" | custom-call | flops 1024 | bytes 1024 | tf_op jit(solution)/shard_map/states/pallas_call | solution.py:404
  87.7 1.4 %fill.2.refs_2_ = bf16[6144,256]{1,0:T(8,128)(2,1)} custom-call(bf16[768,256]{1,0:T(8,128)(2,1)S(1)} %update.1.own_ref.refs_0_, bf16[768,256]{1,0:T(8,128)(2,1)S(1)} %collective-permute-done.8.refs_1_.other_ref, bf16[768,256]{1,0:T(8,128)(2,1)S(1)} %behind.4.refs_1_.refs_2_, bf16[288,256]{1,0:T(8,128)(2,1)S(1)} %behind.6.refs_3_, ...), custom_call_target="tpu_custom_call" | custom-call | flops 1024 | bytes 1024 | tf_op jit(solution)/shard_map/fill/pallas_call | solution.py:466
  89.1 4.7 %collective-permute-done.15.refs_1_ = bf16[768,256]{1,0:T(8,128)(2,1)S(1)} collective-permute-done((bf16[768,256]{1,0:T(8,128)(2,1)S(1)}, bf16[768,256]{1,0:T(8,128)(2,1)S(1)}, u32[]{:S(2)}, u32[]{:S(2)}) %collective-permute-start.15) | collective-permute-done | bytes 393248 | tf_op jit(solution)/shard_map/ppermute | solution.py:493
  93.8 0.9 collective-permute-done.11.refs_0_
  94.7 0.9 fill.3
  (6 shorter events, 0.0 us)
Async XLA Ops:
  0.6 9.2 %copy-start = (bf16[1,512,2048]{2,1,0:T(8,128)(2,1)S(1)}, bf16[1,512,2048]{2,1,0:T(8,128)(2,1)}, u32[]{:S(2)}) copy-start(bf16[1,512,2048]{2,1,0:T(8,128)(2,1)} %param.7) | copy-start | bytes 6291460
  6.9 13.3 %collective-permute-start.4 = (bf16[784,256]{1,0:T(8,128)(2,1)}, bf16[784,256]{1,0:T(8,128)(2,1)S(1)}, u32[]{:S(2)}, u32[]{:S(2)}) collective-permute-start(bf16[784,256]{1,0:T(8,128)(2,1)} %get-tuple-element.12), channel_id=1, source_target_pairs={{0,4},{4,0},{8,12},{12,8},{16,20},{20,16},{24,28},{28,24},{1,5},{5... | collective-permute-start | bytes 1204232 | tf_op jit(solution)/shard_map/ppermute | solution.py:493
  9.9 1.6 %copy-start.1 = (bf16[1,512,2048]{2,1,0:T(8,128)(2,1)S(1)}, bf16[1,512,2048]{2,1,0:T(8,128)(2,1)}, u32[]{:S(2)}) copy-start(bf16[1,512,2048]{2,1,0:T(8,128)(2,1)} %param.8) | copy-start | bytes 6291460
  11.5 1.1 %copy-start.3 = (bf16[3,512,256]{2,1,0:T(8,128)(2,1)S(1)}, bf16[3,512,256]{2,1,0:T(8,128)(2,1)}, u32[]{:S(2)}) copy-start(bf16[3,512,256]{2,1,0:T(8,128)(2,1)} %get-tuple-element.11.refs_2_) | copy-start | bytes 2359300
  13.7 15.1 %collective-permute-start.2 = (bf16[528,256]{1,0:T(8,128)(2,1)S(1)}, bf16[528,256]{1,0:T(8,128)(2,1)S(1)}, u32[]{:S(2)}, u32[]{:S(2)}) collective-permute-start(bf16[528,256]{1,0:T(8,128)(2,1)S(1)} %piece.8.refs_3_), channel_id=1, source_target_pairs={{0,8},{4,12},{8,24},{12,28},{16,0},{20,4},{24,16},{28,20},{1,9},{5... | collective-permute-start | bytes 811016 | tf_op jit(solution)/shard_map/ppermute | solution.py:493
  16.3 11.8 %collective-permute-start = (bf16[528,256]{1,0:T(8,128)(2,1)S(1)}, bf16[528,256]{1,0:T(8,128)(2,1)S(1)}, u32[]{:S(2)}, u32[]{:S(2)}) collective-permute-start(bf16[528,256]{1,0:T(8,128)(2,1)S(1)} %piece.9.refs_3_), channel_id=1, source_target_pairs={{0,4},{4,0},{8,12},{12,8},{16,20},{20,16},{24,28},{28,24},{1,5},{5... | collective-permute-start | bytes 811016 | tf_op jit(solution)/shard_map/ppermute | solution.py:493
  18.3 5.8 %copy-start.2 = (bf16[1,512,2048]{2,1,0:T(8,128)(2,1)S(1)}, bf16[1,512,2048]{2,1,0:T(8,128)(2,1)}, u32[]{:S(2)}) copy-start(bf16[1,512,2048]{2,1,0:T(8,128)(2,1)} %param.8) | copy-start | bytes 6291460
  20.9 12.6 %collective-permute-start.5 = (bf16[784,256]{1,0:T(8,128)(2,1)S(1)}, bf16[784,256]{1,0:T(8,128)(2,1)S(1)}, u32[]{:S(2)}, u32[]{:S(2)}) collective-permute-start(bf16[784,256]{1,0:T(8,128)(2,1)S(1)} %join.4), channel_id=1, source_target_pairs={{0,16},{4,20},{8,0},{12,4},{16,24},{20,28},{24,8},{28,12},{1,17},{... | collective-permute-start | bytes 1204232 | tf_op jit(solution)/shard_map/ppermute | solution.py:493
  25.7 12.3 %collective-permute-start.6 = (bf16[784,256]{1,0:T(8,128)(2,1)S(1)}, bf16[784,256]{1,0:T(8,128)(2,1)S(1)}, u32[]{:S(2)}, u32[]{:S(2)}) collective-permute-start(bf16[784,256]{1,0:T(8,128)(2,1)S(1)} %piece.11.refs_3_), channel_id=1, source_target_pairs={{0,4},{4,0},{8,12},{12,8},{16,20},{20,16},{24,28},{28,24},{1,5},{5... | collective-permute-start | bytes 1204232 | tf_op jit(solution)/shard_map/ppermute | solution.py:493
  28.6 11.7 %collective-permute-start.1 = (bf16[528,256]{1,0:T(8,128)(2,1)S(1)}, bf16[528,256]{1,0:T(8,128)(2,1)S(1)}, u32[]{:S(2)}, u32[]{:S(2)}) collective-permute-start(bf16[528,256]{1,0:T(8,128)(2,1)S(1)} %join.3.refs_5_), channel_id=1, source_target_pairs={{0,8},{4,12},{8,24},{12,28},{16,0},{20,4},{24,16},{28,20},{1,9},{5... | collective-permute-start | bytes 811016 | tf_op jit(solution)/shard_map/ppermute | solution.py:493
  30.4 12.7 %collective-permute-start.3 = (bf16[784,256]{1,0:T(8,128)(2,1)S(1)}, bf16[784,256]{1,0:T(8,128)(2,1)S(1)}, u32[]{:S(2)}, u32[]{:S(2)}) collective-permute-start(bf16[784,256]{1,0:T(8,128)(2,1)S(1)} %piece.14), channel_id=1, source_target_pairs={{0,4},{4,0},{8,12},{12,8},{16,20},{20,16},{24,28},{28,24},{1,5},{5... | collective-permute-start | bytes 1204232 | tf_op jit(solution)/shard_map/ppermute | solution.py:493
  38.6 8.2 %collective-permute-start.7 = (bf16[784,256]{1,0:T(8,128)(2,1)S(1)}, bf16[784,256]{1,0:T(8,128)(2,1)S(1)}, u32[]{:S(2)}, u32[]{:S(2)}) collective-permute-start(bf16[784,256]{1,0:T(8,128)(2,1)S(1)} %join.5), channel_id=1, source_target_pairs={{0,16},{4,20},{8,0},{12,4},{16,24},{20,28},{24,8},{28,12},{1,17},{... | collective-permute-start | bytes 1204232 | tf_op jit(solution)/shard_map/ppermute | solution.py:493
  42.1 17.6 %copy-start.4 = (f32[1,768,256]{2,1,0:T(8,128)S(1)}, f32[1,768,256]{2,1,0:T(8,128)}, u32[]{:S(2)}) copy-start(f32[1,768,256]{2,1,0:T(8,128)} %param.9) | copy-start | bytes 2359300
  42.1 17.6 %copy-start.5 = (f32[1,768,256]{2,1,0:T(8,128)S(1)}, f32[1,768,256]{2,1,0:T(8,128)}, u32[]{:S(2)}) copy-start(f32[1,768,256]{2,1,0:T(8,128)} %param.10) | copy-start | bytes 2359300
  42.1 17.5 %copy-start.6 = (f32[1,768,256]{2,1,0:T(8,128)S(1)}, f32[1,768,256]{2,1,0:T(8,128)}, u32[]{:S(2)}) copy-start(f32[1,768,256]{2,1,0:T(8,128)} %param.11) | copy-start | bytes 2359300
  60.5 11.5 %collective-permute-start.9 = (bf16[768,256]{1,0:T(8,128)(2,1)S(1)}, bf16[768,256]{1,0:T(8,128)(2,1)S(1)}, u32[]{:S(2)}, u32[]{:S(2)}) collective-permute-start(bf16[768,256]{1,0:T(8,128)(2,1)S(1)} %update.1.own_ref.refs_0_), channel_id=1, source_target_pairs={{0,16},{4,20},{8,0},{12,4},{16,24},{20,28},{24,8},{28,12},{1,17},{... | collective-permute-start | bytes 1179656 | tf_op jit(solution)/shard_map/ppermute | solution.py:493
  61.1 10.8 %collective-permute-start.8 = (bf16[768,256]{1,0:T(8,128)(2,1)S(1)}, bf16[768,256]{1,0:T(8,128)(2,1)S(1)}, u32[]{:S(2)}, u32[]{:S(2)}) collective-permute-start(bf16[768,256]{1,0:T(8,128)(2,1)S(1)} %update.1.own_ref.refs_0_), channel_id=1, source_target_pairs={{0,4},{4,0},{8,12},{12,8},{16,20},{20,16},{24,28},{28,24},{1,5},{5... | collective-permute-start | bytes 1179656 | tf_op jit(solution)/shard_map/ppermute | solution.py:493
  61.7 14.0 %collective-permute-start.13 = (bf16[288,256]{1,0:T(8,128)(2,1)S(1)}, bf16[288,256]{1,0:T(8,128)(2,1)S(1)}, u32[]{:S(2)}, u32[]{:S(2)}) collective-permute-start(bf16[288,256]{1,0:T(8,128)(2,1)S(1)} %slice.4), channel_id=1, source_target_pairs={{0,8},{4,12},{8,24},{12,28},{16,0},{20,4},{24,16},{28,20},{1,9},{5... | collective-permute-start | bytes 442376 | tf_op jit(solution)/shard_map/ppermute | solution.py:493
  71.9 11.2 %collective-permute-start.10 = (bf16[768,256]{1,0:T(8,128)(2,1)S(1)}, bf16[768,256]{1,0:T(8,128)(2,1)S(1)}, u32[]{:S(2)}, u32[]{:S(2)}) collective-permute-start(bf16[768,256]{1,0:T(8,128)(2,1)S(1)} %behind.4.refs_1_.refs_2_), channel_id=1, source_target_pairs={{0,4},{4,0},{8,12},{12,8},{16,20},{20,16},{24,28},{28,24},{1,5},{5... | collective-permute-start | bytes 1179656 | tf_op jit(solution)/shard_map/ppermute | solution.py:493
  72.2 12.4 %collective-permute-start.12 = (bf16[768,256]{1,0:T(8,128)(2,1)S(1)}, bf16[768,256]{1,0:T(8,128)(2,1)S(1)}, u32[]{:S(2)}, u32[]{:S(2)}) collective-permute-start(bf16[768,256]{1,0:T(8,128)(2,1)S(1)} %behind.4.refs_1_.refs_2_), channel_id=1, source_target_pairs={{0,16},{4,20},{8,0},{12,4},{16,24},{20,28},{24,8},{28,12},{1,17},{... | collective-permute-start | bytes 1179656 | tf_op jit(solution)/shard_map/ppermute | solution.py:493
  75.7 9.0 %collective-permute-start.14 = (bf16[288,256]{1,0:T(8,128)(2,1)S(1)}, bf16[288,256]{1,0:T(8,128)(2,1)S(1)}, u32[]{:S(2)}, u32[]{:S(2)}) collective-permute-start(bf16[288,256]{1,0:T(8,128)(2,1)S(1)} %behind.6.refs_3_), channel_id=1, source_target_pairs={{0,4},{4,0},{8,12},{12,8},{16,20},{20,16},{24,28},{28,24},{1,5},{5... | collective-permute-start | bytes 442376 | tf_op jit(solution)/shard_map/ppermute | solution.py:493
  83.2 11.5 %collective-permute-start.11 = (bf16[960,256]{1,0:T(8,128)(2,1)S(1)}, bf16[960,256]{1,0:T(8,128)(2,1)S(1)}, u32[]{:S(2)}, u32[]{:S(2)}) collective-permute-start(bf16[960,256]{1,0:T(8,128)(2,1)S(1)} %both.1), channel_id=1, source_target_pairs={{0,8},{4,12},{8,24},{12,28},{16,0},{20,4},{24,16},{28,20},{1,9},{5... | collective-permute-start | bytes 1474568 | tf_op jit(solution)/shard_map/ppermute | solution.py:493
  84.7 9.1 %collective-permute-start.15 = (bf16[768,256]{1,0:T(8,128)(2,1)S(1)}, bf16[768,256]{1,0:T(8,128)(2,1)S(1)}, u32[]{:S(2)}, u32[]{:S(2)}) collective-permute-start(bf16[768,256]{1,0:T(8,128)(2,1)S(1)} %behind.7.refs_6_), channel_id=1, source_target_pairs={{0,4},{4,0},{8,12},{12,8},{16,20},{20,16},{24,28},{28,24},{1,5},{5... | collective-permute-start | bytes 1179656 | tf_op jit(solution)/shard_map/ppermute | solution.py:493
